TPU v7x, 32 devices: a whole 2x2x4 slice. The times are simulated.
32 devices in a mesh: dp: 2 (over core), ctx: 4 (over z), head: 4 (over y, x).
Axes of the slice: x: 2, y: 2, z: 4, core: 2. Of those that a mesh axis runs over, the one named last changes fastest.
Arguments:
- x_raw: bfloat16 [2, 1024, 8192], P('dp', 'ctx', 'head'), may hold values from -6 to 6
- bc_raw: bfloat16 [2, 1024, 2, 1024], P('dp', 'ctx', None, 'head'), may hold values from -6 to 6
- z_gate: bfloat16 [2, 1024, 8192], P('dp', 'ctx', 'head'), may hold values from -20 to 20
- dt_raw: bfloat16 [2, 128, 1024], P('dp', 'head', 'ctx'), may hold values from -4 to 4
- resets: int32 [2, 1024], P('dp', 'ctx'), may hold values 0 or 1
- conv_x_weight: float32 [4, 8192], P(None, 'head'), may hold values from -3 to 3
- conv_x_bias: float32 [8192], P('head'), may hold values from -1.5 to 1.5
- conv_bc_weight: float32 [4, 2, 1024], P(None, None, 'head'), may hold values from -3 to 3
- conv_bc_bias: float32 [2, 1024], P(None, 'head'), may hold values from -1.5 to 1.5
- a_log: float32 [128], P('head'), may hold values from -9 to 1
- dt_bias: float32 [128], P('head'), may hold values from -13 to -3
- skip_weight: float32 [128], P('head'), may hold values from 0.5 to 2
- norm_gain: float32 [8192], P('head'), may hold values from 0.1 to 1.9
- grad_out: bfloat16 [2, 1024, 8192], P('dp', 'ctx', 'head'), may hold values from -6 to 6
Outputs:
- grad_x: bfloat16 [2, 1024, 8192], P('dp', 'ctx', 'head')
- grad_bc: bfloat16 [2, 1024, 2, 1024], P('dp', 'ctx', None, 'head')
- grad_z: bfloat16 [2, 1024, 8192], P('dp', 'ctx', 'head')
- grad_dt: float32 [2, 128, 1024], P('dp', 'head', 'ctx')
- grad_conv_x_weight: float32 [4, 8192], P(None, 'head')
- grad_conv_x_bias: float32 [8192], P('head')
- grad_conv_bc_weight: float32 [4, 2, 1024], P(None, None, 'head')
- grad_conv_bc_bias: float32 [2, 1024], P(None, 'head')
- grad_a_log: float32 [128], P('head')
- grad_dt_bias: float32 [128], P('head')
- grad_skip: float32 [128], P('head')
- grad_gain: float32 [8192], P('head')
All inputs are finite; a program needn't handle non-finite values. No bound on the sum of `resets` on one device may be relied on, other than what follows from the above.
Results may differ from a plain program's by a relative error of at most 0.01595.
Values may be sent and summed in bfloat16 or wider, within the bound.
No kernel may reach another device: no remote copies, remote signals or barrier semaphores. Data moves between devices by JAX's collectives and lax.ppermute only.
A program may use at most 256 MiB of HBM per device.

v0:
```python
import functools

import jax
import jax.numpy as jnp
from jax import lax
from jax.sharding import PartitionSpec as P

HEAD_DIM = 64
NSTATE = 128
CONV = 4
STRETCH = 128
INNER = 8192


norm_eps = 1e-05


def from_behind(value, axis, steps):
    count = lax.axis_size(axis)
    first, last = (max(0, -steps), min(count, count - steps))
    return lax.ppermute(value, axis, [(source, source + steps) for source in range(first, last)])


def entering(value, axis, join, neutral, backward):
    count, mine = (lax.axis_size(axis), lax.axis_index(axis))
    pieces = jax.tree.map(lambda part: lax.all_gather(part, axis), value)
    if backward:
        pieces = jax.tree.map(lambda part: part[::-1], pieces)
        mine = count - 1 - mine
    running = jax.tree.map(
        lambda part, zero: jnp.full_like(part, 0) + jnp.asarray(zero, part.dtype), value, neutral
    )

    def step(position, running):
        longer = join(running, jax.tree.map(lambda part: part[position], pieces))
        return jax.tree.map(lambda new, old: jnp.where(position < mine, new, old), longer, running)

    return lax.fori_loop(0, count - 1, step, running)


def kept(value):
    return lax.optimization_barrier(value)


def causal_conv(extended, counts, weight, conv_bias):
    pad_rows = CONV - 1
    row_count = extended.shape[0] - pad_rows
    shape_tail = (1,) * (extended.ndim - 1)
    summed = conv_bias + weight[0] * extended[pad_rows:]
    for lag_step in range(1, CONV):
        lower = pad_rows - lag_step
        live_mask = (counts[pad_rows:] == counts[lower : lower + row_count]).astype(jnp.float32)
        summed = summed + weight[lag_step] * extended[
            lower : lower + row_count
        ] * live_mask.reshape((row_count,) + shape_tail)
    return kept(jax.nn.silu(summed).astype(jnp.bfloat16))


def rows_to_blocks(array_rows):
    return array_rows.reshape((array_rows.shape[0] // STRETCH, STRETCH) + array_rows.shape[1:])


def steps_to_blocks(steps_dt):
    shape_now = steps_dt.shape
    reshaped = steps_dt.reshape(shape_now[0], shape_now[1], shape_now[2] // STRETCH, STRETCH)
    return jnp.transpose(reshaped, (2, 0, 1, 3))


def from_before(block_c, prior_state, running, resets_seen):
    from_start = jnp.where(resets_seen == 0.0, jnp.exp(running), 0.0)
    state_half = prior_state.astype(jnp.bfloat16)
    carried = jnp.einsum("tgn,ghpn->tghp", block_c, state_half, preferred_element_type=jnp.float32)
    return carried * jnp.transpose(from_start, (2, 0, 1))[..., None]


def keep_factor(running, resets_seen):
    return jnp.where(resets_seen[-1] == 0.0, jnp.exp(running[..., -1]), 0.0)


def block_end(block_x, block_b, block_dt, running, resets_seen):
    to_end = jnp.where(resets_seen == resets_seen[-1], jnp.exp(running[..., -1:] - running), 0.0)
    scaled = (
        block_x.astype(jnp.float32) * jnp.transpose(block_dt * to_end, (2, 0, 1))[..., None]
    ).astype(jnp.bfloat16)
    return jnp.einsum("sghp,sgn->ghpn", scaled, block_b, preferred_element_type=jnp.float32)


def block_terms(prior_state, block_piece, decay_rate):
    block_x, block_b, block_c, block_dt, block_flags = block_piece
    running = jnp.cumsum(-decay_rate[:, :, None] * block_dt, axis=-1)
    resets_seen = jnp.cumsum(block_flags)
    position = jnp.arange(block_flags.shape[0])
    same_doc = (resets_seen[:, None] == resets_seen[None, :]) & (
        position[:, None] >= position[None, :]
    )
    spread = running[..., :, None] - running[..., None, :]
    segment = jnp.where(same_doc, jnp.exp(jnp.where(same_doc, spread, 0.0)), 0.0)
    scores = jnp.einsum("tgn,sgn->gts", block_c, block_b, preferred_element_type=jnp.float32)
    weights = (scores[:, None] * segment * block_dt[:, :, None, :]).astype(jnp.bfloat16)
    within = jnp.einsum("ghts,sghp->tghp", weights, block_x, preferred_element_type=jnp.float32)
    carried = from_before(block_c, prior_state, running, resets_seen)
    fresh_state = block_end(block_x, block_b, block_dt, running, resets_seen)
    next_state = keep_factor(running, resets_seen)[..., None, None] * prior_state + fresh_state
    return (next_state, within + carried)


def scan_blocks(inputs, b_rows, c_rows, steps_dt, decay_rate, reset_flags, state_in):
    row_count = inputs.shape[0]
    pieces = (
        rows_to_blocks(inputs),
        rows_to_blocks(b_rows),
        rows_to_blocks(c_rows),
        steps_to_blocks(steps_dt),
        rows_to_blocks(reset_flags),
    )
    stepper = functools.partial(block_terms, decay_rate=decay_rate)
    final_state, outputs = lax.scan(stepper, state_in, pieces)
    return (outputs.reshape((row_count,) + inputs.shape[1:]), final_state)


def block_ends(inputs, b_rows, steps_dt, decay_rate, reset_flags):

    def block_advance(carried_pair, block_piece):
        product, prior_state = carried_pair
        part_x, part_b, part_dt, part_flags = block_piece
        running = jnp.cumsum(-decay_rate[:, :, None] * part_dt, axis=-1)
        resets_seen = jnp.cumsum(part_flags)
        keep_all = keep_factor(running, resets_seen)
        fresh_state = block_end(part_x, part_b, part_dt, running, resets_seen)
        return ((product * keep_all, keep_all[..., None, None] * prior_state + fresh_state), None)

    start_pair = (
        jnp.ones(decay_rate.shape, jnp.float32),
        jnp.zeros(decay_rate.shape + (HEAD_DIM, NSTATE), jnp.float32),
    )
    pieces = (
        rows_to_blocks(inputs),
        rows_to_blocks(b_rows),
        steps_to_blocks(steps_dt),
        rows_to_blocks(reset_flags),
    )
    end_pair, unused = lax.scan(block_advance, start_pair, pieces)
    return end_pair


def carried_only(c_rows, steps_dt, decay_rate, reset_flags, prior_state):

    def carried_advance(state_now, block_piece):
        part_c, part_dt, part_flags = block_piece
        running = jnp.cumsum(-decay_rate[:, :, None] * part_dt, axis=-1)
        resets_seen = jnp.cumsum(part_flags)
        carried = from_before(part_c, state_now, running, resets_seen)
        return (keep_factor(running, resets_seen)[..., None, None] * state_now, carried)

    pieces = (rows_to_blocks(c_rows), steps_to_blocks(steps_dt), rows_to_blocks(reset_flags))
    final_state, outputs = lax.scan(carried_advance, prior_state, pieces)
    return outputs.reshape((c_rows.shape[0], c_rows.shape[1], steps_dt.shape[1], HEAD_DIM))


def gate_output(y_ssd, inputs, z_in, skip_weight):
    row_count = inputs.shape[0]
    skip_term = skip_weight.reshape(inputs.shape[1], inputs.shape[2])[
        None, :, :, None
    ] * inputs.astype(jnp.float32)
    mixed = kept((y_ssd + skip_term).astype(jnp.bfloat16))
    return mixed.astype(jnp.float32).reshape(row_count, -1) * jax.nn.silu(z_in)


def combine_pairs(earlier, later):
    return (earlier[0] * later[0], later[0][..., None, None] * earlier[1] + later[1])


def per_device(
    x_raw,
    bc_raw,
    z_gate,
    dt_raw,
    resets,
    conv_x_weight,
    conv_x_bias,
    conv_bc_weight,
    conv_bc_bias,
    a_log,
    dt_bias,
    skip_weight,
    norm_gain,
    grad_out,
):
    halo_rows = CONV - 1
    row_count = x_raw.shape[1]
    g_count = bc_raw.shape[3] // NSTATE
    heads_dev = a_log.shape[0]
    per_group = heads_dev // g_count
    reset_flags = resets[0].astype(jnp.float32)
    counts = jnp.cumsum(reset_flags)
    tail_keep = (counts[-halo_rows:] == counts[-1]).astype(jnp.float32)
    tail_half = tail_keep.astype(jnp.bfloat16)
    x_own = x_raw[0]
    bc_own = bc_raw[0]
    x_prev, bc_prev = from_behind(
        (x_own[-halo_rows:] * tail_half[:, None], bc_own[-halo_rows:] * tail_half[:, None, None]),
        "ctx",
        1,
    )
    x_ext = jnp.concatenate([x_prev, x_own]).astype(jnp.float32)
    bc_ext = jnp.concatenate([bc_prev, bc_own]).astype(jnp.float32)
    padded_counts = jnp.concatenate([jnp.zeros((halo_rows,), jnp.float32), counts])
    z_in = z_gate[0].astype(jnp.float32)
    dt_in = dt_raw[0].astype(jnp.float32)

    def conv_part(x_wide, bc_wide, dt_values, cx_weight, cx_bias, cb_weight, cb_bias, bias_dt):
        inputs = causal_conv(x_wide, padded_counts, cx_weight, cx_bias).reshape(
            row_count, g_count, per_group, HEAD_DIM
        )
        bc_conv = causal_conv(bc_wide, padded_counts, cb_weight, cb_bias)
        b_rows = bc_conv[:, 0].reshape(row_count, g_count, NSTATE)
        c_rows = bc_conv[:, 1].reshape(row_count, g_count, NSTATE)
        steps_dt = jax.nn.softplus(dt_values + bias_dt[:, None]).reshape(
            g_count, per_group, row_count
        )
        return (inputs, b_rows, c_rows, steps_dt)

    conv_outs, conv_pull = jax.vjp(
        conv_part,
        x_ext,
        bc_ext,
        dt_in,
        conv_x_weight,
        conv_x_bias,
        conv_bc_weight,
        conv_bc_bias,
        dt_bias,
    )
    inputs, b_rows, c_rows, steps_dt = conv_outs
    decay_rate = jnp.exp(a_log).reshape(g_count, per_group)
    device_decay, device_state = block_ends(inputs, b_rows, steps_dt, decay_rate, reset_flags)
    unit_decay = jnp.ones_like(device_decay)
    prefix_pair = entering(
        (device_decay, device_state),
        "ctx",
        combine_pairs,
        (unit_decay, jnp.zeros_like(device_state)),
        False,
    )
    state_in = prefix_pair[1]

    def ssd_part(block_inputs, block_b, block_c, block_dt, log_rate, prior_state):
        rate_now = jnp.exp(log_rate).reshape(g_count, per_group)
        return scan_blocks(
            block_inputs, block_b, block_c, block_dt, rate_now, reset_flags, prior_state
        )

    ssd_outs, ssd_pull = jax.vjp(ssd_part, inputs, b_rows, c_rows, steps_dt, a_log, state_in)
    y_ssd = ssd_outs[0]
    gated, post_pull = jax.vjp(gate_output, y_ssd, inputs, z_in, skip_weight)
    cotangent = grad_out[0].astype(jnp.float32)
    gained_out = cotangent * norm_gain
    row_totals = lax.psum(
        (jnp.sum(gated * gated, axis=-1), jnp.sum(gated * gained_out, axis=-1)), "head"
    )
    inv_rms = lax.rsqrt(row_totals[0] / INNER + norm_eps)
    d_gated = (
        gained_out * inv_rms[:, None]
        - gated * (inv_rms * inv_rms * inv_rms * row_totals[1] / INNER)[:, None]
    )
    gain_local = jnp.sum(cotangent * gated * inv_rms[:, None], axis=0)
    dy_ssd, d_inputs_post, d_z, d_skip = post_pull(d_gated)
    carried_map = functools.partial(carried_only, c_rows, steps_dt, decay_rate, reset_flags)
    unused_out, carried_pull = jax.vjp(carried_map, state_in)
    direct_adjoint = carried_pull(dy_ssd)[0]
    later_pair = entering(
        (device_decay, direct_adjoint),
        "ctx",
        combine_pairs,
        (unit_decay, jnp.zeros_like(direct_adjoint)),
        True,
    )
    d_inputs, d_b, d_c, d_dt, d_alog, d_state = ssd_pull((dy_ssd, later_pair[1]))
    d_inputs = d_inputs + d_inputs_post
    d_x_ext, d_bc_ext, d_dt_in, d_cxw, d_cxb, d_cbw, d_cbb, d_dt_bias = conv_pull(
        (d_inputs, d_b, d_c, d_dt)
    )
    back_x, back_bc = from_behind((d_x_ext[:halo_rows], d_bc_ext[:halo_rows]), "ctx", -1)
    grad_x_rows = jnp.concatenate(
        [d_x_ext[halo_rows:row_count], d_x_ext[row_count:] + back_x * tail_keep[:, None]]
    )
    grad_bc_rows = jnp.concatenate(
        [d_bc_ext[halo_rows:row_count], d_bc_ext[row_count:] + back_bc * tail_keep[:, None, None]]
    )
    local_terms = (d_cxw, d_cxb, d_cbw, d_cbb, d_alog, d_dt_bias, d_skip, gain_local)
    summed_terms = lax.psum(
        (
            local_terms[0],
            local_terms[1],
            local_terms[2],
            local_terms[3],
            local_terms[4],
            local_terms[5],
            local_terms[6],
            local_terms[7],
        ),
        ("dp", "ctx"),
    )
    grad_scale = float(lax.axis_size("dp") * lax.axis_size("ctx") * row_count) ** (-0.5)
    return (
        grad_x_rows[None].astype(jnp.bfloat16),
        grad_bc_rows[None].astype(jnp.bfloat16),
        d_z[None].astype(jnp.bfloat16),
        d_dt_in[None],
        summed_terms[0] * grad_scale,
        summed_terms[1] * grad_scale,
        summed_terms[2] * grad_scale,
        summed_terms[3] * grad_scale,
        summed_terms[4] * grad_scale,
        summed_terms[5] * grad_scale,
        summed_terms[6] * grad_scale,
        summed_terms[7] * grad_scale,
    )


def solution(mesh):
    return jax.shard_map(
        per_device,
        mesh=mesh,
        in_specs=(
            P("dp", "ctx", "head"),
            P("dp", "ctx", None, "head"),
            P("dp", "ctx", "head"),
            P("dp", "head", "ctx"),
            P("dp", "ctx"),
            P(None, "head"),
            P("head"),
            P(None, None, "head"),
            P(None, "head"),
            P("head"),
            P("head"),
            P("head"),
            P("head"),
            P("dp", "ctx", "head"),
        ),
        out_specs=(
            P("dp", "ctx", "head"),
            P("dp", "ctx", None, "head"),
            P("dp", "ctx", "head"),
            P("dp", "head", "ctx"),
            P(None, "head"),
            P("head"),
            P(None, None, "head"),
            P(None, "head"),
            P("head"),
            P("head"),
            P("head"),
            P("head"),
        ),
        check_vma=False,
    )
```

profile of v0, /device:TPU:0, one launch (start us, length us, event | category | flops | bytes accessed | tf_op | source)
XLA Modules:
  0.0 542.5 jit_solution(7446092661809253310)
XLA Ops:
  11.4 4.9 collective-permute-start.1
  17.2 3.5 collective-permute-start
  36.6 3.3 copy.180
  39.9 10.0 %while.160 = (s32[]{:T(128)}, f32[2,16]{1,0:T(2,128)S(1)}, f32[2,16,64,128]{3,2,1,0:T(8,128)S(1)}, f32[2,128]{1,0:T(2,128)S(1)}, f32[2,16,1]{1,0,2:T(2,128)}, /*...) while((s32[]{:T(128)}, f32[2,16]{1,0:T(2,128)S(1)}, ...), condition=%wide.region_5.6_spmd.clone, body=%wide.region_2.5_spmd.clone.sunk | while | flops 69234784 | bytes 2825122 | solution.py:142
  58.3 7.4 %while.158 = (s32[]{:T(128)}, f32[2,128,2,16,1]{1,3,2,4,0:T(8,128)}, f32[2,2,16,1,1]{2,1,4,3,0:T(2,128)S(1)}, f32[2,128]{1,0:T(2,128)S(1)}, f32[2,16,1]{1,0,2:T(...) while((s32[]{:T(128)}, f32[2,128,2,16,1]{1,3,2,4,0:T(8,128)}, ...), condition=%wide.region_19.20_spmd, body=%wide.region_16.19_spmd.sunk | while | flops 544803 | bytes 105219 | solution.py:156
  68.4 9.5 %all-gather.3 = f32[4,2,16]{2,1,0:T(2,128)S(1)} all-gather(f32[1,2,16]{2,1,0:T(2,128)S(1)} %bitcast.631), channel_id=2, replica_groups=mesh['dp'=2,'ctx'=4,'head'=4] {'ctx'}, dimensions={0}, use_global_device_ids=true | all-gather | bytes 640 | tf_op jit(solution)/shard_map/all_gather | solution.py:26
  77.9 53.3 %all-gather.7.cloned.1.call-done = f32[8,16,64,128]{3,2,1,0:T(8,128)} async-done(((f32[2,16,64,128]{3,2,1,0:T(8,128)}), f32[8,16,64,128]{3,2,1,0:T(8,128)}) %all-gather.7.cloned.1.call-update) | async-done | bytes 4194320 | tf_op jit(solution)/shard_map/all_gather | solution.py:26
  131.1 4.5 while.161
  138.7 116.0 %while.159 = (s32[]{:T(128)}, f32[2,16,64,128]{3,2,1,0:T(8,128)S(1)}, f32[2,128,2,16,64]{1,0,4,3,2:T(2,128)}, pred[2,2,16,128,128]{4,3,2,1,0:T(32,128)(4,1)}, f3...) while((s32[]{:T(128)}, ...), condition=%wide.region_11.12_spmd.clone, body=%wide.region_8.11_spmd.clone.sunk | while | flops 222142656 | bytes 53181924 | solution.py:117
  147.9 3.2 fusion.249
  159.7 25.0 %dynamic_update_slice.324 = f32[2,128,2,16,64]{1,0,4,3,2:T(2,128)} dynamic-update-slice(f32[2,128,2,16,64]{1,0,4,3,2:T(2,128)} %get-tuple-element.3483, f32[1,128,2,16,64]{1,0,4,3,2:T(1,128)} %bitcast.608, s32[]{:T(128)} %get-tuple-element.3481, s32[]{:T(128)} %constant.351.clone.1..sunk, s32[]{:T(128)} %constant.351.clone.1..sunk, s32[]{:T(128)} %constant.351.clone.1..sunk, s32[]{:T(128)} %constant.351.clone.1..sunk) | dynamic-update-slice | bytes 2097156 | tf_op jit(solution)/shard_map/jvp()/while/body/jit(dynamic_update_index_in_dim)/dynamic_update_slice | solution.py:117
  205.9 3.2 fusion.249
  217.7 25.0 %dynamic_update_slice.324 = f32[2,128,2,16,64]{1,0,4,3,2:T(2,128)} dynamic-update-slice(f32[2,128,2,16,64]{1,0,4,3,2:T(2,128)} %get-tuple-element.3483, f32[1,128,2,16,64]{1,0,4,3,2:T(1,128)} %bitcast.608, s32[]{:T(128)} %get-tuple-element.3481, s32[]{:T(128)} %constant.351.clone.1..sunk, s32[]{:T(128)} %constant.351.clone.1..sunk, s32[]{:T(128)} %constant.351.clone.1..sunk, s32[]{:T(128)} %constant.351.clone.1..sunk) | dynamic-update-slice | bytes 2097156 | tf_op jit(solution)/shard_map/jvp()/while/body/jit(dynamic_update_index_in_dim)/dynamic_update_slice | solution.py:117
  254.8 4.3 reshape.606
  263.5 10.1 %all-reduce.22 = (f32[256]{0:T(256)S(1)}, f32[256]{0:T(256)S(1)}) all-reduce(f32[256]{0:T(256)S(1)} %get-tuple-element.2453, f32[256]{0:T(256)S(1)} %get-tuple-element.2452), channel_id=1, replica_groups=mesh['dp'=2,'ctx'=4,'head'=4] {'head'}, use_global_device_ids=true, to_apply=%region_15.16 | all-reduce | flops 512 | bytes 4096 | tf_op jit(solution)/shard_map/psum | solution.py:258
  292.0 3.9 fusion.159
  298.3 59.4 %all-gather.9.cloned.1.call-done = f32[8,16,64,128]{3,2,1,0:T(8,128)} async-done(((f32[2,16,64,128]{3,2,1,0:T(8,128)}), f32[8,16,64,128]{3,2,1,0:T(8,128)}) %all-gather.9.cloned.1.call-update) | async-done | bytes 4194320 | tf_op jit(solution)/shard_map/all_gather | solution.py:26
  357.7 4.7 rev.7
  362.4 4.5 while.163
  370.3 97.4 %while.164 = (s32[]{:T(128)}, f32[2,16]{1,0:T(2,128)}, f32[2,16,64,128]{3,2,1,0:T(8,128)S(1)}, bf16[2,128,2,16,64]{1,4,3,2,0:T(8,128)(2,1)}, bf16[2,128,2,128]{3...) while((s32[]{:T(128)}, f32[2,16]{1,0:T(2,128)}, ...), condition=%wide.region_35.36_spmd.clone, body=%wide.region_24.35_spmd.clone.sunk | while | flops 431345728 | bytes 51170820 | solution.py:117
  380.5 5.1 fusion.275
  428.9 5.1 fusion.275
  478.0 4.6 multiply_reduce_fusion.3
  489.2 27.6 %all-reduce.21 = (f32[4,2048]{1,0:T(4,128)S(1)}, f32[2048]{0:T(1024)}, f32[4,2,256]{2,1,0:T(2,128)S(1)}, f32[2,256]{1,0:T(2,128)}, f32[32]{0:T(128)}, /*index=5*/f32[32]{0:T(128)}, f32[32]{0:T(128)}, f32[2048]{0:T(1024)}) all-reduce(f32[4,2048]{1,0:T(4,128)S(1)} %pad_add_fusion.4, ...), channel_id=1, replica_groups=mesh['dp'=2,'ctx'=4,'head'=4] {'dp','ctx'}, use_global_device_ids=true, to_apply=%region_40.41 | all-reduce | flops 14944 | bytes 119552 | tf_op jit(solution)/shard_map/psum | solution.py:291
  (690 shorter events, 267.1 us)
Async XLA Ops:
  7.2 20.5 %copy-start.124 = (f32[2,256]{1,0:T(2,128)S(1)}, f32[2,256]{1,0:T(2,128)}, u32[]{:S(2)}) copy-start(f32[2,256]{1,0:T(2,128)} %param.36) | copy-start | bytes 6148
  7.2 123.9 %all-gather.7.cloned.1.call-start = ((), (), s32[]{:S(2)}) async-start(), calls=%async_computation | async-start | bytes 5242880 | tf_op jit(solution)/shard_map/all_gather | solution.py:26
  11.4 15.4 %collective-permute-start.1 = (bf16[3,2,256]{2,0,1:T(4,128)(2,1)S(1)}, bf16[3,2,256]{2,0,1:T(4,128)(2,1)S(1)}, u32[]{:S(2)}, u32[]{:S(2)}) collective-permute-start(bf16[3,2,256]{2,0,1:T(4,128)(2,1)S(1)} %fusion.175), channel_id=1, source_target_pairs={{0,4},{4,8},{8,12},{1,5},{5,9},{9,13},{2,6},{6,10},{10,14},{3,7},{... | collective-permute-start | bytes 9224 | tf_op jit(solution)/shard_map/ppermute | solution.py:21
  17.2 11.9 %collective-permute-start = (bf16[3,2048]{1,0:T(4,128)(2,1)S(1)}, bf16[3,2048]{1,0:T(4,128)(2,1)S(1)}, u32[]{:S(2)}, u32[]{:S(2)}) collective-permute-start(bf16[3,2048]{1,0:T(4,128)(2,1)S(1)} %bitcast_multiply_fusion.16), channel_id=1, source_target_pairs={{0,4},{4,8},{8,12},{1,5},{5,9},{9,13},{2,6},{6,10},{10,14},{3,7},{... | collective-permute-start | bytes 36872 | tf_op jit(solution)/shard_map/ppermute | solution.py:21
  20.7 8.7 %copy-start.83 = (f32[256]{0:T(256)}, f32[256]{0:T(256)S(1)}, u32[]{:S(2)}) copy-start(f32[256]{0:T(256)S(1)} %get-tuple-element.2724) | copy-start | bytes 3076
  20.7 8.7 %copy-start.85 = (f32[256]{0:T(256)}, f32[256]{0:T(256)S(1)}, u32[]{:S(2)}) copy-start(f32[256]{0:T(256)S(1)} %get-tuple-element.2725) | copy-start | bytes 3076
  20.8 8.7 %copy-start.87 = (f32[256]{0:T(256)}, f32[256]{0:T(256)S(1)}, u32[]{:S(2)}) copy-start(f32[256]{0:T(256)S(1)} %get-tuple-element.2726) | copy-start | bytes 3076
  21.5 7.4 %copy-start.101 = (f32[2,256]{1,0:T(2,128)}, f32[2,256]{1,0:T(2,128)S(1)}, u32[]{:S(2)}) copy-start(f32[2,256]{1,0:T(2,128)S(1)} %get-tuple-element.2718) | copy-start | bytes 6148
  21.5 7.4 %copy-start.103 = (f32[2,256]{1,0:T(2,128)}, f32[2,256]{1,0:T(2,128)S(1)}, u32[]{:S(2)}) copy-start(f32[2,256]{1,0:T(2,128)S(1)} %get-tuple-element.2719) | copy-start | bytes 6148
  21.5 7.4 %copy-start.105 = (f32[2,256]{1,0:T(2,128)}, f32[2,256]{1,0:T(2,128)S(1)}, u32[]{:S(2)}) copy-start(f32[2,256]{1,0:T(2,128)S(1)} %get-tuple-element.2720) | copy-start | bytes 6148
  21.5 7.4 %copy-start.107 = (f32[2,256]{1,0:T(2,128)}, f32[2,256]{1,0:T(2,128)S(1)}, u32[]{:S(2)}) copy-start(f32[2,256]{1,0:T(2,128)S(1)} %get-tuple-element.2721) | copy-start | bytes 6148
  22.5 7.0 %copy-start.70 = (f32[1,2048]{1,0:T(1,128)}, f32[1,2048]{1,0:T(1,128)S(1)}, u32[]{:S(2)}) copy-start(f32[1,2048]{1,0:T(1,128)S(1)} %get-tuple-element.2714) | copy-start | bytes 24580
  39.9 11.3 %copy-start.127 = (f32[32]{0:T(128)S(1)}, f32[32]{0:T(128)}, u32[]{:S(2)}) copy-start(f32[32]{0:T(128)} %param.39) | copy-start | bytes 388
  50.9 306.7 %all-gather.9.cloned.1.call-start = ((), (), s32[]{:S(2)}) async-start(), calls=%async_computation.1 | async-start | bytes 5242880 | tf_op jit(solution)/shard_map/all_gather | solution.py:26
  65.7 65.4 %copy-start.99 = (f32[2,2,16,1,1]{2,1,4,3,0:T(2,128)}, f32[2,2,16,1,1]{2,1,4,3,0:T(2,128)S(1)}, u32[]{:S(2)}) copy-start(f32[2,2,16,1,1]{2,1,4,3,0:T(2,128)S(1)} %get-tuple-element.3580) | copy-start | bytes 772
  189.6 7.1 %copy-start.121 = (f32[2,128]{1,0:T(2,128)S(1)}, f32[2,128]{1,0:T(2,128)}, u32[]{:S(2)}) copy-start(f32[2,128]{1,0:T(2,128)} %copy-done.120) | copy-start | bytes 3076 | tf_op jit(solution)/shard_map/jvp()/while
  247.7 7.1 %copy-start.121 = (f32[2,128]{1,0:T(2,128)S(1)}, f32[2,128]{1,0:T(2,128)}, u32[]{:S(2)}) copy-start(f32[2,128]{1,0:T(2,128)} %copy-done.120) | copy-start | bytes 3076 | tf_op jit(solution)/shard_map/jvp()/while
  262.5 11.1 %copy-start.13 = (f32[1,256,2048]{1,2,0:T(8,128)S(1)}, f32[1,256,2048]{1,2,0:T(8,128)}, u32[]{:S(2)}) copy-start(f32[1,256,2048]{1,2,0:T(8,128)} %copy.183) | copy-start | bytes 6291460
  458.9 7.0 %copy-start.55 = (f32[2,128,2,16,1]{1,3,2,4,0:T(8,128)S(1)}, f32[2,128,2,16,1]{1,3,2,4,0:T(8,128)}, u32[]{:S(2)}) copy-start(f32[2,128,2,16,1]{1,3,2,4,0:T(8,128)} %get-tuple-element.3726) | copy-start | bytes 98308 | tf_op jit(solution)/shard_map/transpose(jvp())/while
  458.9 7.0 %copy-start.3 = (f32[128,2,16,64]{0,3,2,1:T(8,128)S(1)}, f32[128,2,16,64]{0,3,2,1:T(8,128)}, u32[]{:S(2)}) copy-start(f32[128,2,16,64]{0,3,2,1:T(8,128)} %get-tuple-element.3386) | copy-start | bytes 3145732 | tf_op jit(solution)/shard_map/transpose(jvp())/while
  458.9 7.0 %copy-start.19 = (bf16[2,2,16,128,128]{4,3,2,1,0:T(8,128)(2,1)S(1)}, bf16[2,2,16,128,128]{4,3,2,1,0:T(8,128)(2,1)}, u32[]{:S(2)}) copy-start(bf16[2,2,16,128,128]{4,3,2,1,0:T(8,128)(2,1)} %get-tuple-element.3727) | copy-start | bytes 6291460 | tf_op jit(solution)/shard_map/transpose(jvp())/while
  486.4 41.0 %copy-start.78 = (bf16[1,32,256]{2,1,0:T(8,128)(2,1)S(1)}, bf16[1,32,256]{2,1,0:T(8,128)(2,1)}, u32[]{:S(2)}) copy-start(bf16[1,32,256]{2,1,0:T(8,128)(2,1)} %param.31) | copy-start | bytes 49156
  522.2 9.3 %collective-permute-start.3 = (f32[3,2,256]{2,0,1:T(4,128)}, f32[3,2,256]{2,0,1:T(4,128)}, u32[]{:S(2)}, u32[]{:S(2)}) collective-permute-start(f32[3,2,256]{2,0,1:T(4,128)} %pad_add_fusion.5), channel_id=1, source_target_pairs={{4,0},{8,4},{12,8},{5,1},{9,5},{13,9},{6,2},{10,6},{14,10},{7,3},{... | collective-permute-start | bytes 18440 | tf_op jit(solution)/shard_map/ppermute | solution.py:21
  525.9 7.3 %collective-permute-start.2 = (f32[3,2048]{1,0:T(4,128)S(1)}, f32[3,2048]{1,0:T(4,128)S(1)}, u32[]{:S(2)}, u32[]{:S(2)}) collective-permute-start(f32[3,2048]{1,0:T(4,128)S(1)} %pad_add_fusion.3), channel_id=1, source_target_pairs={{4,0},{8,4},{12,8},{5,1},{9,5},{13,9},{6,2},{10,6},{14,10},{7,3},{... | collective-permute-start | bytes 73736 | tf_op jit(solution)/shard_map/ppermute | solution.py:21
  (164 other events, 444.7 us)
Sparse Core Ops, SparseCore 0:
  51.0 80.0 all-gather.6
  280.1 77.4 all-gather.8
where the time goes:
time: 551 us; the launch traced here: 542 us
  local copies, waits for them, and re-layouts  173 us (31%)
  other arithmetic  140 us (25%)
  waiting for transfers between devices  113 us (21%)
  blocking collectives  47.2 us (9%)
  matrix products  37.5 us (7%)
  between operations  15.2 us (3%)
  starting transfers between devices  11 us (2%)
    all_gather x2, waiting for transfers between devices, entering(): pieces = jax.tree.map(lambda part: lax.all_gather(part, axis), value)  113 us
    dynamic_update_slice x20, local copies, waits for them, and re-layouts, scan_blocks(): final_state, outputs = lax.scan(stepper, state_in, pieces)  58.1 us
    psum x1, blocking collectives, per_device(): lax.psum((local_terms[0], local_terms[1], local_terms[2], local_terms[3],...  27.6 us
    dynamic_update_slice x18, other arithmetic, scan_blocks(): final_state, outputs = lax.scan(stepper, state_in, pieces)  19.2 us
    dot_general x6, matrix products, block_terms(): jnp.einsum('ghts,sghp->tghp', weights, block_x, preferred_element_type=jn...  16.6 us
    unnamed x162, local copies, waits for them, and re-layouts  14.1 us
    another operation x24, local copies, waits for them, and re-layouts  12.9 us
  transfers between devices with their start and end apart: 6, of which 2 were waited for; matrix products, arithmetic and copies ran while one was open for 9% of the time, Pallas kernels for 0%

commit v1 on v0

v1 whole, which is shorter than its diff:
```python
import functools

import jax
import jax.numpy as jnp
from jax import lax
from jax.experimental import pallas as pl
from jax.experimental.pallas import tpu as pltpu
from jax.sharding import PartitionSpec as P

HEAD_DIM = 64
NSTATE = 128
CONV = 4
STRETCH = 128
INNER = 8192
HALO = CONV - 1
PAD = 8
CHUNK = 256
PAIR = 2 * HEAD_DIM
NORM_EPS = 1e-05
LOWEST = -1e30
VMEM_LIMIT = 40 * 1024 * 1024

f32 = jnp.float32
bf16 = jnp.bfloat16


def dot(a, b, contract=((1,), (0,))):
    return lax.dot_general(a, b, (contract, ((), ())), preferred_element_type=f32)


def dot_full(a, b):
    return lax.dot_general(
        a, b, (((1,), (0,)), ((), ())), precision=lax.Precision.HIGHEST, preferred_element_type=f32
    )


def iota(shape, dim):
    return lax.broadcasted_iota(jnp.int32, shape, dim)


def split3(value):
    high = value.astype(bf16)
    rest = value - high.astype(f32)
    middle = rest.astype(bf16)
    low = (rest - middle.astype(f32)).astype(bf16)
    return jnp.concatenate([high, middle, low], axis=0)


def spread_heads(rows, width):
    heads = rows.shape[0]
    shape = (heads, heads * width)
    pick = (iota(shape, 1) // width == iota(shape, 0)).astype(f32).astype(bf16)
    return dot(split3(rows), jnp.concatenate([pick] * 3, axis=0), ((0,), (0,)))


def head_sums(value, first, heads):
    shape = (heads, value.shape[1])
    pick = ((iota(shape, 1) + first) // HEAD_DIM == iota(shape, 0)).astype(f32).astype(bf16)
    high = value.astype(bf16)
    low = (value - high.astype(f32)).astype(bf16)
    last = ((1,), (1,))
    return dot(pick, high, last) + dot(pick, low, last)


def as_columns(row):
    return jnp.transpose(jnp.broadcast_to(row, (STRETCH, STRETCH)))


def sigmoid(value):
    return 0.5 * jnp.tanh(0.5 * value) + 0.5


def upper_ones():
    shape = (STRETCH, STRETCH)
    return (iota(shape, 0) <= iota(shape, 1)).astype(f32)


def resets_seen(flags_row):
    flags = jnp.broadcast_to(flags_row.astype(f32), (PAD, STRETCH)).astype(bf16)
    return dot(flags, upper_ones().astype(bf16))[0:1]


def decay_mask(seen):
    shape = (STRETCH, STRETCH)
    same = (as_columns(seen) == jnp.broadcast_to(seen, shape)) & (iota(shape, 0) >= iota(shape, 1))
    return jnp.where(same, 0.0, LOWEST)


def lanes(position, size):
    return pl.ds(pl.multiple_of(position * size, size), size)


def fill_extended(extended, halo_ref, rows_ref):
    extended[0:PAD, :] = halo_ref[...]
    extended[PAD:, :] = rows_ref[...].astype(f32)


def tap(extended, first, lag, part):
    return extended[PAD + first - lag : PAD + first - lag + STRETCH, part]


def conv_taps(extended, live_ref, first, part):
    width = extended[0:PAD, part].shape[1]
    taps = [tap(extended, first, 0, part)]
    for lag in range(1, CONV):
        mask = live_ref[PAD + first : PAD + first + STRETCH, lag - 1 : lag]
        taps.append(tap(extended, first, lag, part) * jnp.broadcast_to(mask, (STRETCH, width)))
    return taps


def conv_sum(taps, weight_ref, bias_ref, part):
    total = bias_ref[0:1, part] + weight_ref[0:1, part] * taps[0]
    for lag in range(1, CONV):
        total = total + weight_ref[lag : lag + 1, part] * taps[lag]
    return total


def conv_and_state(
    x_ref, xh_ref, bc_ref, bch_ref, wx_ref, bx_ref, wb_ref, bb_ref, dt_ref, alog_ref, flags_ref,
    live_ref, xc_ref, xp_ref, bcc_ref, run_ref, keep_ref, sdev_ref, sloc_ref,
    x_ext, bc_ext, dt_wide, end_wide, state,
):
    rows, channels = x_ref.shape
    fill_extended(x_ext, xh_ref, x_ref)
    fill_extended(bc_ext, bch_ref, bc_ref)
    blocks = rows // STRETCH
    rate = jnp.exp(alog_ref[...])
    product = None
    for block in range(blocks):
        first = block * STRETCH
        here = slice(first, first + STRETCH)
        every = slice(None)
        total = conv_sum(conv_taps(bc_ext, live_ref, first, every), wb_ref, bb_ref, every)
        bc_now = (total * sigmoid(total)).astype(bf16)
        bcc_ref[here, :] = bc_now
        b_turned = jnp.transpose(bc_now[:, 0:NSTATE].astype(f32)).astype(bf16)
        seen = resets_seen(flags_ref[:, here])
        dt = dt_ref[:, here]
        running = dot_full(-rate * dt, upper_ones())
        run_ref[:, here] = running
        final = running[:, STRETCH - 1 : STRETCH]
        seen_final = seen[:, STRETCH - 1 : STRETCH]
        to_end = jnp.where(seen == seen_final, jnp.exp(final - running), 0.0)
        keep = jnp.where(seen_final == 0.0, jnp.exp(final), 0.0)
        keep_row = spread_heads(jnp.broadcast_to(keep, (keep.shape[0], STRETCH)), HEAD_DIM)[0:1]
        keep_ref[block : block + 1, :] = keep_row
        product = keep_row if product is None else product * keep_row
        dt_wide[...] = spread_heads(dt, HEAD_DIM)
        end_wide[...] = spread_heads(to_end, HEAD_DIM)

        def chunk(step, carry):
            part = lanes(step, CHUNK)
            total = conv_sum(conv_taps(x_ext, live_ref, first, part), wx_ref, bx_ref, part)
            xc = (total * sigmoid(total)).astype(bf16)
            xc_ref[here, part] = xc
            stepped = (xc.astype(f32) * dt_wide[:, part]).astype(bf16)
            xp_ref[here, part] = stepped
            ended = (stepped.astype(f32) * end_wide[:, part]).astype(bf16)
            fresh = dot(b_turned, ended)
            if block > 0:
                fresh = keep_ref[block : block + 1, part] * state[:, part] + fresh
            if block < blocks - 1:
                state[:, part] = fresh
                sloc_ref[block, :, part] = fresh.astype(bf16)
            else:
                sdev_ref[:, part] = fresh.astype(bf16)
            return carry

        lax.fori_loop(0, channels // CHUNK, chunk, 0)
    keep_ref[blocks : blocks + 1, :] = product


def place_runs(run_ref, here, run_wide, run_tall):
    running = run_ref[:, here]
    run_wide[...] = spread_heads(running, STRETCH)
    for head in range(running.shape[0]):
        run_tall[head * PAD : (head + 1) * PAD, :] = jnp.broadcast_to(
            running[head : head + 1], (PAD, STRETCH)
        )


def block_weights(scores, mask, run_wide, run_tall, head):
    column = run_wide[:, lanes(head, STRETCH)]
    row = run_tall[pl.ds(pl.multiple_of(head * PAD, PAD), PAD), :][0:1]
    segment = jnp.exp(column - row + mask)
    return segment, (scores * segment).astype(bf16)


def both_heads(value):
    is_first = iota(value.shape, 1) < HEAD_DIM
    wide = value.astype(f32)
    zero = jnp.zeros_like(wide)
    return jnp.concatenate(
        [jnp.where(is_first, wide, zero).astype(bf16), jnp.where(is_first, zero, wide).astype(bf16)],
        axis=0,
    )


def within_blocks(xp_ref, bcc_ref, run_ref, flags_ref, y_ref, run_wide, run_tall):
    rows, channels = xp_ref.shape
    for block in range(rows // STRETCH):
        here = slice(block * STRETCH, (block + 1) * STRETCH)
        mask = decay_mask(resets_seen(flags_ref[:, here]))
        scores = dot(bcc_ref[here, NSTATE:], bcc_ref[here, 0:NSTATE], ((1,), (1,)))
        place_runs(run_ref, here, run_wide, run_tall)

        def pair(step, carry):
            _, w_first = block_weights(scores, mask, run_wide, run_tall, 2 * step)
            _, w_second = block_weights(scores, mask, run_wide, run_tall, 2 * step + 1)
            part = lanes(step, PAIR)
            y_ref[here, part] = dot(
                jnp.concatenate([w_first, w_second], axis=1), both_heads(xp_ref[here, part])
            )
            return carry

        lax.fori_loop(0, channels // PAIR, pair, 0)


def start_factor(run_ref, flags_ref, here):
    seen = resets_seen(flags_ref[:, here])
    return spread_heads(jnp.where(seen == 0.0, jnp.exp(run_ref[:, here]), 0.0), HEAD_DIM)


def block_state(block, prior_ref, sloc_ref, keep_ref, part):
    state = prior_ref[:, part]
    if block == 0:
        return state
    whole = keep_ref[0:1, part]
    for step in range(1, block):
        whole = whole * keep_ref[step : step + 1, part]
    return (whole * state.astype(f32) + sloc_ref[block - 1, :, part].astype(f32)).astype(bf16)


def gate_forward(
    y_ref, prior_ref, sloc_ref, keep_ref, bcc_ref, run_ref, flags_ref, xc_ref, skip_ref, z_ref,
    go_ref, gain_ref, yssd_ref, mixed_ref, sums_ref, start_wide,
):
    rows, channels = xc_ref.shape
    for block in range(rows // STRETCH):
        here = slice(block * STRETCH, (block + 1) * STRETCH)
        start_wide[...] = start_factor(run_ref, flags_ref, here)
        c_now = bcc_ref[here, NSTATE:]

        def chunk(step, carry):
            squares, products = carry
            part = lanes(step, CHUNK)
            carried = dot(c_now, block_state(block, prior_ref, sloc_ref, keep_ref, part))
            y_ssd = y_ref[here, part] + carried * start_wide[:, part]
            yssd_ref[here, part] = y_ssd
            mixed = (y_ssd + skip_ref[0:1, part] * xc_ref[here, part].astype(f32)).astype(bf16)
            mixed_ref[here, part] = mixed
            z = z_ref[here, part].astype(f32)
            gated = mixed.astype(f32) * (z * sigmoid(z))
            gained = go_ref[here, part].astype(f32) * gain_ref[0:1, part]
            return squares + gated * gated, products + gated * gained

        zero = jnp.zeros((STRETCH, CHUNK), f32)
        squares, products = lax.fori_loop(0, channels // CHUNK, chunk, (zero, zero))
        square_column = jnp.sum(squares, axis=1, keepdims=True)
        product_column = jnp.sum(products, axis=1, keepdims=True)
        shape = (STRETCH, STRETCH)
        mixed_up = jnp.where(
            iota(shape, 1) == 0,
            jnp.broadcast_to(square_column, shape),
            jnp.broadcast_to(product_column, shape),
        )
        sums_ref[:, here] = jnp.transpose(mixed_up)[0:PAD]


def norm_factors(totals_ref, here):
    squares = totals_ref[0:1, here]
    products = totals_ref[1:2, here]
    inv_rms = lax.rsqrt(squares * (1.0 / INNER) + NORM_EPS)
    pull = inv_rms * inv_rms * inv_rms * products * (1.0 / INNER)
    return (
        jnp.concatenate([as_columns(inv_rms)] * (CHUNK // STRETCH), axis=1),
        jnp.concatenate([as_columns(pull)] * (CHUNK // STRETCH), axis=1),
    )


def gate_backward(
    totals_ref, mixed_ref, z_ref, go_ref, gain_ref, keep_ref, bcc_ref, run_ref, flags_ref,
    dy_ref, adev_ref, aloc_ref, start_wide, adjoint,
):
    rows, channels = mixed_ref.shape
    blocks = rows // STRETCH
    for block in reversed(range(blocks)):
        here = slice(block * STRETCH, (block + 1) * STRETCH)
        start_wide[...] = start_factor(run_ref, flags_ref, here)
        inv_rms, pull = norm_factors(totals_ref, here)
        c_turned = jnp.transpose(bcc_ref[here, NSTATE:].astype(f32)).astype(bf16)

        def chunk(step, carry):
            part = lanes(step, CHUNK)
            z = z_ref[here, part].astype(f32)
            gate = z * sigmoid(z)
            gained = go_ref[here, part].astype(f32) * gain_ref[0:1, part]
            d_gated = gained * inv_rms - mixed_ref[here, part].astype(f32) * gate * pull
            dy = (d_gated * gate).astype(bf16)
            dy_ref[here, part] = dy
            fresh = dot(c_turned, (dy.astype(f32) * start_wide[:, part]).astype(bf16))
            if block < blocks - 1:
                fresh = fresh + keep_ref[block : block + 1, part] * adjoint[:, part]
            if block > 0:
                adjoint[:, part] = fresh
                aloc_ref[block - 1, :, part] = fresh.astype(bf16)
            else:
                adev_ref[:, part] = fresh.astype(bf16)
            return carry

        lax.fori_loop(0, channels // CHUNK, chunk, 0)


def within_backward(
    totals_ref, mixed_ref, z_ref, go_ref, gain_ref, dy_ref, yssd_ref, xc_ref, xp_ref, bcc_ref,
    run_ref, flags_ref, prior_ref, sloc_ref, keep_ref,
    gz_ref, dxp_ref, dbc_ref, drun_ref, chan_ref, run_wide, run_tall, start_wide,
):
    rows, channels = mixed_ref.shape
    heads = run_ref.shape[0]
    chan_ref[...] = jnp.zeros_like(chan_ref)
    for block in range(rows // STRETCH):
        here = slice(block * STRETCH, (block + 1) * STRETCH)
        mask = decay_mask(resets_seen(flags_ref[:, here]))
        b_now = bcc_ref[here, 0:NSTATE]
        c_now = bcc_ref[here, NSTATE:]
        scores = dot(c_now, b_now, ((1,), (1,)))
        place_runs(run_ref, here, run_wide, run_tall)
        start_wide[...] = start_factor(run_ref, flags_ref, here)
        inv_rms, pull = norm_factors(totals_ref, here)

        def chunk(step, carry):
            d_c, d_run = carry
            part = lanes(step, CHUNK)
            z = z_ref[here, part].astype(f32)
            gate_up = sigmoid(z)
            gate = z * gate_up
            go = go_ref[here, part].astype(f32)
            mixed = mixed_ref[here, part].astype(f32)
            gated = mixed * gate
            d_gated = go * gain_ref[0:1, part] * inv_rms - gated * pull
            slope = gate_up + gate * (1.0 - gate_up)
            gz_ref[here, part] = (d_gated * mixed * slope).astype(bf16)
            dy = dy_ref[here, part].astype(f32)
            chan_ref[0:1, part] += jnp.sum(go * gated * inv_rms, axis=0, keepdims=True)
            chan_ref[1:2, part] += jnp.sum(dy * xc_ref[here, part].astype(f32), axis=0, keepdims=True)
            d_run = d_run + head_sums(dy * yssd_ref[here, part], step * CHUNK, heads)
            started = (dy * start_wide[:, part]).astype(bf16)
            state = block_state(block, prior_ref, sloc_ref, keep_ref, part)
            return d_c + dot(started, state, ((1,), (1,))), d_run

        d_c, d_run = lax.fori_loop(
            0,
            channels // CHUNK,
            chunk,
            (jnp.zeros((STRETCH, NSTATE), f32), jnp.zeros((heads, STRETCH), f32)),
        )
        drun_ref[:, here] = d_run

        def pair(step, d_scores):
            part = lanes(step, PAIR)
            s_first, w_first = block_weights(scores, mask, run_wide, run_tall, 2 * step)
            s_second, w_second = block_weights(scores, mask, run_wide, run_tall, 2 * step + 1)
            dy = dy_ref[here, part]
            d_weights = dot(dy, both_heads(xp_ref[here, part]), ((1,), (1,)))
            dxp_ref[here, part] = dot(
                jnp.concatenate([w_first, w_second], axis=0), both_heads(dy), ((0,), (0,))
            )
            return (
                d_scores + d_weights[:, 0:STRETCH] * s_first + d_weights[:, STRETCH:] * s_second
            )

        d_scores = lax.fori_loop(
            0, channels // PAIR, pair, jnp.zeros((STRETCH, STRETCH), f32)
        ).astype(bf16)
        dbc_ref[here, 0:NSTATE] = dot(d_scores, c_now, ((0,), (0,)))
        dbc_ref[here, NSTATE:] = d_c + dot(d_scores, b_now)


def conv_backward(
    extended, d_ext, live_ref, weight_ref, bias_ref, d_ref, grad_ref, tail_ref, back_ref, dw_ref,
    rows, part,
):
    width = d_ref[0:PAD, part].shape[1]
    sums = None
    for first in range(0, rows, STRETCH):
        taps = conv_taps(extended, live_ref, first, part)
        total = conv_sum(taps, weight_ref, bias_ref, part)
        up = sigmoid(total)
        d_total = d_ref[first : first + STRETCH, part] * (up + total * up * (1.0 - up))
        d_ext[PAD + first : PAD + first + STRETCH, part] = d_total
        now = [jnp.sum(d_total * each, axis=0, keepdims=True) for each in taps]
        now.append(jnp.sum(d_total, axis=0, keepdims=True))
        sums = now if sums is None else [old + new for old, new in zip(sums, now)]
    for row, value in enumerate(sums):
        dw_ref[row : row + 1, part] = value
    for first, count in [(-PAD, PAD)] + [(at, STRETCH) for at in range(0, rows, STRETCH)]:
        begin = PAD + first
        grad = weight_ref[0:1, part] * d_ext[begin : begin + count, part]
        for lag in range(1, CONV):
            mask = live_ref[begin : begin + count, HALO + lag - 1 : HALO + lag]
            grad = grad + weight_ref[lag : lag + 1, part] * (
                d_ext[begin + lag : begin + lag + count, part]
                * jnp.broadcast_to(mask, (count, width))
            )
        if first < 0:
            back_ref[:, part] = grad
        else:
            grad_ref[first : first + count, part] = grad.astype(bf16)
            if first + count == rows:
                tail_ref[:, part] = grad[count - PAD :]


def finish_backward(
    later_ref, aloc_ref, prior_ref, sloc_ref, keep_ref, dxp_ref, dbc_ref, drun_ref, xp_ref, dy_ref,
    skip_ref, bcc_ref, run_ref, dt_ref, flags_ref, live_ref, x_ref, xh_ref, bc_ref, bch_ref,
    wx_ref, bx_ref, wb_ref, bb_ref, alog_ref, dtb_ref, dtr_ref,
    gx_ref, xtail_ref, xback_ref, dwx_ref, gbc_ref, bctail_ref, bcback_ref, dwb_ref, gdt_ref,
    heads_ref, x_ext, bc_ext, dx_ext, dbc_ext, d_x, d_bc, dt_wide, end_wide, ends,
):
    rows, channels = xp_ref.shape
    heads = run_ref.shape[0]
    blocks = rows // STRETCH
    fill_extended(x_ext, xh_ref, x_ref)
    fill_extended(bc_ext, bch_ref, bc_ref)
    for ext in (dx_ext, dbc_ext):
        ext[0:PAD, :] = jnp.zeros((PAD, ext.shape[1]), f32)
        ext[PAD + rows :, :] = jnp.zeros((PAD, ext.shape[1]), f32)
    rate = jnp.exp(alog_ref[...])
    d_alog = jnp.zeros((heads, 1), f32)
    d_dtb = jnp.zeros((heads, 1), f32)
    for block in range(blocks):
        here = slice(block * STRETCH, (block + 1) * STRETCH)
        seen = resets_seen(flags_ref[:, here])
        running = run_ref[:, here]
        dt = dt_ref[:, here]
        to_end = jnp.where(
            seen == seen[:, STRETCH - 1 : STRETCH],
            jnp.exp(running[:, STRETCH - 1 : STRETCH] - running),
            0.0,
        )
        dt_wide[...] = spread_heads(dt, HEAD_DIM)
        end_wide[...] = spread_heads(to_end, HEAD_DIM)
        b_now = bcc_ref[here, 0:NSTATE]

        def chunk(step, carry):
            d_b, per_step = carry
            part = lanes(step, CHUNK)
            later = later_ref[:, part]
            if block < blocks - 1:
                whole = keep_ref[block + 1 : block + 2, part]
                for place in range(block + 2, blocks):
                    whole = whole * keep_ref[place : place + 1, part]
                later = (aloc_ref[block, :, part].astype(f32) + whole * later.astype(f32)).astype(bf16)
            state = block_state(block, prior_ref, sloc_ref, keep_ref, part)
            d_keep = jnp.sum(later.astype(f32) * state.astype(f32), axis=0, keepdims=True)
            stepped = xp_ref[here, part].astype(f32)
            end = end_wide[:, part]
            d_end = dot(b_now, later) * end
            d_stepped = dxp_ref[here, part] + d_end
            ended = stepped * end
            ends[0:1, part] = (
                jnp.sum(stepped * d_end, axis=0, keepdims=True)
                + d_keep * keep_ref[block : block + 1, part]
            )
            d_x[here, part] = d_stepped * dt_wide[:, part] + skip_ref[0:1, part] * dy_ref[
                here, part
            ].astype(f32)
            return (
                d_b + dot(ended.astype(bf16), later, ((1,), (1,))),
                per_step + head_sums(stepped * d_stepped, step * CHUNK, heads),
            )

        d_b, per_step = lax.fori_loop(
            0,
            channels // CHUNK,
            chunk,
            (jnp.zeros((STRETCH, NSTATE), f32), jnp.zeros((heads, STRETCH), f32)),
        )
        d_bc[here, 0:NSTATE] = dbc_ref[here, 0:NSTATE] + d_b
        d_bc[here, NSTATE:] = dbc_ref[here, NSTATE:]
        at_end = head_sums(jnp.broadcast_to(ends[0:1, :], (STRETCH, channels)), 0, heads)
        is_last = iota((heads, STRETCH), 1) == STRETCH - 1
        d_run = drun_ref[:, here] - per_step + jnp.where(is_last, at_end, 0.0)
        shape = (STRETCH, STRETCH)
        d_log = dot_full(d_run, (iota(shape, 0) >= iota(shape, 1)).astype(f32))
        d_dt = per_step / dt - rate * d_log
        raw = dtr_ref[:, here].astype(f32) + dtb_ref[...]
        d_raw = d_dt / (1.0 + jnp.exp(-raw))
        gdt_ref[:, here] = d_raw
        d_alog = d_alog - jnp.sum(d_log * dt, axis=1, keepdims=True) * rate
        d_dtb = d_dtb + jnp.sum(d_raw, axis=1, keepdims=True)
    shape = heads_ref.shape
    heads_ref[...] = jnp.where(
        iota(shape, 1) == 0, jnp.broadcast_to(d_alog, shape), jnp.broadcast_to(d_dtb, shape)
    )

    def conv_chunk(step, carry):
        conv_backward(
            x_ext, dx_ext, live_ref, wx_ref, bx_ref, d_x, gx_ref, xtail_ref, xback_ref, dwx_ref,
            rows, lanes(step, STRETCH),
        )
        return carry

    lax.fori_loop(0, channels // STRETCH, conv_chunk, 0)
    for step in range(2):
        conv_backward(
            bc_ext, dbc_ext, live_ref, wb_ref, bb_ref, d_bc, gbc_ref, bctail_ref, bcback_ref,
            dwb_ref, rows, slice(step * NSTATE, (step + 1) * NSTATE),
        )


def call(kernel, operands, outs, scratch, flops, name):
    specs, arrays, count = [], [], 0
    for array, block, index in operands:
        block = array.shape if block is None else block
        index = (0,) * len(block) if index is None else index
        specs.append(pl.BlockSpec(block, functools.partial(lambda fixed, i: fixed, index)))
        arrays.append(array)
        size = 1
        for extent in block:
            size *= extent
        count += size * array.dtype.itemsize
    shapes = [jax.ShapeDtypeStruct(shape, dtype) for shape, dtype in outs]
    out_specs = [
        pl.BlockSpec(shape, functools.partial(lambda rank, i: (0,) * rank, len(shape)))
        for shape, _ in outs
    ]
    for shape in shapes:
        count += shape.size * shape.dtype.itemsize
    return pl.pallas_call(
        kernel,
        grid=(1,),
        in_specs=specs,
        out_specs=out_specs,
        out_shape=shapes,
        scratch_shapes=[pltpu.VMEM(shape, f32) for shape in scratch],
        compiler_params=pltpu.CompilerParams(vmem_limit_bytes=VMEM_LIMIT),
        cost_estimate=pl.CostEstimate(flops=flops, bytes_accessed=count, transcendentals=0),
        name=name,
    )(*arrays)


def chain(parts, decays, axis, backward):
    count = lax.axis_size(axis)
    arrived = [jnp.zeros(part.shape, bf16) for part in parts]
    for hop in range(count - 1):
        pairs = [(count - 1 - hop, count - 2 - hop)] if backward else [(hop, hop + 1)]
        for place, part in enumerate(parts):
            leaving = part
            if hop > 0:
                leaving = (decays[place] * arrived[place].astype(f32) + part.astype(f32)).astype(bf16)
            moved = lax.ppermute(leaving, axis, pairs)
            arrived[place] = moved if hop == 0 else arrived[place] + moved
    return arrived


def exchange_sum(value, axis):
    count = lax.axis_size(axis)
    stride = 1
    while stride < count:
        value = value + lax.ppermute(value, axis, [(i, i ^ stride) for i in range(count)])
        stride *= 2
    return value


def per_device(
    x_raw, bc_raw, z_gate, dt_raw, resets, conv_x_weight, conv_x_bias, conv_bc_weight,
    conv_bc_bias, a_log, dt_bias, skip_weight, norm_gain, grad_out,
):
    rows, inner = x_raw.shape[1:]
    groups = bc_raw.shape[3] // NSTATE
    heads = a_log.shape[0] // groups
    channels = inner // groups
    blocks = rows // STRETCH
    width = 2 * NSTATE

    def by_group(value):
        lead = value.shape[:-2]
        split = value.reshape(lead + (2, groups, NSTATE))
        return jnp.moveaxis(split, -3, -2).reshape(lead + (groups * width,))

    x_own, z_own, go_own, dt_own = x_raw[0], z_gate[0], grad_out[0], dt_raw[0]
    bc_own = by_group(bc_raw[0])
    flags = resets
    clear = 1.0 - resets[0].astype(f32)
    tail_keep = jnp.stack([clear[-1] * clear[-2], clear[-1], jnp.ones((), f32)])[:, None]
    tails = jnp.concatenate([x_own[-HALO:], bc_own[-HALO:]], axis=1) * tail_keep.astype(bf16)
    count = lax.axis_size("ctx")
    halo = lax.ppermute(tails, "ctx", [(i, i + 1) for i in range(count - 1)])
    halo = jnp.pad(halo.astype(f32), ((PAD - HALO, 0), (0, 0)))
    x_halo, bc_halo = halo[:, :inner], halo[:, inner:]
    one = jnp.ones((HALO,), f32)
    before = jnp.concatenate([one, clear])
    live = [clear]
    for lag in range(2, CONV):
        live.append(live[-1] * before[HALO + 1 - lag : HALO + 1 - lag + rows])
    back_live = [
        jnp.concatenate([jnp.zeros((PAD - lag,), f32), mask, jnp.zeros((lag,), f32)])
        for lag, mask in enumerate(live, 1)
    ]
    live = [jnp.concatenate([jnp.zeros((PAD,), f32), mask]) for mask in live]
    live = jnp.stack(live + back_live + [jnp.zeros((rows + PAD,), f32)] * 2, axis=1)
    dt = jax.nn.softplus(dt_own.astype(f32) + dt_bias[:, None])
    alog_column, dtb_column = a_log[:, None], dt_bias[:, None]
    bx, gain = conv_x_bias[None], norm_gain[None]
    wb, bb = by_group(conv_bc_weight), by_group(conv_bc_bias)[None]
    skip = jnp.repeat(skip_weight, HEAD_DIM)[None]

    def wide(array, group):
        return (array, (array.shape[0], channels), (0, group))

    def narrow(array, group):
        return (array, (array.shape[0], width), (0, group))

    def per_head(array, group):
        return (array, (heads, array.shape[1]), (group, 0))

    def whole(array):
        return (array, None, None)

    keep_rows = -(-(blocks + 1) // PAD) * PAD
    tall = (rows, channels)
    state_shape = (NSTATE, channels)
    local_shape = (blocks - 1, NSTATE, channels)
    work = rows * channels * STRETCH
    group_range = range(groups)
    held = []
    for g in group_range:
        held.append(
            call(
                conv_and_state,
                [
                    wide(x_own, g), wide(x_halo, g), narrow(bc_own, g), narrow(bc_halo, g),
                    wide(conv_x_weight, g), wide(bx, g), narrow(wb, g), narrow(bb, g),
                    per_head(dt, g), per_head(alog_column, g), whole(flags), whole(live),
                ],
                [
                    (tall, bf16), (tall, bf16), ((rows, width), bf16), ((heads, rows), f32),
                    ((keep_rows, channels), f32), (state_shape, bf16), (local_shape, bf16),
                ],
                [
                    (rows + PAD, channels), (rows + PAD, width), (STRETCH, channels),
                    (STRETCH, channels), state_shape,
                ],
                2 * work,
                "conv_and_state",
            )
        )
    xc, xp, bcc, run, keep, s_dev, s_loc = zip(*held)
    decay = [k[blocks : blocks + 1] for k in keep]
    prior = chain(s_dev, decay, "ctx", False)
    y_within = [
        call(
            within_blocks,
            [whole(xp[g]), whole(bcc[g]), whole(run[g]), whole(flags)],
            [(tall, f32)],
            [(STRETCH, heads * STRETCH), (heads * PAD, STRETCH)],
            6 * work,
            "within_blocks",
        )[0]
        for g in group_range
    ]
    held = [
        call(
            gate_forward,
            [
                whole(y_within[g]), whole(prior[g]), whole(s_loc[g]), whole(keep[g]), whole(bcc[g]),
                whole(run[g]), whole(flags), whole(xc[g]), wide(skip, g), wide(z_own, g),
                wide(go_own, g), wide(gain, g),
            ],
            [(tall, f32), (tall, bf16), ((PAD, rows), f32)],
            [(STRETCH, channels)],
            2 * work,
            "gate_forward",
        )
        for g in group_range
    ]
    y_ssd, mixed, sums = zip(*held)
    totals = exchange_sum(sum(sums[1:], sums[0]), "head")
    held = [
        call(
            gate_backward,
            [
                whole(totals), whole(mixed[g]), wide(z_own, g), wide(go_own, g), wide(gain, g),
                whole(keep[g]), whole(bcc[g]), whole(run[g]), whole(flags),
            ],
            [(tall, bf16), (state_shape, bf16), (local_shape, bf16)],
            [(STRETCH, channels), state_shape],
            2 * work,
            "gate_backward",
        )
        for g in group_range
    ]
    dy, a_dev, a_loc = zip(*held)
    later = chain(a_dev, decay, "ctx", True)
    held = [
        call(
            within_backward,
            [
                whole(totals), whole(mixed[g]), wide(z_own, g), wide(go_own, g), wide(gain, g),
                whole(dy[g]), whole(y_ssd[g]), whole(xc[g]), whole(xp[g]), whole(bcc[g]),
                whole(run[g]), whole(flags), whole(prior[g]), whole(s_loc[g]), whole(keep[g]),
            ],
            [
                (tall, bf16), (tall, f32), ((rows, width), f32), ((heads, rows), f32),
                ((PAD, channels), f32),
            ],
            [(STRETCH, heads * STRETCH), (heads * PAD, STRETCH), (STRETCH, channels)],
            10 * work,
            "within_backward",
        )
        for g in group_range
    ]
    gz, dxp, dbc, drun, chan = zip(*held)
    held = [
        call(
            finish_backward,
            [
                whole(later[g]), whole(a_loc[g]), whole(prior[g]), whole(s_loc[g]), whole(keep[g]),
                whole(dxp[g]), whole(dbc[g]), whole(drun[g]), whole(xp[g]), whole(dy[g]),
                wide(skip, g), whole(bcc[g]), whole(run[g]), per_head(dt, g), whole(flags),
                whole(live), wide(x_own, g), wide(x_halo, g), narrow(bc_own, g), narrow(bc_halo, g),
                wide(conv_x_weight, g), wide(bx, g), narrow(wb, g), narrow(bb, g),
                per_head(alog_column, g), per_head(dtb_column, g), per_head(dt_own, g),
            ],
            [
                (tall, bf16), ((PAD, channels), f32), ((PAD, channels), f32), ((PAD, channels), f32),
                ((rows, width), bf16), ((PAD, width), f32), ((PAD, width), f32), ((PAD, width), f32),
                ((heads, rows), f32), ((heads, STRETCH), f32),
            ],
            [
                (rows + PAD, channels), (rows + PAD, width), (rows + 2 * PAD, channels),
                (rows + 2 * PAD, width), tall, (rows, width), (STRETCH, channels),
                (STRETCH, channels), (PAD, channels),
            ],
            4 * work,
            "finish_backward",
        )
        for g in group_range
    ]
    gx, x_tail, x_back, dwx, gbc, bc_tail, bc_back, dwb, gdt, head_terms = zip(*held)

    def joined(pieces):
        return jnp.concatenate(pieces, axis=1)

    back = joined(x_back + bc_back)[PAD - HALO :]
    back = lax.ppermute(back, "ctx", [(i + 1, i) for i in range(count - 1)])
    ending = (joined(x_tail + bc_tail)[PAD - HALO :] + back * tail_keep).astype(bf16)
    grad_x = lax.dynamic_update_slice(joined(gx), ending[:, :inner], (rows - HALO, 0))
    grad_bc = lax.dynamic_update_slice(joined(gbc), ending[:, inner:], (rows - HALO, 0))

    def ungroup(value):
        lead = value.shape[:-1]
        split = value.reshape(lead + (groups, 2, NSTATE))
        return jnp.moveaxis(split, -3, -2).reshape(lead + (2, groups * NSTATE))

    chan_all, dwx_all, dwb_all = joined(chan), joined(dwx), joined(dwb)
    head_all = jnp.concatenate(head_terms, axis=0)[:, :2]
    pieces = [
        dwx_all[: CONV + 1].reshape(-1),
        dwb_all[: CONV + 1].reshape(-1),
        chan_all[0],
        jnp.sum(chan_all[1].reshape(-1, HEAD_DIM), axis=1),
        head_all[:, 0],
        head_all[:, 1],
    ]
    sizes = [piece.shape[0] for piece in pieces]
    flat = jnp.concatenate(pieces)
    flat = exchange_sum(exchange_sum(flat, "dp"), "ctx")
    flat = flat * float(lax.axis_size("dp") * count * rows) ** (-0.5)
    cut, at = [], 0
    for size in sizes:
        cut.append(flat[at : at + size])
        at += size
    x_terms = cut[0].reshape(CONV + 1, inner)
    bc_terms = ungroup(cut[1].reshape(CONV + 1, groups * width))
    return (
        grad_x[None],
        ungroup(grad_bc)[None],
        joined(gz)[None],
        jnp.concatenate(gdt, axis=0)[None],
        x_terms[:CONV],
        x_terms[CONV],
        bc_terms[:CONV],
        bc_terms[CONV],
        cut[4],
        cut[5],
        cut[3],
        cut[2],
    )


def solution(mesh):
    return jax.shard_map(
        per_device,
        mesh=mesh,
        in_specs=(
            P("dp", "ctx", "head"),
            P("dp", "ctx", None, "head"),
            P("dp", "ctx", "head"),
            P("dp", "head", "ctx"),
            P("dp", "ctx"),
            P(None, "head"),
            P("head"),
            P(None, None, "head"),
            P(None, "head"),
            P("head"),
            P("head"),
            P("head"),
            P("head"),
            P("dp", "ctx", "head"),
        ),
        out_specs=(
            P("dp", "ctx", "head"),
            P("dp", "ctx", None, "head"),
            P("dp", "ctx", "head"),
            P("dp", "head", "ctx"),
            P(None, "head"),
            P("head"),
            P(None, None, "head"),
            P(None, "head"),
            P("head"),
            P("head"),
            P("head"),
            P("head"),
        ),
        check_vma=False,
    )
```

time: 551 us -> 159 us (0.29); the launches traced: 542 us -> 158 us
  local copies, waits for them, and re-layouts: 173 us -> 25.4 us
  other arithmetic: 140 us -> 13.3 us
  waiting for transfers between devices: 113 us -> 28.9 us
  Pallas kernels: 0 us -> 58.2 us
  blocking collectives: 47.2 us -> 0 us
  matrix products: 37.5 us -> 0 us
  starting transfers between devices: 11 us -> 27.7 us
  between operations: 15.2 us -> 4.09 us
    all_gather x2 -> x0, waiting for transfers between devices: 113 us -> none  [entering(): pieces = jax.tree.map(lambda part: lax.all_gather(part, axis), value)]
    pallas_call x0 -> x12, Pallas kernels: none -> 58.2 us  [call(): pl.pallas_call(kernel, grid=(1,), in_specs=specs, out_specs=out_specs, ou...]
    dynamic_update_slice x20 -> x2, local copies, waits for them, and re-layouts: 58.1 us -> 0.31 us  [the longest x1 0.17 us: per_device(): lax.dynamic_update_slice(joined(gx), ending[:, :inner], (rows - HALO, 0))]
    psum x2 -> x0, blocking collectives: 37.7 us -> none  [the longest x1 27.6 us: per_device(): lax.psum((local_terms[0], local_terms[1], local_terms[2], local_terms[3],...]
    dot_general x28 -> x0, matrix products: 37.5 us -> none  [the longest x6 16.6 us: block_terms(): jnp.einsum('ghts,sghp->tghp', weights, block_x, preferred_element_type=jn...]
    ppermute x4 -> x19, waiting for transfers between devices: 0.01 us -> 28.9 us  [the longest x12 19.9 us: chain(): moved = lax.ppermute(leaving, axis, pairs)]
    reduce_sum x14 -> x1, other arithmetic: 25.3 us -> 0.12 us  [per_device(): jnp.sum(chan_all[1].reshape(-1, HEAD_DIM), axis=1)]
    mul x24 -> x3, other arithmetic: 21 us -> 0.16 us  [the longest x1 0.08 us: per_device(): jnp.concatenate([x_own[-HALO:], bc_own[-HALO:]], axis=1)]
  transfers between devices with their start and end apart: 6 -> 19, of which waited for: 2 -> 8; matrix products, arithmetic and copies ran while one was open for 9% -> 10% of each run, Pallas kernels for 0% -> 25%
where the time goes in v1:
time: 159 us; the launch traced here: 158 us
  Pallas kernels  58.2 us (37%)
  waiting for transfers between devices  28.9 us (18%)
  starting transfers between devices  27.7 us (17%)
  local copies, waits for them, and re-layouts  25.4 us (16%)
  other arithmetic  13.3 us (8%)
  between operations  4.09 us (3%)
    pallas_call x12, Pallas kernels, call(): pl.pallas_call(kernel, grid=(1,), in_specs=specs, out_specs=out_specs, ou...  58.2 us
    ppermute x12, waiting for transfers between devices, chain(): moved = lax.ppermute(leaving, axis, pairs)  19.9 us
    ppermute x12, starting transfers between devices, chain(): moved = lax.ppermute(leaving, axis, pairs)  14.7 us
    unnamed x262, local copies, waits for them, and re-layouts  14 us
    ppermute x5, waiting for transfers between devices, exchange_sum(): lax.ppermute(value, axis, [(i, i ^ stride) for i in range(count)])  8.76 us
    ppermute x5, starting transfers between devices, exchange_sum(): lax.ppermute(value, axis, [(i, i ^ stride) for i in range(count)])  6.77 us
    ppermute x1, starting transfers between devices, per_device(): halo = lax.ppermute(tails, 'ctx', [(i, i + 1) for i in range(count - 1)])  4.92 us
    convert_element_type x8, other arithmetic, chain(): (decays[place] * arrived[place].astype(f32) + part.astype(f32)).astype(bf16)  4.55 us
  transfers between devices with their start and end apart: 19, of which 8 were waited for; matrix products, arithmetic and copies ran while one was open for 10% of the time, Pallas kernels for 25%

profile of v1, /device:TPU:0, one launch (start us, length us, event | category | flops | bytes accessed | tf_op | source)
XLA Modules:
  0.0 157.6 jit_solution(16115416425788799085)
XLA Ops:
  6.1 4.9 %collective-permute-start = (bf16[3,2560]{1,0:T(4,128)(2,1)S(1)}, bf16[3,2560]{1,0:T(4,128)(2,1)S(1)}, u32[]{:S(2)}, u32[]{:S(2)}) collective-permute-start(bf16[3,2560]{1,0:T(4,128)(2,1)S(1)} %maximum_multiply_fusion), channel_id=1, source_target_pairs={{0,4},{4,8},{8,12},{1,5},{5,9},{9,13},{2,6},{6,10},{10,14},{3,7},{... | collective-permute-start | bytes 46088 | tf_op jit(solution)/shard_map/ppermute | solution.py:590
  15.1 4.4 %conv_and_state.2 = (bf16[256,1024]{1,0:T(8,128)(2,1)S(1)}, bf16[256,1024]{1,0:T(8,128)(2,1)S(1)}, bf16[256,256]{1,0:T(8,128)(2,1)S(1)}, f32[16,256]{1,0:T(8,128...) custom-call(bf16[256,2048]{1,0:T(8,128)(2,1)S(1)} %bitcast.56, ...), custom_call_target="tpu_custom_call" | custom-call | flops 67108864 | bytes 2500928 | tf_op jit(solution)/shard_map/conv_and_state/pallas_call | solution.py:531
  20.3 3.5 %collective-permute-start.1 = (bf16[128,1024]{1,0:T(8,128)(2,1)S(1)}, bf16[128,1024]{1,0:T(8,128)(2,1)S(1)}, u32[]{:S(2)}, u32[]{:S(2)}) collective-permute-start(bf16[128,1024]{1,0:T(8,128)(2,1)S(1)} %get-tuple-element.71), channel_id=1, source_target_pairs={{0,4},{1,5},{2,6},{3,7},{16,20},{17,21},{18,22},{19,23}} | collective-permute-start | bytes 786440 | tf_op jit(solution)/shard_map/ppermute | solution.py:553
  23.8 4.4 %conv_and_state.3 = (bf16[256,1024]{1,0:T(8,128)(2,1)S(1)}, bf16[256,1024]{1,0:T(8,128)(2,1)S(1)}, bf16[256,256]{1,0:T(8,128)(2,1)S(1)}, f32[16,256]{1,0:T(8,128...) custom-call(bf16[256,2048]{1,0:T(8,128)(2,1)S(1)} %bitcast.57, ...), custom_call_target="tpu_custom_call" | custom-call | flops 67108864 | bytes 2500928 | tf_op jit(solution)/shard_map/conv_and_state/pallas_call | solution.py:531
  30.5 4.4 %collective-permute-done.4 = bf16[128,1024]{1,0:T(8,128)(2,1)S(1)} collective-permute-done((bf16[128,1024]{1,0:T(8,128)(2,1)S(1)}, bf16[128,1024]{1,0:T(8,128)(2,1)S(1)}, u32[]{:S(2)}, u32[]{:S(2)}) %collective-permute-start.4) | collective-permute-done | bytes 262176 | tf_op jit(solution)/shard_map/ppermute | solution.py:553
  39.0 1.4 collective-permute-start.6
  41.2 3.4 %within_blocks.2.y_ref = f32[256,1024]{1,0:T(8,128)S(1)} custom-call(bf16[256,1024]{1,0:T(8,128)(2,1)S(1)} %get-tuple-element.68.xp_ref, bf16[256,256]{1,0:T(8,128)(2,1)S(1)} %get-tuple-element.69.bcc_ref, f32[16,256]{1,0:T(8,128)S(1)} %get-tuple-element.70.run_ref, s32[1,256]{1,0:T(1,128)S(1)} %copy-done.105), custom_call_target="tpu_custom_call" | custom-call | flops 201326592 | bytes 1721344 | tf_op jit(solution)/shard_map/within_blocks/pallas_call | solution.py:531
  47.3 3.4 %within_blocks.3.y_ref = f32[256,1024]{1,0:T(8,128)S(1)} custom-call(bf16[256,1024]{1,0:T(8,128)(2,1)S(1)} %copy-done.7, bf16[256,256]{1,0:T(8,128)(2,1)S(1)} %copy-done.21, f32[16,256]{1,0:T(8,128)S(1)} %copy-done.83, s32[1,256]{1,0:T(1,128)S(1)} %copy-done.105), custom_call_target="tpu_custom_call" | custom-call | flops 201326592 | bytes 1721344 | tf_op jit(solution)/shard_map/within_blocks/pallas_call | solution.py:531
  51.9 2.8 %gate_forward.2 = (f32[256,1024]{1,0:T(8,128)S(1)}, bf16[256,1024]{1,0:T(8,128)(2,1)S(1)}, f32[8,256]{1,0:T(8,128)S(1)}) custom-call(f32[256,1024]{1,0:T(8,128)S(1)} %within_blocks.2.y_ref, bf16[128,1024]{1,0:T(8,128)(2,1)S(1)} %add.97.prior_ref, bf16[1,128,1024]{2,1,0:T(8,128)(2,1)S(1)} %copy-done.26, f32[8,1024]{1,0:T(8,128)S(1)} %copy-done.64, ...), custom_call_target="tpu_custom_call" | custom-call | flops 67108864 | bytes 4916224 | tf_op jit(solution)/shard_map/gate_forward/pallas_call | solution.py:531
  57.6 2.8 %gate_forward.3 = (f32[256,1024]{1,0:T(8,128)S(1)}, bf16[256,1024]{1,0:T(8,128)(2,1)S(1)}, f32[8,256]{1,0:T(8,128)S(1)}) custom-call(f32[256,1024]{1,0:T(8,128)S(1)} %within_blocks.3.y_ref, bf16[128,1024]{1,0:T(8,128)(2,1)S(1)} %add.101.prior_ref, bf16[1,128,1024]{2,1,0:T(8,128)(2,1)S(1)} %copy-done.30, f32[8,1024]{1,0:T(8,128)S(1)} %copy-done.68, ...), custom_call_target="tpu_custom_call" | custom-call | flops 67108864 | bytes 4916224 | tf_op jit(solution)/shard_map/gate_forward/pallas_call | solution.py:531
  62.2 1.5 collective-permute-start.7
  63.7 2.2 %collective-permute-done.7 = f32[8,256]{1,0:T(8,128)S(1)} collective-permute-done((f32[8,256]{1,0:T(8,128)S(1)}, f32[8,256]{1,0:T(8,128)S(1)}, u32[]{:S(2)}, u32[]{:S(2)}) %collective-permute-start.7) | collective-permute-done | bytes 8224 | tf_op jit(solution)/shard_map/ppermute | solution.py:562
  66.4 1.5 collective-permute-start.8
  74.6 2.6 %gate_backward.3 = (bf16[256,1024]{1,0:T(8,128)(2,1)S(1)}, bf16[128,1024]{1,0:T(8,128)(2,1)S(1)}, bf16[1,128,1024]{2,1,0:T(8,128)(2,1)S(1)}) custom-call(f32[8,256]{1,0:T(8,128)S(1)} %add.104.totals_ref, bf16[256,1024]{1,0:T(8,128)(2,1)S(1)} %copy-done.46, bf16[256,2048]{1,0:T(8,128)(2,1)S(1)} %bitcast.46, bf16[256,2048]{1,0:T(8,128)(2,1)S(1)} %bitcast.52, ...), custom_call_target="tpu_custom_call" | custom-call | flops 67108864 | bytes 2814976 | tf_op jit(solution)/shard_map/gate_backward/pallas_call | solution.py:531
  78.7 2.6 %gate_backward.2 = (bf16[256,1024]{1,0:T(8,128)(2,1)S(1)}, bf16[128,1024]{1,0:T(8,128)(2,1)S(1)}, bf16[1,128,1024]{2,1,0:T(8,128)(2,1)S(1)}) custom-call(f32[8,256]{1,0:T(8,128)S(1)} %add.104.totals_ref, bf16[256,1024]{1,0:T(8,128)(2,1)S(1)} %copy-done.44, bf16[256,2048]{1,0:T(8,128)(2,1)S(1)} %bitcast.47, bf16[256,2048]{1,0:T(8,128)(2,1)S(1)} %bitcast.53, ...), custom_call_target="tpu_custom_call" | custom-call | flops 67108864 | bytes 2814976 | tf_op jit(solution)/shard_map/gate_backward/pallas_call | solution.py:531
  83.0 6.9 %within_backward.3 = (bf16[256,1024]{1,0:T(8,128)(2,1)S(1)}, f32[256,1024]{1,0:T(8,128)S(1)}, f32[256,256]{1,0:T(8,128)S(1)}, f32[16,256]{1,0:T(8,128)S(1)}, f32[8,1024]{1,0:T(8,128)S(1)}) custom-call(f32[8,256]{1,0:T(8,128)S(1)} %add.104.totals_ref, bf16[256,1024]{1,0:T(8,128)(2,1)S(1)} %copy-done.47, bf16[256,2048]{1,0:T(8,128)(2,1)S(1)} %bitcast.48, ...), custom_call_target="tpu_custom_call" | custom-call | flops 335544320 | bytes 6796288 | tf_op jit(solution)/shard_map/within_backward/pallas_call | solution.py:531
  90.1 6.9 %within_backward.2 = (bf16[256,1024]{1,0:T(8,128)(2,1)S(1)}, f32[256,1024]{1,0:T(8,128)S(1)}, f32[256,256]{1,0:T(8,128)S(1)}, f32[16,256]{1,0:T(8,128)S(1)}, f32[8,1024]{1,0:T(8,128)S(1)}) custom-call(f32[8,256]{1,0:T(8,128)S(1)} %add.104.totals_ref, bf16[256,1024]{1,0:T(8,128)(2,1)S(1)} %copy-done.44, bf16[256,2048]{1,0:T(8,128)(2,1)S(1)} %bitcast.49, ...), custom_call_target="tpu_custom_call" | custom-call | flops 335544320 | bytes 6796288 | tf_op jit(solution)/shard_map/within_backward/pallas_call | solution.py:531
  103.8 1.4 collective-permute-start.11
  106.4 15.5 %collective-permute-done.14 = bf16[128,1024]{1,0:T(8,128)(2,1)S(1)} collective-permute-done((bf16[128,1024]{1,0:T(8,128)(2,1)S(1)}, bf16[128,1024]{1,0:T(8,128)(2,1)S(1)}, u32[]{:S(2)}, u32[]{:S(2)}) %collective-permute-start.14) | collective-permute-done | bytes 262176 | tf_op jit(solution)/shard_map/ppermute | solution.py:553
  122.3 9.0 %finish_backward.3 = (bf16[256,1024]{1,0:T(8,128)(2,1)S(1)}, f32[8,1024]{1,0:T(8,128)S(1)}, f32[8,1024]{1,0:T(8,128)S(1)}, f32[8,1024]{1,0:T(8,128)S(1)}, bf16[2...) custom-call(bf16[128,1024]{1,0:T(8,128)(2,1)S(1)} %add.112.later_ref, ...), custom_call_target="tpu_custom_call" | custom-call | flops 134217728 | bytes 5167488 | tf_op jit(solution)/shard_map/finish_backward/pallas_call | solution.py:531
  132.4 9.0 %finish_backward.2 = (bf16[256,1024]{1,0:T(8,128)(2,1)S(1)}, f32[8,1024]{1,0:T(8,128)S(1)}, f32[8,1024]{1,0:T(8,128)S(1)}, f32[8,1024]{1,0:T(8,128)S(1)}, bf16[2...) custom-call(bf16[128,1024]{1,0:T(8,128)(2,1)S(1)} %add.108.later_ref, ...), custom_call_target="tpu_custom_call" | custom-call | flops 134217728 | bytes 5167488 | tf_op jit(solution)/shard_map/finish_backward/pallas_call | solution.py:531
  144.3 2.7 %collective-permute-start.17 = (f32[14944]{0:T(1024)S(1)}, f32[14944]{0:T(1024)S(1)}, u32[]{:S(2)}, u32[]{:S(2)}) collective-permute-start(f32[14944]{0:T(1024)S(1)} %add.114), channel_id=1, source_target_pairs={{0,4},{4,0},{8,12},{12,8},{1,5},{5,1},{9,13},{13,9},{2,6},{6,2},{1... | collective-permute-start | bytes 179336 | tf_op jit(solution)/shard_map/ppermute | solution.py:562
  147.4 2.0 %collective-permute-done.17 = f32[14944]{0:T(1024)S(1)} collective-permute-done((f32[14944]{0:T(1024)S(1)}, f32[14944]{0:T(1024)S(1)}, u32[]{:S(2)}, u32[]{:S(2)}) %collective-permute-start.17) | collective-permute-done | bytes 59808 | tf_op jit(solution)/shard_map/ppermute | solution.py:562
  151.5 3.0 %collective-permute-done.18 = f32[14944]{0:T(1024)S(1)} collective-permute-done((f32[14944]{0:T(1024)S(1)}, f32[14944]{0:T(1024)S(1)}, u32[]{:S(2)}, u32[]{:S(2)}) %collective-permute-start.18) | collective-permute-done | bytes 59808 | tf_op jit(solution)/shard_map/ppermute | solution.py:562
  (372 shorter events, 51.3 us)
Async XLA Ops:
  6.1 8.8 %collective-permute-start = (bf16[3,2560]{1,0:T(4,128)(2,1)S(1)}, bf16[3,2560]{1,0:T(4,128)(2,1)S(1)}, u32[]{:S(2)}, u32[]{:S(2)}) collective-permute-start(bf16[3,2560]{1,0:T(4,128)(2,1)S(1)} %maximum_multiply_fusion), channel_id=1, source_target_pairs={{0,4},{4,8},{8,12},{1,5},{5,9},{9,13},{2,6},{6,10},{10,14},{3,7},{... | collective-permute-start | bytes 46088 | tf_op jit(solution)/shard_map/ppermute | solution.py:590
  20.3 20.9 %copy-start.3 = (bf16[256,1024]{1,0:T(8,128)(2,1)}, bf16[256,1024]{1,0:T(8,128)(2,1)S(1)}, u32[]{:S(2)}) copy-start(bf16[256,1024]{1,0:T(8,128)(2,1)S(1)} %get-tuple-element.68.xp_ref) | copy-start | bytes 1572868
  20.3 20.9 %copy-start.16 = (bf16[256,256]{1,0:T(8,128)(2,1)}, bf16[256,256]{1,0:T(8,128)(2,1)S(1)}, u32[]{:S(2)}) copy-start(bf16[256,256]{1,0:T(8,128)(2,1)S(1)} %get-tuple-element.69.bcc_ref) | copy-start | bytes 393220
  20.3 20.9 %copy-start.78 = (f32[16,256]{1,0:T(8,128)}, f32[16,256]{1,0:T(8,128)S(1)}, u32[]{:S(2)}) copy-start(f32[16,256]{1,0:T(8,128)S(1)} %get-tuple-element.70.run_ref) | copy-start | bytes 49156
  20.3 9.4 %collective-permute-start.1 = (bf16[128,1024]{1,0:T(8,128)(2,1)S(1)}, bf16[128,1024]{1,0:T(8,128)(2,1)S(1)}, u32[]{:S(2)}, u32[]{:S(2)}) collective-permute-start(bf16[128,1024]{1,0:T(8,128)(2,1)S(1)} %get-tuple-element.71), channel_id=1, source_target_pairs={{0,4},{1,5},{2,6},{3,7},{16,20},{17,21},{18,22},{19,23}} | collective-permute-start | bytes 786440 | tf_op jit(solution)/shard_map/ppermute | solution.py:553
  28.3 6.6 %collective-permute-start.4 = (bf16[128,1024]{1,0:T(8,128)(2,1)S(1)}, bf16[128,1024]{1,0:T(8,128)(2,1)S(1)}, u32[]{:S(2)}, u32[]{:S(2)}) collective-permute-start(bf16[128,1024]{1,0:T(8,128)(2,1)S(1)} %get-tuple-element.79), channel_id=1, source_target_pairs={{0,4},{1,5},{2,6},{3,7},{16,20},{17,21},{18,22},{19,23}} | collective-permute-start | bytes 786440 | tf_op jit(solution)/shard_map/ppermute | solution.py:553
  29.8 5.9 %collective-permute-start.2 = (bf16[128,1024]{1,0:T(8,128)(2,1)S(1)}, bf16[128,1024]{1,0:T(8,128)(2,1)S(1)}, u32[]{:S(2)}, u32[]{:S(2)}) collective-permute-start(bf16[128,1024]{1,0:T(8,128)(2,1)S(1)} %fusion), channel_id=1, source_target_pairs={{4,8},{5,9},{6,10},{7,11},{20,24},{21,25},{22,26},{23,27}} | collective-permute-start | bytes 786440 | tf_op jit(solution)/shard_map/ppermute | solution.py:553
  35.0 3.1 %collective-permute-start.5 = (bf16[128,1024]{1,0:T(8,128)(2,1)S(1)}, bf16[128,1024]{1,0:T(8,128)(2,1)S(1)}, u32[]{:S(2)}, u32[]{:S(2)}) collective-permute-start(bf16[128,1024]{1,0:T(8,128)(2,1)S(1)} %fusion.2), channel_id=1, source_target_pairs={{4,8},{5,9},{6,10},{7,11},{20,24},{21,25},{22,26},{23,27}} | collective-permute-start | bytes 786440 | tf_op jit(solution)/shard_map/ppermute | solution.py:553
  36.7 14.0 %collective-permute-start.3 = (bf16[128,1024]{1,0:T(8,128)(2,1)}, bf16[128,1024]{1,0:T(8,128)(2,1)}, u32[]{:S(2)}, u32[]{:S(2)}) collective-permute-start(bf16[128,1024]{1,0:T(8,128)(2,1)} %get-tuple-element.132), channel_id=1, source_target_pairs={{8,12},{9,13},{10,14},{11,15},{24,28},{25,29},{26,30},{27,31}} | collective-permute-start | bytes 786440 | tf_op jit(solution)/shard_map/ppermute | solution.py:553
  39.0 17.4 %collective-permute-start.6 = (bf16[128,1024]{1,0:T(8,128)(2,1)}, bf16[128,1024]{1,0:T(8,128)(2,1)}, u32[]{:S(2)}, u32[]{:S(2)}) collective-permute-start(bf16[128,1024]{1,0:T(8,128)(2,1)} %get-tuple-element.130), channel_id=1, source_target_pairs={{8,12},{9,13},{10,14},{11,15},{24,28},{25,29},{26,30},{27,31}} | collective-permute-start | bytes 786440 | tf_op jit(solution)/shard_map/ppermute | solution.py:553
  62.2 3.7 %collective-permute-start.7 = (f32[8,256]{1,0:T(8,128)S(1)}, f32[8,256]{1,0:T(8,128)S(1)}, u32[]{:S(2)}, u32[]{:S(2)}) collective-permute-start(f32[8,256]{1,0:T(8,128)S(1)} %add.102), channel_id=1, source_target_pairs={{0,1},{1,0},{2,3},{3,2},{4,5},{5,4},{6,7},{7,6},{8,9},{9,8},{10,11... | collective-permute-start | bytes 24584 | tf_op jit(solution)/shard_map/ppermute | solution.py:562
  66.4 4.0 %collective-permute-start.8 = (f32[8,256]{1,0:T(8,128)}, f32[8,256]{1,0:T(8,128)}, u32[]{:S(2)}, u32[]{:S(2)}) collective-permute-start(f32[8,256]{1,0:T(8,128)} %add.103), channel_id=1, source_target_pairs={{0,2},{1,3},{2,0},{3,1},{4,6},{5,7},{6,4},{7,5},{8,10},{9,11},{10,... | collective-permute-start | bytes 24584 | tf_op jit(solution)/shard_map/ppermute | solution.py:562
  77.9 19.9 %copy-start.56 = (bf16[128,1024]{1,0:T(8,128)(2,1)}, bf16[128,1024]{1,0:T(8,128)(2,1)S(1)}, u32[]{:S(2)}) copy-start(bf16[128,1024]{1,0:T(8,128)(2,1)S(1)} %get-tuple-element.94) | copy-start | bytes 786436
  77.9 19.9 %collective-permute-start.12 = (bf16[128,1024]{1,0:T(8,128)(2,1)S(1)}, bf16[128,1024]{1,0:T(8,128)(2,1)S(1)}, u32[]{:S(2)}, u32[]{:S(2)}) collective-permute-start(bf16[128,1024]{1,0:T(8,128)(2,1)S(1)} %get-tuple-element.94), channel_id=1, source_target_pairs={{12,8},{13,9},{14,10},{15,11},{28,24},{29,25},{30,26},{31,27}} | collective-permute-start | bytes 786440 | tf_op jit(solution)/shard_map/ppermute | solution.py:553
  82.0 17.6 %collective-permute-start.9 = (bf16[128,1024]{1,0:T(8,128)(2,1)S(1)}, bf16[128,1024]{1,0:T(8,128)(2,1)S(1)}, u32[]{:S(2)}, u32[]{:S(2)}) collective-permute-start(bf16[128,1024]{1,0:T(8,128)(2,1)S(1)} %get-tuple-element.85), channel_id=1, source_target_pairs={{12,8},{13,9},{14,10},{15,11},{28,24},{29,25},{30,26},{31,27}} | collective-permute-start | bytes 786440 | tf_op jit(solution)/shard_map/ppermute | solution.py:553
  98.8 2.1 %collective-permute-start.13 = (bf16[128,1024]{1,0:T(8,128)(2,1)}, bf16[128,1024]{1,0:T(8,128)(2,1)S(1)}, u32[]{:S(2)}, u32[]{:S(2)}) collective-permute-start(bf16[128,1024]{1,0:T(8,128)(2,1)} %fusion.6), channel_id=1, source_target_pairs={{8,4},{9,5},{10,6},{11,7},{24,20},{25,21},{26,22},{27,23}} | collective-permute-start | bytes 786440 | tf_op jit(solution)/shard_map/ppermute | solution.py:553
  99.8 3.7 %collective-permute-start.10 = (bf16[128,1024]{1,0:T(8,128)(2,1)S(1)}, bf16[128,1024]{1,0:T(8,128)(2,1)S(1)}, u32[]{:S(2)}, u32[]{:S(2)}) collective-permute-start(bf16[128,1024]{1,0:T(8,128)(2,1)S(1)} %fusion.4), channel_id=1, source_target_pairs={{8,4},{9,5},{10,6},{11,7},{24,20},{25,21},{26,22},{27,23}} | collective-permute-start | bytes 786440 | tf_op jit(solution)/shard_map/ppermute | solution.py:553
  102.2 19.7 %collective-permute-start.14 = (bf16[128,1024]{1,0:T(8,128)(2,1)S(1)}, bf16[128,1024]{1,0:T(8,128)(2,1)S(1)}, u32[]{:S(2)}, u32[]{:S(2)}) collective-permute-start(bf16[128,1024]{1,0:T(8,128)(2,1)S(1)} %get-tuple-element.128), channel_id=1, source_target_pairs={{4,0},{5,1},{6,2},{7,3},{20,16},{21,17},{22,18},{23,19}} | collective-permute-start | bytes 786440 | tf_op jit(solution)/shard_map/ppermute | solution.py:553
  103.5 18.4 %copy-start.73 = (f32[4,2048]{1,0:T(4,128)S(1)}, f32[4,2048]{1,0:T(4,128)}, u32[]{:S(2)}) copy-start(f32[4,2048]{1,0:T(4,128)} %wx_ref.7) | copy-start | bytes 98308
  103.8 27.5 %collective-permute-start.11 = (bf16[128,1024]{1,0:T(8,128)(2,1)S(1)}, bf16[128,1024]{1,0:T(8,128)(2,1)S(1)}, u32[]{:S(2)}, u32[]{:S(2)}) collective-permute-start(bf16[128,1024]{1,0:T(8,128)(2,1)S(1)} %get-tuple-element.126), channel_id=1, source_target_pairs={{4,0},{5,1},{6,2},{7,3},{20,16},{21,17},{22,18},{23,19}} | collective-permute-start | bytes 786440 | tf_op jit(solution)/shard_map/ppermute | solution.py:553
  141.4 5.9 %collective-permute-start.15 = (f32[3,2560]{1,0:T(4,128)S(1)}, f32[3,2560]{1,0:T(4,128)S(1)}, u32[]{:S(2)}, u32[]{:S(2)}) collective-permute-start(f32[3,2560]{1,0:T(4,128)S(1)} %pad_maximum_fusion.2), channel_id=1, source_target_pairs={{4,0},{8,4},{12,8},{5,1},{9,5},{13,9},{6,2},{10,6},{14,10},{7,3},{... | collective-permute-start | bytes 92168 | tf_op jit(solution)/shard_map/ppermute | solution.py:748
  143.0 1.3 collective-permute-start.16
  144.3 5.0 %collective-permute-start.17 = (f32[14944]{0:T(1024)S(1)}, f32[14944]{0:T(1024)S(1)}, u32[]{:S(2)}, u32[]{:S(2)}) collective-permute-start(f32[14944]{0:T(1024)S(1)} %add.114), channel_id=1, source_target_pairs={{0,4},{4,0},{8,12},{12,8},{1,5},{5,1},{9,13},{13,9},{2,6},{6,2},{1... | collective-permute-start | bytes 179336 | tf_op jit(solution)/shard_map/ppermute | solution.py:562
  149.3 5.2 %collective-permute-start.18 = (f32[14944]{0:T(1024)S(1)}, f32[14944]{0:T(1024)S(1)}, u32[]{:S(2)}, u32[]{:S(2)}) collective-permute-start(f32[14944]{0:T(1024)S(1)} %add.115), channel_id=1, source_target_pairs={{0,8},{4,12},{8,0},{12,4},{1,9},{5,13},{9,1},{13,5},{2,10},{6,14},... | collective-permute-start | bytes 179336 | tf_op jit(solution)/shard_map/ppermute | solution.py:562
  (125 other events, 1006.0 us)

commit v2 on v1

v2 whole, which is shorter than its diff:
```python
import functools

import jax
import jax.numpy as jnp
from jax import lax
from jax.experimental import pallas as pl
from jax.experimental.pallas import tpu as pltpu
from jax.sharding import PartitionSpec as P

HEAD_DIM = 64
NSTATE = 128
CONV = 4
STRETCH = 128
INNER = 8192
HALO = CONV - 1
PAD = 8
CHUNK = 256
PAIR = 2 * HEAD_DIM
NORM_EPS = 1e-05
LOWEST = -1e30
GAIN, SKIP, BACK = CONV + 1, CONV + 2, CONV + 3
PACKED = BACK + HALO
BLOCKED_LIMIT = 40 * 1024 * 1024
VMEM_LIMIT = 24 * 1024 * 1024
UNROLL = 2

f32 = jnp.float32
bf16 = jnp.bfloat16


def dot(a, b, contract=((1,), (0,))):
    return lax.dot_general(a, b, (contract, ((), ())), preferred_element_type=f32)


def dot_full(a, b):
    return lax.dot_general(
        a, b, (((1,), (0,)), ((), ())), precision=lax.Precision.HIGHEST, preferred_element_type=f32
    )


def iota(shape, dim):
    return lax.broadcasted_iota(jnp.int32, shape, dim)


def split3(value):
    high = value.astype(bf16)
    rest = value - high.astype(f32)
    middle = rest.astype(bf16)
    low = (rest - middle.astype(f32)).astype(bf16)
    return jnp.concatenate([high, middle, low], axis=0)


def spread_heads(rows, width):
    heads = rows.shape[0]
    shape = (heads, heads * width)
    pick = (iota(shape, 1) // width == iota(shape, 0)).astype(f32).astype(bf16)
    return dot(split3(rows), jnp.concatenate([pick] * 3, axis=0), ((0,), (0,)))


def head_sums(value, first, heads):
    shape = (heads, value.shape[1])
    pick = ((iota(shape, 1) + first) // HEAD_DIM == iota(shape, 0)).astype(f32).astype(bf16)
    high = value.astype(bf16)
    low = (value - high.astype(f32)).astype(bf16)
    last = ((1,), (1,))
    return dot(pick, high, last) + dot(pick, low, last)


def as_columns(row):
    return jnp.transpose(jnp.broadcast_to(row, (STRETCH, STRETCH)))


def sigmoid(value):
    return 0.5 * jnp.tanh(0.5 * value) + 0.5


def upper_ones():
    shape = (STRETCH, STRETCH)
    return (iota(shape, 0) <= iota(shape, 1)).astype(f32)


def resets_seen(flags_row):
    flags = jnp.broadcast_to(flags_row.astype(f32), (PAD, STRETCH)).astype(bf16)
    return dot(flags, upper_ones().astype(bf16))[0:1]


def decay_mask(seen):
    shape = (STRETCH, STRETCH)
    same = (as_columns(seen) == jnp.broadcast_to(seen, shape)) & (iota(shape, 0) >= iota(shape, 1))
    return jnp.where(same, 0.0, LOWEST)


def lanes(position, size):
    return pl.ds(pl.multiple_of(position * size, size), size)


def to_column(row, first, heads):
    shape = (heads, row.shape[1])
    pick = iota(shape, 1) == iota(shape, 0) + first
    return jnp.sum(jnp.where(pick, jnp.broadcast_to(row, shape), 0.0), axis=1, keepdims=True)


def over_channels(column):
    return spread_heads(jnp.broadcast_to(column, (column.shape[0], STRETCH)), HEAD_DIM)[0:1]


def softplus(value):
    small = jnp.exp(-jnp.abs(value))
    series = small * (1.0 - small * (1 / 2 - small * (1 / 3 - small * (1 / 4 - small * (1 / 5)))))
    return jnp.maximum(value, 0.0) + jnp.where(small < 0.03, series, jnp.log(1.0 + small))


def step_sizes(dtr_ref, dtb_ref, group):
    heads = dtr_ref.shape[0]
    return softplus(dtr_ref[...].astype(f32) + to_column(dtb_ref[...], group * heads, heads))


def to_end_factor(running, seen):
    final = running[:, STRETCH - 1 : STRETCH]
    return jnp.where(seen == seen[:, STRETCH - 1 : STRETCH], jnp.exp(final - running), 0.0)


def doubled(value):
    return jnp.concatenate([value, value], axis=1)


def fill_live(flags_ref, clear, live):
    rows = flags_ref.shape[1]
    clear[0:PAD, :] = jnp.ones((PAD, STRETCH), f32)
    for first in range(0, rows, STRETCH):
        flags = flags_ref[:, first : first + STRETCH].astype(f32)
        clear[PAD + first : PAD + first + STRETCH, :] = as_columns(1.0 - flags)
    for first in range(0, rows, STRETCH):
        begin = PAD + first
        product = clear[begin : begin + STRETCH, :]
        live[0, begin : begin + STRETCH, :] = product
        for lag in range(2, CONV):
            product = product * clear[begin - lag + 1 : begin - lag + 1 + STRETCH, :]
            live[lag - 1, begin : begin + STRETCH, :] = product


def fill_extended(extended, halo_ref, rows_ref):
    extended[PAD - HALO : PAD, :] = halo_ref[...]
    extended[PAD:, :] = rows_ref[...].astype(f32)


def conv_total(extended, live, weight_ref, bias_ref, first, part):
    begin = PAD + first
    total = bias_ref[0:1, part] + weight_ref[0:1, part] * extended[begin : begin + STRETCH, part]
    width = total.shape[1] // STRETCH
    for lag in range(1, CONV):
        mask = jnp.concatenate([live[lag - 1, begin : begin + STRETCH, :]] * width, axis=1)
        total = total + weight_ref[lag : lag + 1, part] * (
            extended[begin - lag : begin - lag + STRETCH, part] * mask
        )
    return total


def tail_factors(flags_ref):
    flags = flags_ref[:, flags_ref.shape[1] - STRETCH :].astype(f32)
    clear = as_columns(1.0 - flags)
    last = clear[STRETCH - 1 :]
    both = last * clear[STRETCH - 2 : STRETCH - 1]
    return jnp.concatenate([both, last, jnp.ones_like(last)], axis=0)[:, 0:1]


def tails(x_ref, bc_ref, flags_ref, out_ref):
    keep = tail_factors(flags_ref)
    inner = x_ref.shape[2]
    out_ref[:, 0:inner] = x_ref[0].astype(f32)[x_ref.shape[1] - HALO :] * keep
    groups = bc_ref.shape[3] // NSTATE
    for which in range(2):
        rows = bc_ref[0, :, which, :].astype(f32)[bc_ref.shape[1] - HALO :] * keep
        for group in range(groups):
            first = inner + (2 * group + which) * NSTATE
            out_ref[:, first : first + NSTATE] = rows[:, group * NSTATE : (group + 1) * NSTATE]


def conv_and_state(
    x_ref, xh_ref, bc_ref, bch_ref, wx_ref, bx_ref, wb_ref, bb_ref, dtr_ref, dtb_ref, alog_ref,
    flags_ref, xc_ref, xp_ref, ux_ref, bcc_ref, ubc_ref, dt_ref, run_ref, keep_ref, sdev_ref,
    sloc_ref, x_ext, bc_ext, clear, live, dt_wide, end_wide, state, *, group,
):
    rows, channels = x_ref.shape
    heads = dtr_ref.shape[0]
    fill_extended(x_ext, xh_ref, x_ref)
    fill_extended(bc_ext, bch_ref, bc_ref)
    fill_live(flags_ref, clear, live)
    blocks = rows // STRETCH
    rate = to_column(jnp.exp(alog_ref[...]), group * heads, heads)
    dt_ref[...] = step_sizes(dtr_ref, dtb_ref, group)
    product = None
    for block in range(blocks):
        first = block * STRETCH
        here = slice(first, first + STRETCH)
        every = slice(None)
        total = conv_total(bc_ext, live, wb_ref, bb_ref, first, every)
        ubc_ref[here, :] = total
        bc_now = (total * sigmoid(total)).astype(bf16)
        bcc_ref[here, :] = bc_now
        b_turned = jnp.transpose(bc_now[:, 0:NSTATE].astype(f32)).astype(bf16)
        seen = resets_seen(flags_ref[:, here])
        dt = dt_ref[:, here]
        running = dot_full(-rate * dt, upper_ones())
        run_ref[:, here] = running
        final = running[:, STRETCH - 1 : STRETCH]
        keep = jnp.where(seen[:, STRETCH - 1 : STRETCH] == 0.0, jnp.exp(final), 0.0)
        keep_row = over_channels(keep)
        keep_ref[block : block + 1, :] = keep_row
        product = keep_row if product is None else product * keep_row
        dt_wide[...] = spread_heads(dt, HEAD_DIM)
        end_wide[...] = spread_heads(to_end_factor(running, seen), HEAD_DIM)

        def chunk(step, carry):
            part = lanes(step, CHUNK)
            total = conv_total(x_ext, live, wx_ref, bx_ref, first, part)
            ux_ref[here, part] = total
            xc = (total * sigmoid(total)).astype(bf16)
            xc_ref[here, part] = xc
            stepped = (xc.astype(f32) * dt_wide[:, part]).astype(bf16)
            xp_ref[here, part] = stepped
            ended = (stepped.astype(f32) * end_wide[:, part]).astype(bf16)
            fresh = dot(b_turned, ended)
            if block > 0:
                fresh = keep_ref[block : block + 1, part] * state[:, part] + fresh
            if block < blocks - 1:
                state[:, part] = fresh
                sloc_ref[block, :, part] = fresh.astype(bf16)
            else:
                sdev_ref[:, part] = fresh.astype(bf16)
            return carry

        lax.fori_loop(0, channels // CHUNK, chunk, 0, unroll=UNROLL)
    keep_ref[blocks : blocks + 1, :] = product


def place_runs(run_ref, here, run_wide, run_tall):
    running = run_ref[:, here]
    run_wide[...] = spread_heads(running, STRETCH)
    for head in range(running.shape[0]):
        run_tall[head * PAD : (head + 1) * PAD, :] = jnp.broadcast_to(
            running[head : head + 1], (PAD, STRETCH)
        )


def block_weights(scores, mask, run_wide, run_tall, head):
    column = run_wide[:, lanes(head, STRETCH)]
    row = run_tall[pl.ds(pl.multiple_of(head * PAD, PAD), PAD), :][0:1]
    segment = jnp.exp(column - row + mask)
    return segment, (scores * segment).astype(bf16)


def both_heads(value):
    is_first = iota(value.shape, 1) < HEAD_DIM
    wide = value.astype(f32)
    zero = jnp.zeros_like(wide)
    return jnp.concatenate(
        [jnp.where(is_first, wide, zero).astype(bf16), jnp.where(is_first, zero, wide).astype(bf16)],
        axis=0,
    )


def slope_of(total):
    up = sigmoid(total)
    return up + total * up * (1.0 - up)


def within_blocks(
    xp_ref, bcc_ref, run_ref, flags_ref, ux_ref, ubc_ref, y_ref, sx_ref, sbc_ref, run_wide, run_tall
):
    rows, channels = xp_ref.shape
    for block in range(rows // STRETCH):
        here = slice(block * STRETCH, (block + 1) * STRETCH)
        mask = decay_mask(resets_seen(flags_ref[:, here]))
        scores = dot(bcc_ref[here, NSTATE:], bcc_ref[here, 0:NSTATE], ((1,), (1,)))
        place_runs(run_ref, here, run_wide, run_tall)
        sbc_ref[here, :] = slope_of(ubc_ref[here, :])

        def pair(step, carry):
            _, w_first = block_weights(scores, mask, run_wide, run_tall, 2 * step)
            _, w_second = block_weights(scores, mask, run_wide, run_tall, 2 * step + 1)
            part = lanes(step, PAIR)
            y_ref[here, part] = dot(
                jnp.concatenate([w_first, w_second], axis=1), both_heads(xp_ref[here, part])
            )
            sx_ref[here, part] = slope_of(ux_ref[here, part])
            return carry

        lax.fori_loop(0, channels // PAIR, pair, 0, unroll=UNROLL)


def start_factor(run_ref, flags_ref, here):
    seen = resets_seen(flags_ref[:, here])
    return spread_heads(jnp.where(seen == 0.0, jnp.exp(run_ref[:, here]), 0.0), HEAD_DIM)


def block_state(block, prior_ref, sloc_ref, keep_ref, part):
    state = prior_ref[0][:, part] + prior_ref[1][:, part]
    if block == 0:
        return state
    whole = keep_ref[0:1, part]
    for step in range(1, block):
        whole = whole * keep_ref[step : step + 1, part]
    return (whole * state.astype(f32) + sloc_ref[block - 1, :, part].astype(f32)).astype(bf16)


def gate_forward(
    y_ref, early_ref, last_ref, sloc_ref, keep_ref, bcc_ref, run_ref, flags_ref, xc_ref, skip_ref,
    z_ref, go_ref, gain_ref, yssd_ref, mixed_ref, sums_ref, start_wide, skip_wide, *, group,
):
    rows, channels = xc_ref.shape
    heads = run_ref.shape[0]
    prior_ref = (early_ref, last_ref)
    skip_wide[0:1, :] = over_channels(to_column(skip_ref[...], group * heads, heads))
    for block in range(rows // STRETCH):
        here = slice(block * STRETCH, (block + 1) * STRETCH)
        start_wide[...] = start_factor(run_ref, flags_ref, here)
        c_now = bcc_ref[here, NSTATE:]

        def chunk(step, carry):
            squares, products = carry
            part = lanes(step, CHUNK)
            carried = dot(c_now, block_state(block, prior_ref, sloc_ref, keep_ref, part))
            y_ssd = y_ref[here, part] + carried * start_wide[:, part]
            yssd_ref[here, part] = y_ssd
            mixed = (y_ssd + skip_wide[0:1, part] * xc_ref[here, part].astype(f32)).astype(bf16)
            mixed_ref[here, part] = mixed
            z = z_ref[here, part].astype(f32)
            gated = mixed.astype(f32) * (z * sigmoid(z))
            gained = go_ref[here, part].astype(f32) * gain_ref[0:1, part]
            return squares + gated * gated, products + gated * gained

        zero = jnp.zeros((STRETCH, CHUNK), f32)
        squares, products = lax.fori_loop(
            0, channels // CHUNK, chunk, (zero, zero), unroll=UNROLL
        )
        square_column = jnp.sum(squares, axis=1, keepdims=True)
        product_column = jnp.sum(products, axis=1, keepdims=True)
        shape = (STRETCH, STRETCH)
        mixed_up = jnp.where(
            iota(shape, 1) == 0,
            jnp.broadcast_to(square_column, shape),
            jnp.broadcast_to(product_column, shape),
        )
        sums_ref[:, here] = jnp.transpose(mixed_up)[0:PAD]


def norm_factors(totals_ref, here):
    squares = totals_ref[0:1, here]
    products = totals_ref[1:2, here]
    inv_rms = lax.rsqrt(squares * (1.0 / INNER) + NORM_EPS)
    pull = inv_rms * inv_rms * inv_rms * products * (1.0 / INNER)
    return doubled(as_columns(inv_rms)), doubled(as_columns(pull))


def gate_backward(
    totals_ref, mixed_ref, z_ref, go_ref, gain_ref, keep_ref, bcc_ref, run_ref, flags_ref,
    dy_ref, adev_ref, aloc_ref, start_wide, adjoint,
):
    rows, channels = mixed_ref.shape
    blocks = rows // STRETCH
    for block in reversed(range(blocks)):
        here = slice(block * STRETCH, (block + 1) * STRETCH)
        start_wide[...] = start_factor(run_ref, flags_ref, here)
        inv_rms, pull = norm_factors(totals_ref, here)
        c_turned = jnp.transpose(bcc_ref[here, NSTATE:].astype(f32)).astype(bf16)

        def chunk(step, carry):
            part = lanes(step, CHUNK)
            z = z_ref[here, part].astype(f32)
            gate = z * sigmoid(z)
            gained = go_ref[here, part].astype(f32) * gain_ref[0:1, part]
            d_gated = gained * inv_rms - mixed_ref[here, part].astype(f32) * gate * pull
            dy = (d_gated * gate).astype(bf16)
            dy_ref[here, part] = dy
            fresh = dot(c_turned, (dy.astype(f32) * start_wide[:, part]).astype(bf16))
            if block < blocks - 1:
                fresh = fresh + keep_ref[block : block + 1, part] * adjoint[:, part]
            if block > 0:
                adjoint[:, part] = fresh
                aloc_ref[block - 1, :, part] = fresh.astype(bf16)
            else:
                adev_ref[:, part] = fresh.astype(bf16)
            return carry

        lax.fori_loop(0, channels // CHUNK, chunk, 0, unroll=UNROLL)


def within_backward(
    totals_ref, mixed_ref, z_ref, go_ref, gain_ref, dy_ref, yssd_ref, xc_ref, xp_ref, bcc_ref,
    run_ref, flags_ref, early_ref, last_ref, sloc_ref, keep_ref,
    gz_ref, dxp_ref, dbc_ref, drun_ref, chan_ref, run_wide, run_tall, start_wide,
):
    rows, channels = mixed_ref.shape
    heads = run_ref.shape[0]
    prior_ref = (early_ref, last_ref)
    chan_ref[...] = jnp.zeros_like(chan_ref)
    for block in range(rows // STRETCH):
        here = slice(block * STRETCH, (block + 1) * STRETCH)
        mask = decay_mask(resets_seen(flags_ref[:, here]))
        b_now = bcc_ref[here, 0:NSTATE]
        c_now = bcc_ref[here, NSTATE:]
        scores = dot(c_now, b_now, ((1,), (1,)))
        place_runs(run_ref, here, run_wide, run_tall)
        start_wide[...] = start_factor(run_ref, flags_ref, here)
        inv_rms, pull = norm_factors(totals_ref, here)

        def chunk(step, carry):
            d_c, d_run = carry
            part = lanes(step, CHUNK)
            z = z_ref[here, part].astype(f32)
            gate_up = sigmoid(z)
            gate = z * gate_up
            go = go_ref[here, part].astype(f32)
            mixed = mixed_ref[here, part].astype(f32)
            gated = mixed * gate
            d_gated = go * gain_ref[0:1, part] * inv_rms - gated * pull
            slope = gate_up + gate * (1.0 - gate_up)
            gz_ref[here, part] = (d_gated * mixed * slope).astype(bf16)
            dy = dy_ref[here, part].astype(f32)
            chan_ref[0:1, part] += jnp.sum(go * gated * inv_rms, axis=0, keepdims=True)
            chan_ref[1:2, part] += jnp.sum(dy * xc_ref[here, part].astype(f32), axis=0, keepdims=True)
            d_run = d_run + head_sums(dy * yssd_ref[here, part], step * CHUNK, heads)
            started = (dy * start_wide[:, part]).astype(bf16)
            state = block_state(block, prior_ref, sloc_ref, keep_ref, part)
            return d_c + dot(started, state, ((1,), (1,))), d_run

        d_c, d_run = lax.fori_loop(
            0,
            channels // CHUNK,
            chunk,
            (jnp.zeros((STRETCH, NSTATE), f32), jnp.zeros((heads, STRETCH), f32)),
            unroll=UNROLL,
        )
        drun_ref[:, here] = d_run

        def pair(step, d_scores):
            part = lanes(step, PAIR)
            s_first, w_first = block_weights(scores, mask, run_wide, run_tall, 2 * step)
            s_second, w_second = block_weights(scores, mask, run_wide, run_tall, 2 * step + 1)
            dy = dy_ref[here, part]
            d_weights = dot(dy, both_heads(xp_ref[here, part]), ((1,), (1,)))
            dxp_ref[here, part] = dot(
                jnp.concatenate([w_first, w_second], axis=0), both_heads(dy), ((0,), (0,))
            )
            return (
                d_scores + d_weights[:, 0:STRETCH] * s_first + d_weights[:, STRETCH:] * s_second
            )

        d_scores = lax.fori_loop(
            0, channels // PAIR, pair, jnp.zeros((STRETCH, STRETCH), f32), unroll=UNROLL
        ).astype(bf16)
        dbc_ref[here, 0:NSTATE] = dot(d_scores, c_now, ((0,), (0,)))
        dbc_ref[here, NSTATE:] = d_c + dot(d_scores, b_now)


def conv_backward(d_ext, live, weight_ref, slope_ref, d_ref, x_ref, halo_ref, grad_ref, tail_ref,
                  pack_ref, rows, part):
    sums = None
    total = None
    for first in range(0, rows, STRETCH):
        here = slice(first, first + STRETCH)
        d_total = d_ref[here, part] * slope_ref[here, part]
        d_ext[PAD + first : PAD + first + STRETCH, part] = d_total
        now = jnp.sum(d_total, axis=0, keepdims=True)
        total = now if total is None else total + now
    pack_ref[CONV : CONV + 1, part] = total
    for first, count in [(-PAD, PAD)] + [(at, STRETCH) for at in range(0, rows, STRETCH)]:
        begin = PAD + first
        pieces = [d_ext[begin : begin + count, part]]
        for lag in range(1, CONV):
            moved = slice(begin + lag, begin + lag + count)
            pieces.append(d_ext[moved, part] * live[lag - 1, moved, :])
        grad = weight_ref[0:1, part] * pieces[0]
        for lag in range(1, CONV):
            grad = grad + weight_ref[lag : lag + 1, part] * pieces[lag]
        if first < 0:
            pack_ref[BACK : BACK + HALO, part] = grad[PAD - HALO :]
            seen = halo_ref[:, part]
            pieces = [piece[PAD - HALO :] for piece in pieces]
        else:
            grad_ref[first : first + count, part] = grad.astype(bf16)
            if first + count == rows:
                tail_ref[:, part] = grad[count - HALO :]
            seen = x_ref[first : first + count, part].astype(f32)
        now = [jnp.sum(seen * piece, axis=0, keepdims=True) for piece in pieces]
        sums = now if sums is None else [old + new for old, new in zip(sums, now)]
    for row, value in enumerate(sums):
        pack_ref[row : row + 1, part] = value


def finish_backward(
    later_early, later_last, aloc_ref, early_ref, last_ref, sloc_ref, keep_ref, dxp_ref, dbc_ref,
    drun_ref, xp_ref, dy_ref, skip_ref, bcc_ref, run_ref, dt_ref, flags_ref, sx_ref, sbc_ref,
    x_ref, xh_ref, bc_ref, bch_ref, wx_ref, wb_ref, alog_ref, dtb_ref, dtr_ref, chan_ref,
    gx_ref, xtail_ref, xpack_ref, gbc_ref, bctail_ref, bcpack_ref, gdt_ref,
    clear, live, dx_ext, dbc_ext, d_x, d_bc, dt_wide, end_wide, ends, skip_wide, *, group,
):
    rows, channels = xp_ref.shape
    heads = run_ref.shape[0]
    blocks = rows // STRETCH
    prior_ref = (early_ref, last_ref)
    fill_live(flags_ref, clear, live)
    live[:, PAD + rows :, :] = jnp.zeros((HALO, PAD, STRETCH), f32)
    live[:, 0:PAD, :] = jnp.zeros((HALO, PAD, STRETCH), f32)
    for ext in (dx_ext, dbc_ext):
        ext[0:PAD, :] = jnp.zeros((PAD, ext.shape[1]), f32)
        ext[PAD + rows :, :] = jnp.zeros((PAD, ext.shape[1]), f32)
    skip_wide[0:1, :] = over_channels(to_column(skip_ref[...], group * heads, heads))
    rate = to_column(jnp.exp(alog_ref[...]), group * heads, heads)
    dt_bias = to_column(dtb_ref[...], group * heads, heads)
    d_alog = jnp.zeros((heads, 1), f32)
    d_dtb = jnp.zeros((heads, 1), f32)
    for block in range(blocks):
        here = slice(block * STRETCH, (block + 1) * STRETCH)
        seen = resets_seen(flags_ref[:, here])
        running = run_ref[:, here]
        dt = dt_ref[:, here]
        dt_wide[...] = spread_heads(dt, HEAD_DIM)
        end_wide[...] = spread_heads(to_end_factor(running, seen), HEAD_DIM)
        b_now = bcc_ref[here, 0:NSTATE]

        def chunk(step, carry):
            d_b, per_step = carry
            part = lanes(step, CHUNK)
            later = later_early[:, part] + later_last[:, part]
            if block < blocks - 1:
                whole = keep_ref[block + 1 : block + 2, part]
                for place in range(block + 2, blocks):
                    whole = whole * keep_ref[place : place + 1, part]
                later = (aloc_ref[block, :, part].astype(f32) + whole * later.astype(f32)).astype(bf16)
            state = block_state(block, prior_ref, sloc_ref, keep_ref, part)
            d_keep = jnp.sum(later.astype(f32) * state.astype(f32), axis=0, keepdims=True)
            stepped = xp_ref[here, part].astype(f32)
            end = end_wide[:, part]
            d_end = dot(b_now, later) * end
            d_stepped = dxp_ref[here, part] + d_end
            ended = stepped * end
            ends[0:1, part] = (
                jnp.sum(stepped * d_end, axis=0, keepdims=True)
                + d_keep * keep_ref[block : block + 1, part]
            )
            d_x[here, part] = d_stepped * dt_wide[:, part] + skip_wide[0:1, part] * dy_ref[
                here, part
            ].astype(f32)
            return (
                d_b + dot(ended.astype(bf16), later, ((1,), (1,))),
                per_step + head_sums(stepped * d_stepped, step * CHUNK, heads),
            )

        d_b, per_step = lax.fori_loop(
            0,
            channels // CHUNK,
            chunk,
            (jnp.zeros((STRETCH, NSTATE), f32), jnp.zeros((heads, STRETCH), f32)),
            unroll=UNROLL,
        )
        d_bc[here, 0:NSTATE] = dbc_ref[here, 0:NSTATE] + d_b
        d_bc[here, NSTATE:] = dbc_ref[here, NSTATE:]
        at_end = head_sums(jnp.broadcast_to(ends[0:1, :], (STRETCH, channels)), 0, heads)
        is_last = iota((heads, STRETCH), 1) == STRETCH - 1
        d_run = drun_ref[:, here] - per_step + jnp.where(is_last, at_end, 0.0)
        shape = (STRETCH, STRETCH)
        d_log = dot_full(d_run, (iota(shape, 0) >= iota(shape, 1)).astype(f32))
        d_dt = per_step / dt - rate * d_log
        raw = dtr_ref[:, here].astype(f32) + dt_bias
        d_raw = d_dt / (1.0 + jnp.exp(-raw))
        gdt_ref[:, here] = d_raw
        d_alog = d_alog - jnp.sum(d_log * dt, axis=1, keepdims=True) * rate
        d_dtb = d_dtb + jnp.sum(d_raw, axis=1, keepdims=True)
    xpack_ref[GAIN : SKIP + 1, :] = chan_ref[0:2, :]
    bcpack_ref[GAIN : SKIP + 1, :] = jnp.zeros((2, bcpack_ref.shape[1]), f32)
    for place, column in enumerate((d_alog, d_dtb)):
        shape = (heads, STRETCH)
        pick = iota(shape, 1) == iota(shape, 0) + group * heads
        row = jnp.sum(jnp.where(pick, jnp.broadcast_to(column, shape), 0.0), axis=0, keepdims=True)
        bcpack_ref[GAIN : GAIN + 1, place * STRETCH : (place + 1) * STRETCH] = row

    def conv_chunk(step, carry):
        conv_backward(
            dx_ext, live, wx_ref, sx_ref, d_x, x_ref, xh_ref, gx_ref, xtail_ref, xpack_ref, rows,
            lanes(step, STRETCH),
        )
        return carry

    lax.fori_loop(0, channels // STRETCH, conv_chunk, 0, unroll=UNROLL)
    for step in range(2):
        conv_backward(
            dbc_ext, live, wb_ref, sbc_ref, d_bc, bc_ref, bch_ref, gbc_ref, bctail_ref, bcpack_ref,
            rows, slice(step * NSTATE, (step + 1) * NSTATE),
        )


def final_sums(mine_ref, pick_ref, flags_ref, *refs, arrivals, groups, scale):
    arrived, tails_x, tails_bc = refs[:arrivals], refs[arrivals], refs[arrivals + 1]
    out_wx, out_bx, out_wb, out_alog, out_dtb, out_skip, out_gain, ending_ref = refs[arrivals + 2 :]
    inner = tails_x.shape[1]
    total = mine_ref[0:BACK, :]
    back = jnp.zeros((HALO, total.shape[1]), f32)
    for place, ref in enumerate(arrived):
        value = ref[...].astype(f32)
        total = total + value[0:BACK]
        back = back + value[BACK:PACKED] * pick_ref[place : place + 1, 0:1]
    total = total * scale
    back = back * tail_factors(flags_ref)
    ending_ref[:, 0:inner] = (tails_x[...] + back[:, 0:inner]).astype(bf16)
    ending_ref[:, inner:] = (tails_bc[...] + back[:, inner:]).astype(bf16)
    out_wx[...] = total[0:CONV, 0:inner]
    out_bx[...] = total[CONV : CONV + 1, 0:inner]
    out_wb[...] = total[0 : CONV + 1, inner:]
    out_gain[...] = total[GAIN : GAIN + 1, 0:inner]
    heads = out_skip.shape[1]
    for out, shift in ((out_alog, 0), (out_dtb, STRETCH)):
        row = None
        for group in range(groups):
            first = inner + 2 * group * NSTATE + shift
            piece = total[GAIN : GAIN + 1, first : first + STRETCH]
            row = piece if row is None else row + piece
        out[...] = row[:, 0:heads]
    lane_sums = jnp.broadcast_to(total[SKIP : SKIP + 1, 0:inner], (PAD, inner))
    shape = (heads, inner)
    pick = (iota(shape, 1) // HEAD_DIM == iota(shape, 0)).astype(f32).astype(bf16)
    high = lane_sums.astype(bf16)
    low = (lane_sums - high.astype(f32)).astype(bf16)
    last = ((1,), (1,))
    out_skip[...] = (dot(high, pick, last) + dot(low, pick, last))[0:1]


def call(kernel, operands, outs, scratch, flops, name, blocked=False):
    cuts = [cut or {} for _, cut in operands]
    arrays = [array for array, _ in operands]
    shapes = [jax.ShapeDtypeStruct(shape, dtype) for shape, dtype in outs]

    def body(*refs):
        seen = []
        for ref, cut in zip(refs, cuts):
            if cut:
                ref = ref.at[tuple(cut.get(dim, slice(None)) for dim in range(len(ref.shape)))]
            seen.append(ref)
        kernel(*seen, *refs[len(cuts) :])

    def block_of(array, cut):
        shape, index = [], []
        for dim, extent in enumerate(array.shape):
            part = cut.get(dim, slice(0, extent))
            size = part.stop - part.start
            shape.append(size)
            index.append(part.start // size)
        return pl.BlockSpec(tuple(shape), functools.partial(lambda fixed, i: fixed, tuple(index)))

    in_vmem = pl.BlockSpec(memory_space=pltpu.VMEM)
    if blocked:
        grid, limit = {"grid": (1,)}, BLOCKED_LIMIT
        in_specs = [block_of(array, cut) for array, cut in zip(arrays, cuts)]
        out_specs = [block_of(shape, {}) for shape in shapes]
    else:
        grid, limit = {}, VMEM_LIMIT
        in_specs, out_specs = [in_vmem] * len(arrays), [in_vmem] * len(shapes)
    count = sum(each.size * each.dtype.itemsize for each in arrays + shapes)
    return pl.pallas_call(
        kernel if blocked else body,
        in_specs=in_specs,
        out_specs=out_specs,
        out_shape=shapes,
        scratch_shapes=[pltpu.VMEM(shape, f32) for shape in scratch],
        compiler_params=pltpu.CompilerParams(vmem_limit_bytes=limit),
        cost_estimate=pl.CostEstimate(flops=flops, bytes_accessed=count, transcendentals=0),
        name=name,
        **grid,
    )(*arrays)


def together(*values):
    return lax.optimization_barrier(values)


def chain(parts, decays, axis, backward, fillers):
    count = lax.axis_size(axis)
    zero = [jnp.zeros(part.shape, bf16) for part in parts]
    early, last = list(zero), list(zero)
    results = []
    for hop in range(count - 1):
        pairs = [(count - 1 - hop, count - 2 - hop)] if backward else [(hop, hop + 1)]
        leaving = list(parts)
        if hop > 0:
            for place, part in enumerate(parts):
                early[place] = early[place] + last[place] if hop > 1 else last[place]
                arrived = early[place].astype(f32)
                leaving[place] = (decays[place] * arrived + part.astype(f32)).astype(bf16)
        if hop < len(fillers):
            work, array = fillers[hop]
            array = together(array, *leaving)[0]
        last = [lax.ppermute(each, axis, pairs) for each in leaving]
        if hop < len(fillers):
            done = work(array)
            last[0], *done = together(last[0], *done)
            results.append(done)
    for work, array in fillers[len(results) :]:
        results.append(work(array))
    return list(zip(early, last)), results


def exchange_sum(value, axis):
    count = lax.axis_size(axis)
    stride = 1
    while stride < count:
        value = value + lax.ppermute(value, axis, [(i, i ^ stride) for i in range(count)])
        stride *= 2
    return value


def per_device(
    x_raw, bc_raw, z_gate, dt_raw, resets, conv_x_weight, conv_x_bias, conv_bc_weight,
    conv_bc_bias, a_log, dt_bias, skip_weight, norm_gain, grad_out,
):
    rows, inner = x_raw.shape[1:]
    groups = bc_raw.shape[3] // NSTATE
    heads = a_log.shape[0] // groups
    channels = inner // groups
    blocks = rows // STRETCH
    width = 2 * NSTATE

    def by_group(value):
        lead = value.shape[:-2]
        split = value.reshape(lead + (2, groups, NSTATE))
        return jnp.moveaxis(split, -3, -2).reshape(lead + (groups * width,))

    x_own, z_own, go_own, dt_own = x_raw[0], z_gate[0], grad_out[0], dt_raw[0]
    bc_own = by_group(bc_raw[0])
    flags = resets
    count = lax.axis_size("ctx")
    sent = call(
        tails,
        [
            (x_raw, {1: slice(rows - 16, rows)}),
            (bc_raw, {1: slice(rows - 16, rows)}),
            (flags, {1: slice(rows - STRETCH, rows)}),
        ],
        [((HALO, inner + groups * width), f32)],
        [],
        rows,
        "tails",
        True,
    )[0]
    halo = lax.ppermute(sent, "ctx", [(i, i + 1) for i in range(count - 1)])
    alog_row, dtb_row, skip_row = a_log[None], dt_bias[None], skip_weight[None]
    bx, gain = conv_x_bias[None], norm_gain[None]
    wb, bb = by_group(conv_bc_weight), by_group(conv_bc_bias)[None]

    def wide(array, group):
        return (array, {1: slice(group * channels, (group + 1) * channels)})

    def narrow(array, group, first=0):
        return (array, {1: slice(first + group * width, first + (group + 1) * width)})

    def per_head(array, group):
        return (array, {0: slice(group * heads, (group + 1) * heads)})

    def whole(array):
        return (array, None)

    keep_rows = -(-(blocks + 1) // PAD) * PAD
    tall, thin, row_shape = (rows, channels), (rows, width), (heads, rows)
    state_shape = (NSTATE, channels)
    local_shape = (blocks - 1, NSTATE, channels)
    clear_shape, live_shape = (rows + PAD, STRETCH), (HALO, rows + 2 * PAD, STRETCH)
    wide_scratch = (STRETCH, channels)
    run_scratch = [(STRETCH, heads * STRETCH), (heads * PAD, STRETCH)]
    work = rows * channels * STRETCH
    group_range = range(groups)
    held = []
    for g in group_range:
        held.append(
            call(
                functools.partial(conv_and_state, group=g),
                [
                    wide(x_own, g), wide(halo, g), narrow(bc_own, g), narrow(halo, g, inner),
                    wide(conv_x_weight, g), wide(bx, g), narrow(wb, g), narrow(bb, g),
                    per_head(dt_own, g), whole(dtb_row), whole(alog_row), whole(flags),
                ],
                [
                    (tall, bf16), (tall, bf16), (tall, f32), (thin, bf16), (thin, f32),
                    (row_shape, f32), (row_shape, f32), ((keep_rows, channels), f32),
                    (state_shape, bf16), (local_shape, bf16),
                ],
                [
                    (rows + PAD, channels), (rows + PAD, width), clear_shape, live_shape,
                    wide_scratch, wide_scratch, state_shape,
                ],
                2 * work,
                "conv_and_state",
            )
        )
    xc, xp, ux, bcc, ubc, dt, run, keep, s_dev, s_loc = zip(*held)
    decay = [k[blocks : blocks + 1] for k in keep]

    def forward_work(g):
        return lambda bcc_now: call(
            within_blocks,
            [
                whole(xp[g]), whole(bcc_now), whole(run[g]), whole(flags), whole(ux[g]), whole(ubc[g]),
            ],
            [(tall, f32), (tall, f32), (thin, f32)],
            run_scratch,
            6 * work,
            "within_blocks",
        )

    prior, held = chain(
        s_dev, decay, "ctx", False, [(forward_work(g), bcc[g]) for g in group_range]
    )
    y_within, slope_x, slope_bc = zip(*held)
    held = [
        call(
            functools.partial(gate_forward, group=g),
            [
                whole(y_within[g]), whole(prior[g][0]), whole(prior[g][1]), whole(s_loc[g]),
                whole(keep[g]), whole(bcc[g]), whole(run[g]), whole(flags), whole(xc[g]),
                whole(skip_row), wide(z_own, g), wide(go_own, g), wide(gain, g),
            ],
            [(tall, f32), (tall, bf16), ((PAD, rows), f32)],
            [wide_scratch, (PAD, channels)],
            2 * work,
            "gate_forward",
        )
        for g in group_range
    ]
    y_ssd, mixed, sums = zip(*held)
    totals = exchange_sum(sum(sums[1:], sums[0]), "head")
    held = [
        call(
            gate_backward,
            [
                whole(totals), whole(mixed[g]), wide(z_own, g), wide(go_own, g), wide(gain, g),
                whole(keep[g]), whole(bcc[g]), whole(run[g]), whole(flags),
            ],
            [(tall, bf16), (state_shape, bf16), (local_shape, bf16)],
            [wide_scratch, state_shape],
            2 * work,
            "gate_backward",
        )
        for g in group_range
    ]
    dy, a_dev, a_loc = zip(*held)

    def backward_work(g):
        return lambda bcc_now: call(
            within_backward,
            [
                whole(totals), whole(mixed[g]), wide(z_own, g), wide(go_own, g), wide(gain, g),
                whole(dy[g]), whole(y_ssd[g]), whole(xc[g]), whole(xp[g]), whole(bcc_now),
                whole(run[g]), whole(flags), whole(prior[g][0]), whole(prior[g][1]), whole(s_loc[g]),
                whole(keep[g]),
            ],
            [
                (tall, bf16), (tall, f32), (thin, f32), (row_shape, f32), ((PAD, channels), f32),
            ],
            run_scratch + [wide_scratch],
            10 * work,
            "within_backward",
            True,
        )

    later, held = chain(
        a_dev, decay, "ctx", True, [(backward_work(g), bcc[g]) for g in group_range]
    )
    gz, dxp, dbc, drun, chan = zip(*held)
    held = [
        call(
            functools.partial(finish_backward, group=g),
            [
                whole(later[g][0]), whole(later[g][1]), whole(a_loc[g]), whole(prior[g][0]),
                whole(prior[g][1]), whole(s_loc[g]), whole(keep[g]), whole(dxp[g]), whole(dbc[g]),
                whole(drun[g]), whole(xp[g]), whole(dy[g]), whole(skip_row), whole(bcc[g]),
                whole(run[g]), whole(dt[g]), whole(flags), whole(slope_x[g]), whole(slope_bc[g]),
                wide(x_own, g), wide(halo, g), narrow(bc_own, g), narrow(halo, g, inner),
                wide(conv_x_weight, g), narrow(wb, g), whole(alog_row), whole(dtb_row),
                per_head(dt_own, g), whole(chan[g]),
            ],
            [
                (tall, bf16), ((HALO, channels), f32), ((PACKED, channels), f32), (thin, bf16),
                ((HALO, width), f32), ((PACKED, width), f32), (row_shape, f32),
            ],
            [
                clear_shape, live_shape, (rows + 2 * PAD, channels), (rows + 2 * PAD, width), tall,
                thin, wide_scratch, wide_scratch, (PAD, channels), (PAD, channels),
            ],
            4 * work,
            "finish_backward",
            True,
        )
        for g in group_range
    ]
    gx, x_tail, x_pack, gbc, bc_tail, bc_pack, gdt = zip(*held)

    def joined(pieces):
        return jnp.concatenate(pieces, axis=1)

    def ungroup(value):
        lead = value.shape[:-1]
        split = value.reshape(lead + (groups, 2, NSTATE))
        return jnp.moveaxis(split, -3, -2).reshape(lead + (2, groups * NSTATE))

    packed = joined(x_pack + bc_pack)
    mine = packed
    for shift in range(1, lax.axis_size("dp")):
        size = lax.axis_size("dp")
        other = lax.ppermute(packed, "dp", [(i, (i + shift) % size) for i in range(size)])
        mine = jnp.where(jnp.arange(PACKED)[:, None] < BACK, mine + other, mine)
    leaving = mine.astype(bf16)
    here = lax.axis_index("ctx")
    arrived, picks = [], []
    for shift in range(1, count):
        arrived.append(lax.ppermute(leaving, "ctx", [(i, i ^ shift) for i in range(count)]))
        picks.append((here ^ shift) == here + 1)
    pick = jnp.broadcast_to(jnp.stack(picks).astype(f32)[:, None], (count - 1, STRETCH))
    out_wx, out_bx, out_wb, out_alog, out_dtb, out_skip, out_gain, ending = call(
        functools.partial(
            final_sums,
            arrivals=count - 1,
            groups=groups,
            scale=float(lax.axis_size("dp") * count * rows) ** (-0.5),
        ),
        [whole(mine), whole(pick), whole(flags)]
        + [whole(each) for each in arrived]
        + [whole(joined(x_tail)), whole(joined(bc_tail))],
        [
            ((CONV, inner), f32), ((1, inner), f32), ((CONV + 1, groups * width), f32),
            ((1, groups * heads), f32), ((1, groups * heads), f32), ((1, groups * heads), f32),
            ((1, inner), f32), ((HALO, inner + groups * width), bf16),
        ],
        [],
        rows * inner,
        "final_sums",
    )
    grad_x = lax.dynamic_update_slice(joined(gx), ending[:, :inner], (rows - HALO, 0))
    grad_bc = lax.dynamic_update_slice(
        ungroup(joined(gbc)), ungroup(ending[:, inner:]), (rows - HALO, 0, 0)
    )
    bc_terms = ungroup(out_wb)
    return (
        grad_x[None],
        grad_bc[None],
        joined(gz)[None],
        jnp.concatenate(gdt, axis=0)[None],
        out_wx,
        out_bx[0],
        bc_terms[:CONV],
        bc_terms[CONV],
        out_alog[0],
        out_dtb[0],
        out_skip[0],
        out_gain[0],
    )


def solution(mesh):
    return jax.shard_map(
        per_device,
        mesh=mesh,
        in_specs=(
            P("dp", "ctx", "head"),
            P("dp", "ctx", None, "head"),
            P("dp", "ctx", "head"),
            P("dp", "head", "ctx"),
            P("dp", "ctx"),
            P(None, "head"),
            P("head"),
            P(None, None, "head"),
            P(None, "head"),
            P("head"),
            P("head"),
            P("head"),
            P("head"),
            P("dp", "ctx", "head"),
        ),
        out_specs=(
            P("dp", "ctx", "head"),
            P("dp", "ctx", None, "head"),
            P("dp", "ctx", "head"),
            P("dp", "head", "ctx"),
            P(None, "head"),
            P("head"),
            P(None, None, "head"),
            P(None, "head"),
            P("head"),
            P("head"),
            P("head"),
            P("head"),
        ),
        check_vma=False,
    )
```

time: 159 us -> 118 us (0.74)
  Pallas kernels: 58.2 us -> 45.3 us
  local copies, waits for them, and re-layouts: 25.4 us -> 14.7 us
  other arithmetic: 13.3 us -> 4.74 us
  waiting for transfers between devices: 28.9 us -> 24 us
  between operations: 4.09 us -> 2.05 us
    pallas_call x12 -> x14, Pallas kernels: 58.2 us -> 45.3 us  [call(): pl.pallas_call(kernel if blocked else body, in_specs=in_specs, out_specs=...]
    convert_element_type x10, other arithmetic: 5.86 us -> 1.62 us  [the longest x8 0.94 us: chain(): leaving[place] = (decays[place] * arrived + part.astype(f32)).astype(bf16)]
    slice x12 -> x0, local copies, waits for them, and re-layouts: 4.18 us -> none  [the longest x3 1.19 us: per_device(): cut.append(flat[at:at + size])]
    ppermute x5 -> x2, waiting for transfers between devices: 8.76 us -> 4.6 us  [exchange_sum(): lax.ppermute(value, axis, [(i, i ^ stride) for i in range(count)])]
    ppermute x5 -> x2, starting transfers between devices: 6.77 us -> 3.01 us  [exchange_sum(): lax.ppermute(value, axis, [(i, i ^ stride) for i in range(count)])]
    ppermute x14 -> x17, starting transfers between devices: 21 us -> 23.7 us  [the longest x12 14.1 us: chain(): last = [lax.ppermute(each, axis, pairs) for each in leaving]]
    add x4 -> x0, other arithmetic: 2.28 us -> none  [chain(): arrived[place] = moved if hop == 0 else arrived[place] + moved]
    broadcast_in_dim x3 -> x1, local copies, waits for them, and re-layouts: 2.14 us -> 0.07 us  [per_device(): jnp.broadcast_to(jnp.stack(picks).astype(f32)[:, None], (count - 1, STRET...]
  transfers between devices with their start and end apart: 19 -> 19, of which waited for: 8 -> 8; matrix products, arithmetic and copies ran while one was open for 10% -> 4% of each run, Pallas kernels for 25% -> 26%
where the time goes in v2:
time: 118 us
  Pallas kernels  45.3 us (38%)
  starting transfers between devices  26.7 us (23%)
  waiting for transfers between devices  24 us (20%)
  local copies, waits for them, and re-layouts  14.7 us (12%)
  other arithmetic  4.74 us (4%)
  between operations  2.05 us (2%)
    pallas_call x14, Pallas kernels, call(): pl.pallas_call(kernel if blocked else body, in_specs=in_specs, out_specs=...  45.3 us
    ppermute x12, starting transfers between devices, chain(): last = [lax.ppermute(each, axis, pairs) for each in leaving]  14.1 us
    ppermute x12, waiting for transfers between devices, chain(): last = [lax.ppermute(each, axis, pairs) for each in leaving]  13.5 us
    unnamed x183, local copies, waits for them, and re-layouts  12.3 us
    ppermute x1, starting transfers between devices, per_device(): halo = lax.ppermute(sent, 'ctx', [(i, i + 1) for i in range(count - 1)])  5.07 us
    ppermute x2, waiting for transfers between devices, exchange_sum(): lax.ppermute(value, axis, [(i, i ^ stride) for i in range(count)])  4.6 us
    ppermute x3, waiting for transfers between devices, per_device(): lax.ppermute(leaving, 'ctx', [(i, i ^ shift) for i in range(count)])  4.52 us
    ppermute x3, starting transfers between devices, per_device(): lax.ppermute(leaving, 'ctx', [(i, i ^ shift) for i in range(count)])  4.45 us
  transfers between devices with their start and end apart: 19, of which 8 were waited for; matrix products, arithmetic and copies ran while one was open for 4% of the time, Pallas kernels for 26%

profile of v2, /device:TPU:0, one launch (start us, length us, event | category | flops | bytes accessed | tf_op | source)
XLA Modules:
  0.0 117.6 jit_solution(6823626229396654956)
XLA Ops:
  3.7 5.1 %collective-permute-start = (f32[3,2560]{1,0:T(4,128)S(1)}, f32[3,2560]{1,0:T(4,128)S(1)}, u32[]{:S(2)}, u32[]{:S(2)}) collective-permute-start(f32[3,2560]{1,0:T(4,128)S(1)} %tails.1), channel_id=1, source_target_pairs={{0,4},{4,8},{8,12},{1,5},{5,9},{9,13},{2,6},{6,10},{10,14},{3,7},{... | collective-permute-start | bytes 92168 | tf_op jit(solution)/shard_map/ppermute | solution.py:745
  10.5 3.4 %conv_and_state.2 = (bf16[256,1024]{1,0:T(8,128)(2,1)S(1)}, bf16[256,1024]{1,0:T(8,128)(2,1)S(1)}, f32[256,1024]{1,0:T(8,128)S(1)}, bf16[256,256]{1,0:T(8,128)(2...) custom-call(bf16[256,2048]{1,0:T(8,128)(2,1)S(1)} %bitcast.62, ...), custom_call_target="tpu_custom_call" | custom-call | flops 67108864 | bytes 4521216 | tf_op jit(solution)/shard_map/conv_and_state/pallas_call | solution.py:660
  14.6 4.2 %collective-permute-start.1 = (bf16[128,1024]{1,0:T(8,128)(2,1)S(1)}, bf16[128,1024]{1,0:T(8,128)(2,1)S(1)}, u32[]{:S(2)}, u32[]{:S(2)}) collective-permute-start(bf16[128,1024]{1,0:T(8,128)(2,1)S(1)} %get-tuple-element.106), channel_id=1, source_target_pairs={{0,4},{1,5},{2,6},{3,7},{16,20},{17,21},{18,22},{19,23}} | collective-permute-start | bytes 786440 | tf_op jit(solution)/shard_map/ppermute | solution.py:693
  18.9 3.5 %conv_and_state.3 = (bf16[256,1024]{1,0:T(8,128)(2,1)S(1)}, bf16[256,1024]{1,0:T(8,128)(2,1)S(1)}, f32[256,1024]{1,0:T(8,128)S(1)}, bf16[256,256]{1,0:T(8,128)(2...) custom-call(bf16[256,2048]{1,0:T(8,128)(2,1)S(1)} %bitcast.63, ...), custom_call_target="tpu_custom_call" | custom-call | flops 67108864 | bytes 4521216 | tf_op jit(solution)/shard_map/conv_and_state/pallas_call | solution.py:660
  23.8 2.4 %within_blocks.2 = (f32[256,1024]{1,0:T(8,128)S(1)}, f32[256,1024]{1,0:T(8,128)S(1)}, f32[256,256]{1,0:T(8,128)S(1)}) custom-call(bf16[256,1024]{1,0:T(8,128)(2,1)S(1)} %get-tuple-element.107.refs_0_.xp_ref, bf16[256,256]{1,0:T(8,128)(2,1)S(1)} %get-tuple-element.144.refs_1_.refs_5_.refs_6_.bcc_ref, ...), custom_call_target="tpu_custom_call" | custom-call | flops 201326592 | bytes 4342784 | tf_op jit(solution)/shard_map/within_blocks/pallas_call | solution.py:660
  27.0 1.8 %collective-permute-done.3 = bf16[128,1024]{1,0:T(8,128)(2,1)S(1)} collective-permute-done((bf16[128,1024]{1,0:T(8,128)(2,1)S(1)}, bf16[128,1024]{1,0:T(8,128)(2,1)S(1)}, u32[]{:S(2)}, u32[]{:S(2)}) %collective-permute-start.3) | collective-permute-done | bytes 262176 | tf_op jit(solution)/shard_map/ppermute | solution.py:693
  29.7 2.4 %within_blocks.3 = (f32[256,1024]{1,0:T(8,128)S(1)}, f32[256,1024]{1,0:T(8,128)S(1)}, f32[256,256]{1,0:T(8,128)S(1)}) custom-call(bf16[256,1024]{1,0:T(8,128)(2,1)S(1)} %get-tuple-element.120.refs_0_.xp_ref, bf16[256,256]{1,0:T(8,128)(2,1)S(1)} %get-tuple-element.153.refs_1_.refs_5_.refs_6_.bcc_ref, ...), custom_call_target="tpu_custom_call" | custom-call | flops 201326592 | bytes 4342784 | tf_op jit(solution)/shard_map/within_blocks/pallas_call | solution.py:660
  34.2 2.4 %gate_forward.2 = (f32[256,1024]{1,0:T(8,128)S(1)}, bf16[256,1024]{1,0:T(8,128)(2,1)S(1)}, f32[8,256]{1,0:T(8,128)S(1)}) custom-call(f32[256,1024]{1,0:T(8,128)S(1)} %get-tuple-element.117.refs_0_, bf16[128,1024]{1,0:T(8,128)(2,1)S(1)} %get-tuple-element.209.refs_1_.early_ref, bf16[128,1024]{1,0:T(8,128)(2,1)S(1)} %collective-permute-done.4.refs_2_.last_ref, ...), custom_call_target="tpu_custom_call" | custom-call | flops 67108864 | bytes 6227072 | tf_op jit(solution)/shard_map/gate_forward/pallas_call | solution.py:660
  37.5 2.4 %gate_forward.3 = (f32[256,1024]{1,0:T(8,128)S(1)}, bf16[256,1024]{1,0:T(8,128)(2,1)S(1)}, f32[8,256]{1,0:T(8,128)S(1)}) custom-call(f32[256,1024]{1,0:T(8,128)S(1)} %get-tuple-element.134.refs_0_, bf16[128,1024]{1,0:T(8,128)(2,1)S(1)} %get-tuple-element.207.refs_1_.early_ref, bf16[128,1024]{1,0:T(8,128)(2,1)S(1)} %collective-permute-done.6.refs_2_.last_ref, ...), custom_call_target="tpu_custom_call" | custom-call | flops 67108864 | bytes 6227072 | tf_op jit(solution)/shard_map/gate_forward/pallas_call | solution.py:660
  41.8 1.5 %collective-permute-start.7 = (f32[8,256]{1,0:T(8,128)S(1)}, f32[8,256]{1,0:T(8,128)S(1)}, u32[]{:S(2)}, u32[]{:S(2)}) collective-permute-start(f32[8,256]{1,0:T(8,128)S(1)} %add.59), channel_id=1, source_target_pairs={{0,1},{1,0},{2,3},{3,2},{4,5},{5,4},{6,7},{7,6},{8,9},{9,8},{10,11... | collective-permute-start | bytes 24584 | tf_op jit(solution)/shard_map/ppermute | solution.py:707
  43.3 2.2 %collective-permute-done.7 = f32[8,256]{1,0:T(8,128)S(1)} collective-permute-done((f32[8,256]{1,0:T(8,128)S(1)}, f32[8,256]{1,0:T(8,128)S(1)}, u32[]{:S(2)}, u32[]{:S(2)}) %collective-permute-start.7) | collective-permute-done | bytes 8224 | tf_op jit(solution)/shard_map/ppermute | solution.py:707
  46.0 1.5 %collective-permute-start.8 = (f32[8,256]{1,0:T(8,128)}, f32[8,256]{1,0:T(8,128)}, u32[]{:S(2)}, u32[]{:S(2)}) collective-permute-start(f32[8,256]{1,0:T(8,128)} %add.60), channel_id=1, source_target_pairs={{0,2},{1,3},{2,0},{3,1},{4,6},{5,7},{6,4},{7,5},{8,10},{9,11},{10,... | collective-permute-start | bytes 24584 | tf_op jit(solution)/shard_map/ppermute | solution.py:707
  47.5 2.4 %collective-permute-done.8 = f32[8,256]{1,0:T(8,128)} collective-permute-done((f32[8,256]{1,0:T(8,128)}, f32[8,256]{1,0:T(8,128)}, u32[]{:S(2)}, u32[]{:S(2)}) %collective-permute-start.8) | collective-permute-done | bytes 8224 | tf_op jit(solution)/shard_map/ppermute | solution.py:707
  55.5 2.1 %gate_backward.2 = (bf16[256,1024]{1,0:T(8,128)(2,1)S(1)}, bf16[128,1024]{1,0:T(8,128)(2,1)S(1)}, bf16[1,128,1024]{2,1,0:T(8,128)(2,1)S(1)}) custom-call(f32[8,256]{1,0:T(8,128)S(1)} %add.61.refs_0_.totals_ref, bf16[256,1024]{1,0:T(8,128)(2,1)S(1)} %copy-done.28, bf16[256,2048]{1,0:T(8,128)(2,1)S(1)} %bitcast.52, bf16[256,2048]{1,0:T(8,128)(2,1)S(1)} %bitcast.58, ...), custom_call_target="tpu_custom_call" | custom-call | flops 67108864 | bytes 3867648 | tf_op jit(solution)/shard_map/gate_backward/pallas_call | solution.py:660
  59.0 2.1 %gate_backward.3 = (bf16[256,1024]{1,0:T(8,128)(2,1)S(1)}, bf16[128,1024]{1,0:T(8,128)(2,1)S(1)}, bf16[1,128,1024]{2,1,0:T(8,128)(2,1)S(1)}) custom-call(f32[8,256]{1,0:T(8,128)S(1)} %add.61.refs_0_.totals_ref, bf16[256,1024]{1,0:T(8,128)(2,1)S(1)} %copy-done.26, bf16[256,2048]{1,0:T(8,128)(2,1)S(1)} %bitcast.53, bf16[256,2048]{1,0:T(8,128)(2,1)S(1)} %bitcast.59, ...), custom_call_target="tpu_custom_call" | custom-call | flops 67108864 | bytes 3867648 | tf_op jit(solution)/shard_map/gate_backward/pallas_call | solution.py:660
  62.2 5.4 %within_backward.2 = (bf16[256,1024]{1,0:T(8,128)(2,1)S(1)}, f32[256,1024]{1,0:T(8,128)S(1)}, f32[256,256]{1,0:T(8,128)S(1)}, f32[16,256]{1,0:T(8,128)S(1)}, f32[8,1024]{1,0:T(8,128)S(1)}) custom-call(f32[8,256]{1,0:T(8,128)S(1)} %add.61.refs_0_.totals_ref, bf16[256,1024]{1,0:T(8,128)(2,1)S(1)} %copy-done.29, bf16[256,2048]{1,0:T(8,128)(2,1)S(1)} %bitcast.54, ...), custom_call_target="tpu_custom_call" | custom-call | flops 335544320 | bytes 8111104 | tf_op jit(solution)/shard_map/within_backward/pallas_call | solution.py:660
  69.4 5.4 %within_backward.3 = (bf16[256,1024]{1,0:T(8,128)(2,1)S(1)}, f32[256,1024]{1,0:T(8,128)S(1)}, f32[256,256]{1,0:T(8,128)S(1)}, f32[16,256]{1,0:T(8,128)S(1)}, f32[8,1024]{1,0:T(8,128)S(1)}) custom-call(f32[8,256]{1,0:T(8,128)S(1)} %add.61.refs_0_.totals_ref, bf16[256,1024]{1,0:T(8,128)(2,1)S(1)} %copy-done.26, bf16[256,2048]{1,0:T(8,128)(2,1)S(1)} %bitcast.55, ...), custom_call_target="tpu_custom_call" | custom-call | flops 335544320 | bytes 8111104 | tf_op jit(solution)/shard_map/within_backward/pallas_call | solution.py:660
  76.6 1.4 %collective-permute-start.14 = (bf16[128,1024]{1,0:T(8,128)(2,1)S(1)}, bf16[128,1024]{1,0:T(8,128)(2,1)S(1)}, u32[]{:S(2)}, u32[]{:S(2)}) collective-permute-start(bf16[128,1024]{1,0:T(8,128)(2,1)S(1)} %get-tuple-element.204), channel_id=1, source_target_pairs={{4,0},{5,1},{6,2},{7,3},{20,16},{21,17},{22,18},{23,19}} | collective-permute-start | bytes 786440 | tf_op jit(solution)/shard_map/ppermute | solution.py:693
  79.1 11.6 %collective-permute-done.12.later_last = bf16[128,1024]{1,0:T(8,128)(2,1)S(1)} collective-permute-done((bf16[128,1024]{1,0:T(8,128)(2,1)S(1)}, bf16[128,1024]{1,0:T(8,128)(2,1)S(1)}, u32[]{:S(2)}, u32[]{:S(2)}) %collective-permute-start.12) | collective-permute-done | bytes 262176 | tf_op jit(solution)/shard_map/ppermute | solution.py:693
  90.8 6.4 %finish_backward.2 = (bf16[256,1024]{1,0:T(8,128)(2,1)S(1)}, f32[3,1024]{1,0:T(4,128)S(1)}, f32[10,1024]{1,0:T(8,128)S(1)}, bf16[256,256]{1,0:T(8,128)(2,1)S(1)}...) custom-call(bf16[128,1024]{1,0:T(8,128)(2,1)S(1)} %get-tuple-element.203.later_early, ...), custom_call_target="tpu_custom_call" | custom-call | flops 134217728 | bytes 7657856 | tf_op jit(solution)/shard_map/finish_backward/pallas_call | solution.py:660
  97.2 6.4 %finish_backward.3 = (bf16[256,1024]{1,0:T(8,128)(2,1)S(1)}, f32[3,1024]{1,0:T(4,128)S(1)}, f32[10,1024]{1,0:T(8,128)S(1)}, bf16[256,256]{1,0:T(8,128)(2,1)S(1)}...) custom-call(bf16[128,1024]{1,0:T(8,128)(2,1)S(1)} %get-tuple-element.205.later_early, ...), custom_call_target="tpu_custom_call" | custom-call | flops 134217728 | bytes 7657856 | tf_op jit(solution)/shard_map/finish_backward/pallas_call | solution.py:660
  106.3 3.4 %collective-permute-start.16 = (bf16[10,2560]{1,0:T(8,128)(2,1)S(1)}, bf16[10,2560]{1,0:T(8,128)(2,1)S(1)}, u32[]{:S(2)}, u32[]{:S(2)}) collective-permute-start(bf16[10,2560]{1,0:T(8,128)(2,1)S(1)} %get-tuple-element.200), channel_id=1, source_target_pairs={{0,4},{4,0},{8,12},{12,8},{1,5},{5,1},{9,13},{13,9},{2,6},{6,2},{1... | collective-permute-start | bytes 153608 | tf_op jit(solution)/shard_map/ppermute | solution.py:914
  109.7 2.7 %collective-permute-done.18.refs_5_ = bf16[10,2560]{1,0:T(8,128)(2,1)S(1)} collective-permute-done((bf16[10,2560]{1,0:T(8,128)(2,1)S(1)}, bf16[10,2560]{1,0:T(8,128)(2,1)S(1)}, u32[]{:S(2)}, u32[]{:S(2)}) %collective-permute-start.18) | collective-permute-done | bytes 51232 | tf_op jit(solution)/shard_map/ppermute | solution.py:914
  112.5 1.8 %collective-permute-done.17.refs_4_ = bf16[10,2560]{1,0:T(8,128)(2,1)S(1)} collective-permute-done((bf16[10,2560]{1,0:T(8,128)(2,1)S(1)}, bf16[10,2560]{1,0:T(8,128)(2,1)S(1)}, u32[]{:S(2)}, u32[]{:S(2)}) %collective-permute-start.17) | collective-permute-done | bytes 51232 | tf_op jit(solution)/shard_map/ppermute | solution.py:914
  (246 shorter events, 31.4 us)
Async XLA Ops:
  3.7 6.7 %collective-permute-start = (f32[3,2560]{1,0:T(4,128)S(1)}, f32[3,2560]{1,0:T(4,128)S(1)}, u32[]{:S(2)}, u32[]{:S(2)}) collective-permute-start(f32[3,2560]{1,0:T(4,128)S(1)} %tails.1), channel_id=1, source_target_pairs={{0,4},{4,8},{8,12},{1,5},{5,9},{9,13},{2,6},{6,10},{10,14},{3,7},{... | collective-permute-start | bytes 92168 | tf_op jit(solution)/shard_map/ppermute | solution.py:745
  14.6 19.5 %copy-start.12 = (bf16[256,256]{1,0:T(8,128)(2,1)}, bf16[256,256]{1,0:T(8,128)(2,1)S(1)}, u32[]{:S(2)}) copy-start(bf16[256,256]{1,0:T(8,128)(2,1)S(1)} %get-tuple-element.144.refs_1_.refs_5_.refs_6_.bcc_ref) | copy-start | bytes 393220
  14.6 19.5 %copy-start.19 = (bf16[1,128,1024]{2,1,0:T(8,128)(2,1)}, bf16[1,128,1024]{2,1,0:T(8,128)(2,1)S(1)}, u32[]{:S(2)}) copy-start(bf16[1,128,1024]{2,1,0:T(8,128)(2,1)S(1)} %get-tuple-element.131.refs_3_.sloc_ref) | copy-start | bytes 786436
  14.6 19.5 %copy-start.32 = (bf16[256,1024]{1,0:T(8,128)(2,1)}, bf16[256,1024]{1,0:T(8,128)(2,1)S(1)}, u32[]{:S(2)}) copy-start(bf16[256,1024]{1,0:T(8,128)(2,1)S(1)} %get-tuple-element.132.refs_8_.xc_ref) | copy-start | bytes 1572868
  14.6 19.5 %copy-start.46 = (f32[8,1024]{1,0:T(8,128)}, f32[8,1024]{1,0:T(8,128)S(1)}, u32[]{:S(2)}) copy-start(f32[8,1024]{1,0:T(8,128)S(1)} %get-tuple-element.119.refs_4_.refs_5_.keep_ref) | copy-start | bytes 98308
  14.6 19.5 %copy-start.51 = (f32[16,256]{1,0:T(8,128)}, f32[16,256]{1,0:T(8,128)S(1)}, u32[]{:S(2)}) copy-start(f32[16,256]{1,0:T(8,128)S(1)} %get-tuple-element.111.refs_2_.refs_6_.refs_7_.run_ref) | copy-start | bytes 49156
  14.6 11.6 %collective-permute-start.1 = (bf16[128,1024]{1,0:T(8,128)(2,1)S(1)}, bf16[128,1024]{1,0:T(8,128)(2,1)S(1)}, u32[]{:S(2)}, u32[]{:S(2)}) collective-permute-start(bf16[128,1024]{1,0:T(8,128)(2,1)S(1)} %get-tuple-element.106), channel_id=1, source_target_pairs={{0,4},{1,5},{2,6},{3,7},{16,20},{17,21},{18,22},{19,23}} | collective-permute-start | bytes 786440 | tf_op jit(solution)/shard_map/ppermute | solution.py:693
  22.4 6.4 %collective-permute-start.3 = (bf16[128,1024]{1,0:T(8,128)(2,1)S(1)}, bf16[128,1024]{1,0:T(8,128)(2,1)S(1)}, u32[]{:S(2)}, u32[]{:S(2)}) collective-permute-start(bf16[128,1024]{1,0:T(8,128)(2,1)S(1)} %get-tuple-element.109), channel_id=1, source_target_pairs={{0,4},{1,5},{2,6},{3,7},{16,20},{17,21},{18,22},{19,23}} | collective-permute-start | bytes 786440 | tf_op jit(solution)/shard_map/ppermute | solution.py:693
  26.3 5.8 %collective-permute-start.2 = (bf16[128,1024]{1,0:T(8,128)(2,1)S(1)}, bf16[128,1024]{1,0:T(8,128)(2,1)S(1)}, u32[]{:S(2)}, u32[]{:S(2)}) collective-permute-start(bf16[128,1024]{1,0:T(8,128)(2,1)S(1)} %fusion), channel_id=1, source_target_pairs={{4,8},{5,9},{6,10},{7,11},{20,24},{21,25},{22,26},{23,27}} | collective-permute-start | bytes 786440 | tf_op jit(solution)/shard_map/ppermute | solution.py:693
  29.0 4.2 %collective-permute-start.5 = (bf16[128,1024]{1,0:T(8,128)(2,1)S(1)}, bf16[128,1024]{1,0:T(8,128)(2,1)S(1)}, u32[]{:S(2)}, u32[]{:S(2)}) collective-permute-start(bf16[128,1024]{1,0:T(8,128)(2,1)S(1)} %fusion.2), channel_id=1, source_target_pairs={{4,8},{5,9},{6,10},{7,11},{20,24},{21,25},{22,26},{23,27}} | collective-permute-start | bytes 786440 | tf_op jit(solution)/shard_map/ppermute | solution.py:693
  32.4 1.7 %collective-permute-start.4 = (bf16[128,1024]{1,0:T(8,128)(2,1)S(1)}, bf16[128,1024]{1,0:T(8,128)(2,1)S(1)}, u32[]{:S(2)}, u32[]{:S(2)}) collective-permute-start(bf16[128,1024]{1,0:T(8,128)(2,1)S(1)} %get-tuple-element.208), channel_id=1, source_target_pairs={{8,12},{9,13},{10,14},{11,15},{24,28},{25,29},{26,30},{27,31}} | collective-permute-start | bytes 786440 | tf_op jit(solution)/shard_map/ppermute | solution.py:693
  33.4 4.1 %collective-permute-start.6 = (bf16[128,1024]{1,0:T(8,128)(2,1)S(1)}, bf16[128,1024]{1,0:T(8,128)(2,1)S(1)}, u32[]{:S(2)}, u32[]{:S(2)}) collective-permute-start(bf16[128,1024]{1,0:T(8,128)(2,1)S(1)} %get-tuple-element.206), channel_id=1, source_target_pairs={{8,12},{9,13},{10,14},{11,15},{24,28},{25,29},{26,30},{27,31}} | collective-permute-start | bytes 786440 | tf_op jit(solution)/shard_map/ppermute | solution.py:693
  41.8 3.7 %collective-permute-start.7 = (f32[8,256]{1,0:T(8,128)S(1)}, f32[8,256]{1,0:T(8,128)S(1)}, u32[]{:S(2)}, u32[]{:S(2)}) collective-permute-start(f32[8,256]{1,0:T(8,128)S(1)} %add.59), channel_id=1, source_target_pairs={{0,1},{1,0},{2,3},{3,2},{4,5},{5,4},{6,7},{7,6},{8,9},{9,8},{10,11... | collective-permute-start | bytes 24584 | tf_op jit(solution)/shard_map/ppermute | solution.py:707
  46.0 4.0 %collective-permute-start.8 = (f32[8,256]{1,0:T(8,128)}, f32[8,256]{1,0:T(8,128)}, u32[]{:S(2)}, u32[]{:S(2)}) collective-permute-start(f32[8,256]{1,0:T(8,128)} %add.60), channel_id=1, source_target_pairs={{0,2},{1,3},{2,0},{3,1},{4,6},{5,7},{6,4},{7,5},{8,10},{9,11},{10,... | collective-permute-start | bytes 24584 | tf_op jit(solution)/shard_map/ppermute | solution.py:707
  57.6 10.0 %collective-permute-start.9 = (bf16[128,1024]{1,0:T(8,128)(2,1)S(1)}, bf16[128,1024]{1,0:T(8,128)(2,1)S(1)}, u32[]{:S(2)}, u32[]{:S(2)}) collective-permute-start(bf16[128,1024]{1,0:T(8,128)(2,1)S(1)} %get-tuple-element.139), channel_id=1, source_target_pairs={{12,8},{13,9},{14,10},{15,11},{28,24},{29,25},{30,26},{31,27}} | collective-permute-start | bytes 786440 | tf_op jit(solution)/shard_map/ppermute | solution.py:693
  61.2 7.4 %collective-permute-start.11 = (bf16[128,1024]{1,0:T(8,128)(2,1)S(1)}, bf16[128,1024]{1,0:T(8,128)(2,1)S(1)}, u32[]{:S(2)}, u32[]{:S(2)}) collective-permute-start(bf16[128,1024]{1,0:T(8,128)(2,1)S(1)} %get-tuple-element.143), channel_id=1, source_target_pairs={{12,8},{13,9},{14,10},{15,11},{28,24},{29,25},{30,26},{31,27}} | collective-permute-start | bytes 786440 | tf_op jit(solution)/shard_map/ppermute | solution.py:693
  67.8 7.1 %collective-permute-start.10 = (bf16[128,1024]{1,0:T(8,128)(2,1)S(1)}, bf16[128,1024]{1,0:T(8,128)(2,1)S(1)}, u32[]{:S(2)}, u32[]{:S(2)}) collective-permute-start(bf16[128,1024]{1,0:T(8,128)(2,1)S(1)} %fusion.4), channel_id=1, source_target_pairs={{8,4},{9,5},{10,6},{11,7},{24,20},{25,21},{26,22},{27,23}} | collective-permute-start | bytes 786440 | tf_op jit(solution)/shard_map/ppermute | solution.py:693
  68.7 7.6 %collective-permute-start.13 = (bf16[128,1024]{1,0:T(8,128)(2,1)S(1)}, bf16[128,1024]{1,0:T(8,128)(2,1)S(1)}, u32[]{:S(2)}, u32[]{:S(2)}) collective-permute-start(bf16[128,1024]{1,0:T(8,128)(2,1)S(1)} %fusion.6), channel_id=1, source_target_pairs={{8,4},{9,5},{10,6},{11,7},{24,20},{25,21},{26,22},{27,23}} | collective-permute-start | bytes 786440 | tf_op jit(solution)/shard_map/ppermute | solution.py:693
  75.0 15.7 %collective-permute-start.12 = (bf16[128,1024]{1,0:T(8,128)(2,1)S(1)}, bf16[128,1024]{1,0:T(8,128)(2,1)S(1)}, u32[]{:S(2)}, u32[]{:S(2)}) collective-permute-start(bf16[128,1024]{1,0:T(8,128)(2,1)S(1)} %get-tuple-element.202), channel_id=1, source_target_pairs={{4,0},{5,1},{6,2},{7,3},{20,16},{21,17},{22,18},{23,19}} | collective-permute-start | bytes 786440 | tf_op jit(solution)/shard_map/ppermute | solution.py:693
  76.6 20.6 %collective-permute-start.14 = (bf16[128,1024]{1,0:T(8,128)(2,1)S(1)}, bf16[128,1024]{1,0:T(8,128)(2,1)S(1)}, u32[]{:S(2)}, u32[]{:S(2)}) collective-permute-start(bf16[128,1024]{1,0:T(8,128)(2,1)S(1)} %get-tuple-element.204), channel_id=1, source_target_pairs={{4,0},{5,1},{6,2},{7,3},{20,16},{21,17},{22,18},{23,19}} | collective-permute-start | bytes 786440 | tf_op jit(solution)/shard_map/ppermute | solution.py:693
  103.7 1.5 %collective-permute-start.15 = (f32[10,2560]{1,0:T(8,128)S(1)}, f32[10,2560]{1,0:T(8,128)S(1)}, u32[]{:S(2)}, u32[]{:S(2)}) collective-permute-start(f32[10,2560]{1,0:T(8,128)S(1)} %constant_dynamic-update-slice_fusion), channel_id=1, source_target_pairs={{0,16},{16,0},{1,17},{17,1},{2,18},{18,2},{3,19},{19,3},{4,20},{20... | collective-permute-start | bytes 307208 | tf_op jit(solution)/shard_map/ppermute | solution.py:908
  105.2 7.3 %collective-permute-start.18 = (bf16[10,2560]{1,0:T(8,128)(2,1)S(1)}, bf16[10,2560]{1,0:T(8,128)(2,1)S(1)}, u32[]{:S(2)}, u32[]{:S(2)}) collective-permute-start(bf16[10,2560]{1,0:T(8,128)(2,1)S(1)} %get-tuple-element.200), channel_id=1, source_target_pairs={{0,12},{4,8},{8,4},{12,0},{1,13},{5,9},{9,5},{13,1},{2,14},{6,10},... | collective-permute-start | bytes 153608 | tf_op jit(solution)/shard_map/ppermute | solution.py:914
  105.3 9.0 %collective-permute-start.17 = (bf16[10,2560]{1,0:T(8,128)(2,1)S(1)}, bf16[10,2560]{1,0:T(8,128)(2,1)S(1)}, u32[]{:S(2)}, u32[]{:S(2)}) collective-permute-start(bf16[10,2560]{1,0:T(8,128)(2,1)S(1)} %get-tuple-element.200), channel_id=1, source_target_pairs={{0,8},{4,12},{8,0},{12,4},{1,9},{5,13},{9,1},{13,5},{2,10},{6,14},... | collective-permute-start | bytes 153608 | tf_op jit(solution)/shard_map/ppermute | solution.py:914
  106.3 8.0 %collective-permute-start.16 = (bf16[10,2560]{1,0:T(8,128)(2,1)S(1)}, bf16[10,2560]{1,0:T(8,128)(2,1)S(1)}, u32[]{:S(2)}, u32[]{:S(2)}) collective-permute-start(bf16[10,2560]{1,0:T(8,128)(2,1)S(1)} %get-tuple-element.200), channel_id=1, source_target_pairs={{0,4},{4,0},{8,12},{12,8},{1,5},{5,1},{9,13},{13,9},{2,6},{6,2},{1... | collective-permute-start | bytes 153608 | tf_op jit(solution)/shard_map/ppermute | solution.py:914
  (85 other events, 488.0 us)

commit v3 on v2

--- a/solution.py
+++ b/solution.py
@@ -20,6 +20,9 @@
 LOWEST = -1e30
 GAIN, SKIP, BACK = CONV + 1, CONV + 2, CONV + 3
 PACKED = BACK + HALO
+A_LOG, DT_BIAS, SKIP_WEIGHT = range(3)
+STAGES = 2
+STREAM_LIMIT = 62 * 1024 * 1024
 BLOCKED_LIMIT = 40 * 1024 * 1024
 VMEM_LIMIT = 24 * 1024 * 1024
 UNROLL = 2
@@ -110,9 +113,13 @@
     return jnp.maximum(value, 0.0) + jnp.where(small < 0.03, series, jnp.log(1.0 + small))
 
 
-def step_sizes(dtr_ref, dtb_ref, group):
+def head_column(rows_ref, which, group, heads):
+    return to_column(rows_ref[which : which + 1, :], group * heads, heads)
+
+
+def step_sizes(dtr_ref, rows_ref, group):
     heads = dtr_ref.shape[0]
-    return softplus(dtr_ref[...].astype(f32) + to_column(dtb_ref[...], group * heads, heads))
+    return softplus(dtr_ref[...].astype(f32) + head_column(rows_ref, DT_BIAS, group, heads))
 
 
 def to_end_factor(running, seen):
@@ -164,7 +171,8 @@
     return jnp.concatenate([both, last, jnp.ones_like(last)], axis=0)[:, 0:1]
 
 
-def tails(x_ref, bc_ref, flags_ref, out_ref):
+def tails(x_ref, bc_ref, flags_ref, out_ref, *, ready):
+    ready(0)
     keep = tail_factors(flags_ref)
     inner = x_ref.shape[2]
     out_ref[:, 0:inner] = x_ref[0].astype(f32)[x_ref.shape[1] - HALO :] * keep
@@ -177,7 +185,7 @@
 
 
 def conv_and_state(
-    x_ref, xh_ref, bc_ref, bch_ref, wx_ref, bx_ref, wb_ref, bb_ref, dtr_ref, dtb_ref, alog_ref,
+    x_ref, xh_ref, bc_ref, bch_ref, wx_ref, bx_ref, wb_ref, bb_ref, dtr_ref, rows_ref,
     flags_ref, xc_ref, xp_ref, ux_ref, bcc_ref, ubc_ref, dt_ref, run_ref, keep_ref, sdev_ref,
     sloc_ref, x_ext, bc_ext, clear, live, dt_wide, end_wide, state, *, group,
 ):
@@ -187,8 +195,8 @@
     fill_extended(bc_ext, bch_ref, bc_ref)
     fill_live(flags_ref, clear, live)
     blocks = rows // STRETCH
-    rate = to_column(jnp.exp(alog_ref[...]), group * heads, heads)
-    dt_ref[...] = step_sizes(dtr_ref, dtb_ref, group)
+    rate = jnp.exp(head_column(rows_ref, A_LOG, group, heads))
+    dt_ref[...] = step_sizes(dtr_ref, rows_ref, group)
     product = None
     for block in range(blocks):
         first = block * STRETCH
@@ -291,7 +299,7 @@
 
 def start_factor(run_ref, flags_ref, here):
     seen = resets_seen(flags_ref[:, here])
-    return spread_heads(jnp.where(seen == 0.0, jnp.exp(run_ref[:, here]), 0.0), HEAD_DIM)
+    return jnp.where(seen == 0.0, jnp.exp(run_ref[:, here]), 0.0)
 
 
 def block_state(block, prior_ref, sloc_ref, keep_ref, part):
@@ -304,29 +312,48 @@
     return (whole * state.astype(f32) + sloc_ref[block - 1, :, part].astype(f32)).astype(bf16)
 
 
+def bundle_rows(rows):
+    places = [rows]
+    for size in (PAD, PAD, 2 * PAD, NSTATE // 4):
+        places.append(places[-1] + size)
+    return places
+
+
 def gate_forward(
-    y_ref, early_ref, last_ref, sloc_ref, keep_ref, bcc_ref, run_ref, flags_ref, xc_ref, skip_ref,
-    z_ref, go_ref, gain_ref, yssd_ref, mixed_ref, sums_ref, start_wide, skip_wide, *, group,
+    y_ref, early_ref, last_ref, sloc_ref, keep_ref, bcc_ref, run_ref, flags_ref, xc_ref, rows_ref,
+    z_ref, go_ref, gain_ref, *refs, group,
 ):
+    *before, bundle_ref, sums_ref, start_wide, skip_wide = refs
     rows, channels = xc_ref.shape
     heads = run_ref.shape[0]
     prior_ref = (early_ref, last_ref)
-    skip_wide[0:1, :] = over_channels(to_column(skip_ref[...], group * heads, heads))
+    at_keep, at_gain, at_start, at_turned, _ = bundle_rows(rows)
+    bundle_ref[at_keep:at_gain, :] = keep_ref[0:PAD, :]
+    bundle_ref[at_gain:at_start, :] = jnp.broadcast_to(gain_ref[...], (PAD, channels))
+    skip_wide[0:1, :] = over_channels(head_column(rows_ref, SKIP_WEIGHT, group, heads))
+    quarter = NSTATE // 4
     for block in range(rows // STRETCH):
         here = slice(block * STRETCH, (block + 1) * STRETCH)
-        start_wide[...] = start_factor(run_ref, flags_ref, here)
+        start = start_factor(run_ref, flags_ref, here)
+        bundle_ref[at_start : at_start + heads, here] = start
+        start_wide[...] = spread_heads(start, HEAD_DIM)
         c_now = bcc_ref[here, NSTATE:]
+        turned = jnp.transpose(c_now.astype(f32))
+        for turn in range(4):
+            first = turn * rows + block * STRETCH
+            bundle_ref[at_turned : at_turned + quarter, first : first + STRETCH] = turned[
+                turn * quarter : (turn + 1) * quarter
+            ]
 
         def chunk(step, carry):
             squares, products = carry
             part = lanes(step, CHUNK)
             carried = dot(c_now, block_state(block, prior_ref, sloc_ref, keep_ref, part))
-            y_ssd = y_ref[here, part] + carried * start_wide[:, part]
-            yssd_ref[here, part] = y_ssd
-            mixed = (y_ssd + skip_wide[0:1, part] * xc_ref[here, part].astype(f32)).astype(bf16)
-            mixed_ref[here, part] = mixed
+            y_now = y_ref[here, part] + carried * start_wide[:, part]
+            y_now = y_now + skip_wide[0:1, part] * xc_ref[here, part].astype(f32)
+            bundle_ref[here, part] = y_now
             z = z_ref[here, part].astype(f32)
-            gated = mixed.astype(f32) * (z * sigmoid(z))
+            gated = y_now.astype(bf16).astype(f32) * (z * sigmoid(z))
             gained = go_ref[here, part].astype(f32) * gain_ref[0:1, part]
             return squares + gated * gated, products + gated * gained
 
@@ -337,12 +364,15 @@
         square_column = jnp.sum(squares, axis=1, keepdims=True)
         product_column = jnp.sum(products, axis=1, keepdims=True)
         shape = (STRETCH, STRETCH)
-        mixed_up = jnp.where(
+        both = jnp.where(
             iota(shape, 1) == 0,
             jnp.broadcast_to(square_column, shape),
             jnp.broadcast_to(product_column, shape),
         )
-        sums_ref[:, here] = jnp.transpose(mixed_up)[0:PAD]
+        total = jnp.transpose(both)[0:2]
+        for ref in before:
+            total = total + ref[:, here]
+        sums_ref[:, here] = total
 
 
 def norm_factors(totals_ref, here):
@@ -354,28 +384,35 @@
 
 
 def gate_backward(
-    totals_ref, mixed_ref, z_ref, go_ref, gain_ref, keep_ref, bcc_ref, run_ref, flags_ref,
-    dy_ref, adev_ref, aloc_ref, start_wide, adjoint,
+    own_ref, other_ref, bundle_ref, z_ref, go_ref, dy_ref, adev_ref, aloc_ref, totals_ref,
+    start_wide, adjoint, *, heads,
 ):
-    rows, channels = mixed_ref.shape
+    rows, channels = z_ref.shape
     blocks = rows // STRETCH
+    at_keep, at_gain, at_start, at_turned, end = bundle_rows(rows)
+    totals_ref[...] = own_ref[...] + other_ref[...]
     for block in reversed(range(blocks)):
         here = slice(block * STRETCH, (block + 1) * STRETCH)
-        start_wide[...] = start_factor(run_ref, flags_ref, here)
+        start_wide[...] = spread_heads(bundle_ref[at_start : at_start + heads, here], HEAD_DIM)
         inv_rms, pull = norm_factors(totals_ref, here)
-        c_turned = jnp.transpose(bcc_ref[here, NSTATE:].astype(f32)).astype(bf16)
+        firsts = [turn * rows + block * STRETCH for turn in range(4)]
+        c_turned = jnp.concatenate(
+            [bundle_ref[at_turned:end, first : first + STRETCH] for first in firsts], axis=0
+        ).astype(bf16)
 
         def chunk(step, carry):
             part = lanes(step, CHUNK)
             z = z_ref[here, part].astype(f32)
             gate = z * sigmoid(z)
-            gained = go_ref[here, part].astype(f32) * gain_ref[0:1, part]
-            d_gated = gained * inv_rms - mixed_ref[here, part].astype(f32) * gate * pull
+            gained = go_ref[here, part].astype(f32) * bundle_ref[at_gain : at_gain + 1, part]
+            mixed = bundle_ref[here, part].astype(bf16).astype(f32)
+            d_gated = gained * inv_rms - mixed * gate * pull
             dy = (d_gated * gate).astype(bf16)
             dy_ref[here, part] = dy
             fresh = dot(c_turned, (dy.astype(f32) * start_wide[:, part]).astype(bf16))
             if block < blocks - 1:
-                fresh = fresh + keep_ref[block : block + 1, part] * adjoint[:, part]
+                keep = bundle_ref[at_keep + block : at_keep + block + 1, part]
+                fresh = fresh + keep * adjoint[:, part]
             if block > 0:
                 adjoint[:, part] = fresh
                 aloc_ref[block - 1, :, part] = fresh.astype(bf16)
@@ -387,13 +424,15 @@
 
 
 def within_backward(
-    totals_ref, mixed_ref, z_ref, go_ref, gain_ref, dy_ref, yssd_ref, xc_ref, xp_ref, bcc_ref,
-    run_ref, flags_ref, early_ref, last_ref, sloc_ref, keep_ref,
-    gz_ref, dxp_ref, dbc_ref, drun_ref, chan_ref, run_wide, run_tall, start_wide,
+    totals_ref, bundle_ref, z_ref, go_ref, dy_ref, xc_ref, xp_ref, bcc_ref,
+    run_ref, flags_ref, early_ref, last_ref, sloc_ref, keep_ref, rows_ref,
+    gz_ref, dxp_ref, dbc_ref, drun_ref, chan_ref, run_wide, run_tall, start_wide, skip_wide, *, group,
 ):
-    rows, channels = mixed_ref.shape
+    rows, channels = xc_ref.shape
     heads = run_ref.shape[0]
     prior_ref = (early_ref, last_ref)
+    at_gain = bundle_rows(rows)[1]
+    skip_wide[0:1, :] = over_channels(head_column(rows_ref, SKIP_WEIGHT, group, heads))
     chan_ref[...] = jnp.zeros_like(chan_ref)
     for block in range(rows // STRETCH):
         here = slice(block * STRETCH, (block + 1) * STRETCH)
@@ -402,7 +441,7 @@
         c_now = bcc_ref[here, NSTATE:]
         scores = dot(c_now, b_now, ((1,), (1,)))
         place_runs(run_ref, here, run_wide, run_tall)
-        start_wide[...] = start_factor(run_ref, flags_ref, here)
+        start_wide[...] = spread_heads(start_factor(run_ref, flags_ref, here), HEAD_DIM)
         inv_rms, pull = norm_factors(totals_ref, here)
 
         def chunk(step, carry):
@@ -412,15 +451,18 @@
             gate_up = sigmoid(z)
             gate = z * gate_up
             go = go_ref[here, part].astype(f32)
-            mixed = mixed_ref[here, part].astype(f32)
+            xc = xc_ref[here, part].astype(f32)
+            y_now = bundle_ref[here, part]
+            y_ssd = y_now - skip_wide[0:1, part] * xc
+            mixed = y_now.astype(bf16).astype(f32)
             gated = mixed * gate
-            d_gated = go * gain_ref[0:1, part] * inv_rms - gated * pull
+            d_gated = go * bundle_ref[at_gain : at_gain + 1, part] * inv_rms - gated * pull
             slope = gate_up + gate * (1.0 - gate_up)
             gz_ref[here, part] = (d_gated * mixed * slope).astype(bf16)
             dy = dy_ref[here, part].astype(f32)
             chan_ref[0:1, part] += jnp.sum(go * gated * inv_rms, axis=0, keepdims=True)
-            chan_ref[1:2, part] += jnp.sum(dy * xc_ref[here, part].astype(f32), axis=0, keepdims=True)
-            d_run = d_run + head_sums(dy * yssd_ref[here, part], step * CHUNK, heads)
+            chan_ref[1:2, part] += jnp.sum(dy * xc, axis=0, keepdims=True)
+            d_run = d_run + head_sums(dy * y_ssd, step * CHUNK, heads)
             started = (dy * start_wide[:, part]).astype(bf16)
             state = block_state(block, prior_ref, sloc_ref, keep_ref, part)
             return d_c + dot(started, state, ((1,), (1,))), d_run
@@ -491,8 +533,8 @@
 
 def finish_backward(
     later_early, later_last, aloc_ref, early_ref, last_ref, sloc_ref, keep_ref, dxp_ref, dbc_ref,
-    drun_ref, xp_ref, dy_ref, skip_ref, bcc_ref, run_ref, dt_ref, flags_ref, sx_ref, sbc_ref,
-    x_ref, xh_ref, bc_ref, bch_ref, wx_ref, wb_ref, alog_ref, dtb_ref, dtr_ref, chan_ref,
+    drun_ref, xp_ref, dy_ref, bcc_ref, run_ref, dt_ref, flags_ref, sx_ref, sbc_ref,
+    x_ref, xh_ref, bc_ref, bch_ref, wx_ref, wb_ref, rows_ref, dtr_ref, chan_ref,
     gx_ref, xtail_ref, xpack_ref, gbc_ref, bctail_ref, bcpack_ref, gdt_ref,
     clear, live, dx_ext, dbc_ext, d_x, d_bc, dt_wide, end_wide, ends, skip_wide, *, group,
 ):
@@ -506,9 +548,9 @@
     for ext in (dx_ext, dbc_ext):
         ext[0:PAD, :] = jnp.zeros((PAD, ext.shape[1]), f32)
         ext[PAD + rows :, :] = jnp.zeros((PAD, ext.shape[1]), f32)
-    skip_wide[0:1, :] = over_channels(to_column(skip_ref[...], group * heads, heads))
-    rate = to_column(jnp.exp(alog_ref[...]), group * heads, heads)
-    dt_bias = to_column(dtb_ref[...], group * heads, heads)
+    skip_wide[0:1, :] = over_channels(head_column(rows_ref, SKIP_WEIGHT, group, heads))
+    rate = jnp.exp(head_column(rows_ref, A_LOG, group, heads))
+    dt_bias = head_column(rows_ref, DT_BIAS, group, heads)
     d_alog = jnp.zeros((heads, 1), f32)
     d_dtb = jnp.zeros((heads, 1), f32)
     for block in range(blocks):
@@ -593,7 +635,9 @@
 
 def final_sums(mine_ref, pick_ref, flags_ref, *refs, arrivals, groups, scale):
     arrived, tails_x, tails_bc = refs[:arrivals], refs[arrivals], refs[arrivals + 1]
-    out_wx, out_bx, out_wb, out_alog, out_dtb, out_skip, out_gain, ending_ref = refs[arrivals + 2 :]
+    out_wx, out_bx, out_wb, out_bb, out_alog, out_dtb, out_skip, out_gain, ending_ref = refs[
+        arrivals + 2 :
+    ]
     inner = tails_x.shape[1]
     total = mine_ref[0:BACK, :]
     back = jnp.zeros((HALO, total.shape[1]), f32)
@@ -607,7 +651,12 @@
     ending_ref[:, inner:] = (tails_bc[...] + back[:, inner:]).astype(bf16)
     out_wx[...] = total[0:CONV, 0:inner]
     out_bx[...] = total[CONV : CONV + 1, 0:inner]
-    out_wb[...] = total[0 : CONV + 1, inner:]
+    for which in range(2):
+        for group in range(groups):
+            first = inner + (2 * group + which) * NSTATE
+            to = slice(group * NSTATE, (group + 1) * NSTATE)
+            out_wb[:, which, to] = total[0:CONV, first : first + NSTATE]
+            out_bb[which : which + 1, to] = total[CONV : CONV + 1, first : first + NSTATE]
     out_gain[...] = total[GAIN : GAIN + 1, 0:inner]
     heads = out_skip.shape[1]
     for out, shift in ((out_alog, 0), (out_dtb, STRETCH)):
@@ -626,18 +675,55 @@
     out_skip[...] = (dot(high, pick, last) + dot(low, pick, last))[0:1]
 
 
-def call(kernel, operands, outs, scratch, flops, name, blocked=False):
-    cuts = [cut or {} for _, cut in operands]
-    arrays = [array for array, _ in operands]
+def call(kernel, operands, outs, scratch, flops, name, blocked=None, hbm_outs=()):
+    operands = [(each + (None,))[:3] for each in operands]
+    cuts = [cut or {} for _, cut, _ in operands]
+    arrays = [array for array, _, _ in operands]
+    stages = [stage for _, _, stage in operands]
     shapes = [jax.ShapeDtypeStruct(shape, dtype) for shape, dtype in outs]
+    streamed = [place for place, stage in enumerate(stages) if stage is not None]
+    buffers = []
+    for place in streamed:
+        cut = cuts[place]
+        shape = tuple(
+            cut[dim].stop - cut[dim].start if dim in cut else extent
+            for dim, extent in enumerate(arrays[place].shape)
+        )
+        buffers.append(pltpu.VMEM(shape, arrays[place].dtype))
+    copies_made = sum(len(stages[place]) for place in streamed)
 
     def body(*refs):
-        seen = []
-        for ref, cut in zip(refs, cuts):
+        count, made = len(cuts), len(buffers)
+        rest = refs[count:]
+        held = dict(zip(streamed, rest[len(rest) - made - 1 : len(rest) - 1])) if made else {}
+        sems = rest[-1] if made else None
+        seen, copies = [], []
+        for place, (ref, cut) in enumerate(zip(refs, cuts)):
             if cut:
                 ref = ref.at[tuple(cut.get(dim, slice(None)) for dim in range(len(ref.shape)))]
+            if place in held:
+                buffer = held[place]
+                size = buffer.shape[-1] // len(stages[place])
+                for turn, stage in enumerate(stages[place]):
+                    part = (slice(None),) * (len(buffer.shape) - 1) + (
+                        slice(turn * size, (turn + 1) * size),
+                    )
+                    copy = (stage, (ref.at[part], buffer.at[part], sems.at[len(copies)]))
+                    copies.append(copy)
+                ref = buffer
             seen.append(ref)
-        kernel(*seen, *refs[len(cuts) :])
+        for _, copy in sorted(copies, key=lambda each: each[0]):
+            pltpu.make_async_copy(*copy).start()
+
+        def ready(stage):
+            for which, copy in copies:
+                if which == stage:
+                    pltpu.make_async_copy(*copy).wait()
+
+        if made:
+            kernel(*seen, *rest[: len(rest) - made - 1], ready=ready)
+        else:
+            kernel(*seen, *rest)
 
     def block_of(array, cut):
         shape, index = [], []
@@ -649,20 +735,27 @@
         return pl.BlockSpec(tuple(shape), functools.partial(lambda fixed, i: fixed, tuple(index)))
 
     in_vmem = pl.BlockSpec(memory_space=pltpu.VMEM)
+    in_hbm = pl.BlockSpec(memory_space=pltpu.HBM)
+    scratch_shapes = [
+        pltpu.VMEM(each, f32) if isinstance(each, tuple) else each for each in scratch
+    ]
     if blocked:
-        grid, limit = {"grid": (1,)}, BLOCKED_LIMIT
+        grid, limit = {"grid": (1,)}, blocked
         in_specs = [block_of(array, cut) for array, cut in zip(arrays, cuts)]
         out_specs = [block_of(shape, {}) for shape in shapes]
     else:
-        grid, limit = {}, VMEM_LIMIT
-        in_specs, out_specs = [in_vmem] * len(arrays), [in_vmem] * len(shapes)
+        grid, limit = {}, STREAM_LIMIT if buffers else VMEM_LIMIT
+        in_specs = [in_vmem if stage is None else in_hbm for stage in stages]
+        out_specs = [in_hbm if place in hbm_outs else in_vmem for place in range(len(shapes))]
+        if buffers:
+            scratch_shapes += buffers + [pltpu.SemaphoreType.DMA((copies_made,))]
     count = sum(each.size * each.dtype.itemsize for each in arrays + shapes)
     return pl.pallas_call(
         kernel if blocked else body,
         in_specs=in_specs,
         out_specs=out_specs,
         out_shape=shapes,
-        scratch_shapes=[pltpu.VMEM(shape, f32) for shape in scratch],
+        scratch_shapes=scratch_shapes,
         compiler_params=pltpu.CompilerParams(vmem_limit_bytes=limit),
         cost_estimate=pl.CostEstimate(flops=flops, bytes_accessed=count, transcendentals=0),
         name=name,
@@ -700,13 +793,15 @@
     return list(zip(early, last)), results
 
 
-def exchange_sum(value, axis):
+def exchange_terms(value, axis):
     count = lax.axis_size(axis)
+    other = jnp.zeros_like(value)
     stride = 1
     while stride < count:
-        value = value + lax.ppermute(value, axis, [(i, i ^ stride) for i in range(count)])
+        value = value + other if stride > 1 else value
+        other = lax.ppermute(value, axis, [(i, i ^ stride) for i in range(count)])
         stride *= 2
-    return value
+    return value, other
 
 
 def per_device(
@@ -732,18 +827,18 @@
     sent = call(
         tails,
         [
-            (x_raw, {1: slice(rows - 16, rows)}),
-            (bc_raw, {1: slice(rows - 16, rows)}),
-            (flags, {1: slice(rows - STRETCH, rows)}),
+            (x_raw, {1: slice(rows - 16, rows)}, [0]),
+            (bc_raw, {1: slice(rows - 16, rows)}, [0]),
+            (flags, {1: slice(rows - STRETCH, rows)}, [0]),
         ],
         [((HALO, inner + groups * width), f32)],
         [],
         rows,
         "tails",
-        True,
     )[0]
     halo = lax.ppermute(sent, "ctx", [(i, i + 1) for i in range(count - 1)])
-    alog_row, dtb_row, skip_row = a_log[None], dt_bias[None], skip_weight[None]
+    head_rows = jnp.stack([a_log, dt_bias, skip_weight])
+    head_rows = jnp.pad(head_rows, ((0, PAD - 3), (0, -head_rows.shape[1] % STRETCH)))
     bx, gain = conv_x_bias[None], norm_gain[None]
     wb, bb = by_group(conv_bc_weight), by_group(conv_bc_bias)[None]
 
@@ -776,7 +871,7 @@
                 [
                     wide(x_own, g), wide(halo, g), narrow(bc_own, g), narrow(halo, g, inner),
                     wide(conv_x_weight, g), wide(bx, g), narrow(wb, g), narrow(bb, g),
-                    per_head(dt_own, g), whole(dtb_row), whole(alog_row), whole(flags),
+                    per_head(dt_own, g), whole(head_rows), whole(flags),
                 ],
                 [
                     (tall, bf16), (tall, bf16), (tall, f32), (thin, bf16), (thin, f32),
@@ -810,55 +905,54 @@
         s_dev, decay, "ctx", False, [(forward_work(g), bcc[g]) for g in group_range]
     )
     y_within, slope_x, slope_bc = zip(*held)
-    held = [
-        call(
+    held, sums = [], ()
+    for g in group_range:
+        bundle, total = call(
             functools.partial(gate_forward, group=g),
             [
                 whole(y_within[g]), whole(prior[g][0]), whole(prior[g][1]), whole(s_loc[g]),
                 whole(keep[g]), whole(bcc[g]), whole(run[g]), whole(flags), whole(xc[g]),
-                whole(skip_row), wide(z_own, g), wide(go_own, g), wide(gain, g),
-            ],
-            [(tall, f32), (tall, bf16), ((PAD, rows), f32)],
+                whole(head_rows), wide(z_own, g), wide(go_own, g), wide(gain, g),
+            ]
+            + [whole(each) for each in sums],
+            [((bundle_rows(rows)[-1], channels), f32), ((2, rows), f32)],
             [wide_scratch, (PAD, channels)],
             2 * work,
             "gate_forward",
         )
-        for g in group_range
-    ]
-    y_ssd, mixed, sums = zip(*held)
-    totals = exchange_sum(sum(sums[1:], sums[0]), "head")
+        sums = (total,)
+        held.append(bundle)
+    bundle = held
+    own, other = exchange_terms(sums[0], "head")
     held = [
         call(
-            gate_backward,
-            [
-                whole(totals), whole(mixed[g]), wide(z_own, g), wide(go_own, g), wide(gain, g),
-                whole(keep[g]), whole(bcc[g]), whole(run[g]), whole(flags),
-            ],
-            [(tall, bf16), (state_shape, bf16), (local_shape, bf16)],
+            functools.partial(gate_backward, heads=heads),
+            [whole(own), whole(other), whole(bundle[g]), wide(z_own, g), wide(go_own, g)],
+            [(tall, bf16), (state_shape, bf16), (local_shape, bf16), ((2, rows), f32)],
             [wide_scratch, state_shape],
             2 * work,
             "gate_backward",
         )
         for g in group_range
     ]
-    dy, a_dev, a_loc = zip(*held)
+    dy, a_dev, a_loc, totals = zip(*held)
 
     def backward_work(g):
         return lambda bcc_now: call(
-            within_backward,
+            functools.partial(within_backward, group=g),
             [
-                whole(totals), whole(mixed[g]), wide(z_own, g), wide(go_own, g), wide(gain, g),
-                whole(dy[g]), whole(y_ssd[g]), whole(xc[g]), whole(xp[g]), whole(bcc_now),
+                whole(totals[g]), whole(bundle[g]), wide(z_own, g), wide(go_own, g),
+                whole(dy[g]), whole(xc[g]), whole(xp[g]), whole(bcc_now),
                 whole(run[g]), whole(flags), whole(prior[g][0]), whole(prior[g][1]), whole(s_loc[g]),
-                whole(keep[g]),
+                whole(keep[g]), whole(head_rows),
             ],
             [
                 (tall, bf16), (tall, f32), (thin, f32), (row_shape, f32), ((PAD, channels), f32),
             ],
-            run_scratch + [wide_scratch],
+            run_scratch + [wide_scratch, (PAD, channels)],
             10 * work,
             "within_backward",
-            True,
+            BLOCKED_LIMIT,
         )
 
     later, held = chain(
@@ -871,11 +965,10 @@
             [
                 whole(later[g][0]), whole(later[g][1]), whole(a_loc[g]), whole(prior[g][0]),
                 whole(prior[g][1]), whole(s_loc[g]), whole(keep[g]), whole(dxp[g]), whole(dbc[g]),
-                whole(drun[g]), whole(xp[g]), whole(dy[g]), whole(skip_row), whole(bcc[g]),
-                whole(run[g]), whole(dt[g]), whole(flags), whole(slope_x[g]), whole(slope_bc[g]),
-                wide(x_own, g), wide(halo, g), narrow(bc_own, g), narrow(halo, g, inner),
-                wide(conv_x_weight, g), narrow(wb, g), whole(alog_row), whole(dtb_row),
-                per_head(dt_own, g), whole(chan[g]),
+                whole(drun[g]), whole(xp[g]), whole(dy[g]), whole(bcc[g]), whole(run[g]),
+                whole(dt[g]), whole(flags), whole(slope_x[g]), whole(slope_bc[g]), wide(x_own, g),
+                wide(halo, g), narrow(bc_own, g), narrow(halo, g, inner), wide(conv_x_weight, g),
+                narrow(wb, g), whole(head_rows), per_head(dt_own, g), whole(chan[g]),
             ],
             [
                 (tall, bf16), ((HALO, channels), f32), ((PACKED, channels), f32), (thin, bf16),
@@ -887,7 +980,7 @@
             ],
             4 * work,
             "finish_backward",
-            True,
+            BLOCKED_LIMIT,
         )
         for g in group_range
     ]
@@ -914,7 +1007,7 @@
         arrived.append(lax.ppermute(leaving, "ctx", [(i, i ^ shift) for i in range(count)]))
         picks.append((here ^ shift) == here + 1)
     pick = jnp.broadcast_to(jnp.stack(picks).astype(f32)[:, None], (count - 1, STRETCH))
-    out_wx, out_bx, out_wb, out_alog, out_dtb, out_skip, out_gain, ending = call(
+    out_wx, out_bx, out_wb, out_bb, out_alog, out_dtb, out_skip, out_gain, ending = call(
         functools.partial(
             final_sums,
             arrivals=count - 1,
@@ -925,7 +1018,8 @@
         + [whole(each) for each in arrived]
         + [whole(joined(x_tail)), whole(joined(bc_tail))],
         [
-            ((CONV, inner), f32), ((1, inner), f32), ((CONV + 1, groups * width), f32),
+            ((CONV, inner), f32), ((1, inner), f32), ((CONV, 2, groups * NSTATE), f32),
+            ((2, groups * NSTATE), f32),
             ((1, groups * heads), f32), ((1, groups * heads), f32), ((1, groups * heads), f32),
             ((1, inner), f32), ((HALO, inner + groups * width), bf16),
         ],
@@ -937,7 +1031,6 @@
     grad_bc = lax.dynamic_update_slice(
         ungroup(joined(gbc)), ungroup(ending[:, inner:]), (rows - HALO, 0, 0)
     )
-    bc_terms = ungroup(out_wb)
     return (
         grad_x[None],
         grad_bc[None],
@@ -945,8 +1038,8 @@
         jnp.concatenate(gdt, axis=0)[None],
         out_wx,
         out_bx[0],
-        bc_terms[:CONV],
-        bc_terms[CONV],
+        out_wb,
+        out_bb,
         out_alog[0],
         out_dtb[0],
         out_skip[0],

time: 118 us -> 113 us (0.958)
  local copies, waits for them, and re-layouts: 14.7 us -> 5.99 us
  Pallas kernels: 45.3 us -> 49 us
    unnamed x183 -> x141, local copies, waits for them, and re-layouts: 12.3 us -> 5.46 us
    pallas_call x14, Pallas kernels: 45.3 us -> 49 us  [call(): pl.pallas_call(kernel if blocked else body, in_specs=in_specs, out_specs=...]
  transfers between devices with their start and end apart: 19 -> 19, of which waited for: 8 -> 8; matrix products, arithmetic and copies ran while one was open for 4% -> 3% of each run, Pallas kernels for 26% -> 28%
where the time goes in v3:
time: 113 us; the launch traced here: 112 us
  Pallas kernels  49 us (43%)
  starting transfers between devices  26.5 us (23%)
  waiting for transfers between devices  24.8 us (22%)
  local copies, waits for them, and re-layouts  5.99 us (5%)
  other arithmetic  4.02 us (4%)
  between operations  1.93 us (2%)
    pallas_call x14, Pallas kernels, call(): pl.pallas_call(kernel if blocked else body, in_specs=in_specs, out_specs=...  49 us
    ppermute x12, starting transfers between devices, chain(): last = [lax.ppermute(each, axis, pairs) for each in leaving]  14 us
    ppermute x12, waiting for transfers between devices, chain(): last = [lax.ppermute(each, axis, pairs) for each in leaving]  12.6 us
    unnamed x141, local copies, waits for them, and re-layouts  5.46 us
    ppermute x3, waiting for transfers between devices, per_device(): lax.ppermute(leaving, 'ctx', [(i, i ^ shift) for i in range(count)])  5.35 us
    ppermute x1, starting transfers between devices, per_device(): halo = lax.ppermute(sent, 'ctx', [(i, i + 1) for i in range(count - 1)])  4.93 us
    ppermute x2, waiting for transfers between devices, exchange_terms(): other = lax.ppermute(value, axis, [(i, i ^ stride) for i in range(count)])  4.45 us
    ppermute x3, starting transfers between devices, per_device(): lax.ppermute(leaving, 'ctx', [(i, i ^ shift) for i in range(count)])  4.44 us
  transfers between devices with their start and end apart: 19, of which 8 were waited for; matrix products, arithmetic and copies ran while one was open for 3% of the time, Pallas kernels for 28%

profile of v3, /device:TPU:0, one launch (start us, length us, event | category | flops | bytes accessed | tf_op | source)
XLA Modules:
  0.0 112.2 jit_solution(4595885360249572722)
XLA Ops:
  0.8 1.8 %tails.1 = f32[3,2560]{1,0:T(4,128)} custom-call(bf16[1,256,2048]{2,1,0:T(8,128)(2,1)} %refs_0_.1, bf16[1,256,2,256]{3,2,1,0:T(2,128)(2,1)} %refs_1_.1, s32[1,256]{1,0:T(1,128)} %refs_2_.3), custom_call_target="tpu_custom_call" | custom-call | flops 256 | bytes 1342464 | tf_op jit(solution)/shard_map/tails/pallas_call | solution.py:753
  2.5 4.9 %collective-permute-start = (f32[3,2560]{1,0:T(4,128)}, f32[3,2560]{1,0:T(4,128)S(1)}, u32[]{:S(2)}, u32[]{:S(2)}) collective-permute-start(f32[3,2560]{1,0:T(4,128)} %tails.1), channel_id=1, source_target_pairs={{0,4},{4,8},{8,12},{1,5},{5,9},{9,13},{2,6},{6,10},{10,14},{3,7},{... | collective-permute-start | bytes 92168 | tf_op jit(solution)/shard_map/ppermute | solution.py:839
  7.7 1.8 %collective-permute-done.refs_1_.refs_3_.xh_ref.bch_ref = f32[3,2560]{1,0:T(4,128)S(1)} collective-permute-done((f32[3,2560]{1,0:T(4,128)}, f32[3,2560]{1,0:T(4,128)S(1)}, u32[]{:S(2)}, u32[]{:S(2)}) %collective-permute-start) | collective-permute-done | bytes 30752 | tf_op jit(solution)/shard_map/ppermute | solution.py:839
  9.5 3.5 %conv_and_state.2 = (bf16[256,1024]{1,0:T(8,128)(2,1)S(1)}, bf16[256,1024]{1,0:T(8,128)(2,1)S(1)}, f32[256,1024]{1,0:T(8,128)S(1)}, bf16[256,256]{1,0:T(8,128)(2...) custom-call(bf16[256,2048]{1,0:T(8,128)(2,1)S(1)} %bitcast.57, ...), custom_call_target="tpu_custom_call" | custom-call | flops 67108864 | bytes 4525056 | tf_op jit(solution)/shard_map/conv_and_state/pallas_call | solution.py:753
  13.6 4.1 %collective-permute-start.1 = (bf16[128,1024]{1,0:T(8,128)(2,1)S(1)}, bf16[128,1024]{1,0:T(8,128)(2,1)S(1)}, u32[]{:S(2)}, u32[]{:S(2)}) collective-permute-start(bf16[128,1024]{1,0:T(8,128)(2,1)S(1)} %get-tuple-element.108), channel_id=1, source_target_pairs={{0,4},{1,5},{2,6},{3,7},{16,20},{17,21},{18,22},{19,23}} | collective-permute-start | bytes 786440 | tf_op jit(solution)/shard_map/ppermute | solution.py:786
  17.7 3.5 %conv_and_state.3 = (bf16[256,1024]{1,0:T(8,128)(2,1)S(1)}, bf16[256,1024]{1,0:T(8,128)(2,1)S(1)}, f32[256,1024]{1,0:T(8,128)S(1)}, bf16[256,256]{1,0:T(8,128)(2...) custom-call(bf16[256,2048]{1,0:T(8,128)(2,1)S(1)} %bitcast.58, ...), custom_call_target="tpu_custom_call" | custom-call | flops 67108864 | bytes 4525056 | tf_op jit(solution)/shard_map/conv_and_state/pallas_call | solution.py:753
  22.6 2.4 %within_blocks.2 = (f32[256,1024]{1,0:T(8,128)S(1)}, f32[256,1024]{1,0:T(8,128)S(1)}, f32[256,256]{1,0:T(8,128)S(1)}) custom-call(bf16[256,1024]{1,0:T(8,128)(2,1)S(1)} %get-tuple-element.109.refs_0_.xp_ref, bf16[256,256]{1,0:T(8,128)(2,1)S(1)} %get-tuple-element.145.refs_1_.refs_5_.bcc_ref, f32[16,256]{1,0:T(8,128)S(1)} %get-tuple-element.113.refs_2_.refs_6_.run_ref, ...), custom_call_target="tpu_custom_call" | custom-call | flops 201326592 | bytes 4342784 | tf_op jit(solution)/shard_map/within_blocks/pallas_call | solution.py:753
  25.9 1.8 %collective-permute-done.3 = bf16[128,1024]{1,0:T(8,128)(2,1)S(1)} collective-permute-done((bf16[128,1024]{1,0:T(8,128)(2,1)S(1)}, bf16[128,1024]{1,0:T(8,128)(2,1)S(1)}, u32[]{:S(2)}, u32[]{:S(2)}) %collective-permute-start.3) | collective-permute-done | bytes 262176 | tf_op jit(solution)/shard_map/ppermute | solution.py:786
  28.5 2.4 %within_blocks.3 = (f32[256,1024]{1,0:T(8,128)S(1)}, f32[256,1024]{1,0:T(8,128)S(1)}, f32[256,256]{1,0:T(8,128)S(1)}) custom-call(bf16[256,1024]{1,0:T(8,128)(2,1)S(1)} %get-tuple-element.120.refs_0_.xp_ref, bf16[256,256]{1,0:T(8,128)(2,1)S(1)} %get-tuple-element.154.refs_1_.refs_5_.bcc_ref, f32[16,256]{1,0:T(8,128)S(1)} %get-tuple-element.124.refs_2_.refs_6_.run_ref, ...), custom_call_target="tpu_custom_call" | custom-call | flops 201326592 | bytes 4342784 | tf_op jit(solution)/shard_map/within_blocks/pallas_call | solution.py:753
  33.1 2.4 %gate_forward.2 = (f32[320,1024]{1,0:T(8,128)S(1)}, f32[2,256]{1,0:T(2,128)S(1)}) custom-call(f32[256,1024]{1,0:T(8,128)S(1)} %get-tuple-element.133.refs_0_, bf16[128,1024]{1,0:T(8,128)(2,1)S(1)} %get-tuple-element.209.refs_1_.early_ref, bf16[128,1024]{1,0:T(8,128)(2,1)S(1)} %collective-permute-done.6.refs_2_.last_ref, ...), custom_call_target="tpu_custom_call" | custom-call | flops 67108864 | bytes 5962752 | tf_op jit(solution)/shard_map/gate_forward/pallas_call | solution.py:753
  36.6 2.4 %gate_forward.3 = (f32[320,1024]{1,0:T(8,128)S(1)}, f32[2,256]{1,0:T(2,128)S(1)}) custom-call(f32[256,1024]{1,0:T(8,128)S(1)} %get-tuple-element.130.refs_0_, bf16[128,1024]{1,0:T(8,128)(2,1)S(1)} %get-tuple-element.211.refs_1_.early_ref, bf16[128,1024]{1,0:T(8,128)(2,1)S(1)} %collective-permute-done.5.refs_2_.last_ref, ...), custom_call_target="tpu_custom_call" | custom-call | flops 67108864 | bytes 5964800 | tf_op jit(solution)/shard_map/gate_forward/pallas_call | solution.py:753
  40.0 1.5 %collective-permute-start.7 = (f32[2,256]{1,0:T(2,128)S(1)}, f32[2,256]{1,0:T(2,128)S(1)}, u32[]{:S(2)}, u32[]{:S(2)}) collective-permute-start(f32[2,256]{1,0:T(2,128)S(1)} %get-tuple-element.138), channel_id=1, source_target_pairs={{0,1},{1,0},{2,3},{3,2},{4,5},{5,4},{6,7},{7,6},{8,9},{9,8},{10,11... | collective-permute-start | bytes 6152 | tf_op jit(solution)/shard_map/ppermute | solution.py:802
  41.5 2.1 %collective-permute-done.7 = f32[2,256]{1,0:T(2,128)S(1)} collective-permute-done((f32[2,256]{1,0:T(2,128)S(1)}, f32[2,256]{1,0:T(2,128)S(1)}, u32[]{:S(2)}, u32[]{:S(2)}) %collective-permute-start.7) | collective-permute-done | bytes 2080 | tf_op jit(solution)/shard_map/ppermute | solution.py:802
  44.2 1.5 %collective-permute-start.8 = (f32[2,256]{1,0:T(2,128)}, f32[2,256]{1,0:T(2,128)}, u32[]{:S(2)}, u32[]{:S(2)}) collective-permute-start(f32[2,256]{1,0:T(2,128)} %add.55.refs_0_), channel_id=1, source_target_pairs={{0,2},{1,3},{2,0},{3,1},{4,6},{5,7},{6,4},{7,5},{8,10},{9,11},{10,... | collective-permute-start | bytes 6152 | tf_op jit(solution)/shard_map/ppermute | solution.py:802
  45.7 2.4 %collective-permute-done.8.refs_1_ = f32[2,256]{1,0:T(2,128)} collective-permute-done((f32[2,256]{1,0:T(2,128)}, f32[2,256]{1,0:T(2,128)}, u32[]{:S(2)}, u32[]{:S(2)}) %collective-permute-start.8) | collective-permute-done | bytes 2080 | tf_op jit(solution)/shard_map/ppermute | solution.py:802
  49.4 2.6 %gate_backward.2 = (bf16[256,1024]{1,0:T(8,128)(2,1)S(1)}, bf16[128,1024]{1,0:T(8,128)(2,1)S(1)}, bf16[1,128,1024]{2,1,0:T(8,128)(2,1)S(1)}, f32[2,256]{1,0:T(2,128)S(1)}) custom-call(f32[2,256]{1,0:T(2,128)} %add.55.refs_0_, f32[2,256]{1,0:T(2,128)} %collective-permute-done.8.refs_1_, f32[320,1024]{1,0:T(8,128)S(1)} %copy-done.6, ...), custom_call_target="tpu_custom_call" | custom-call | flops 67108864 | bytes 4462592 | tf_op jit(solution)/shard_map/gate_backward/pallas_call | solution.py:753
  53.5 2.7 %gate_backward.3 = (bf16[256,1024]{1,0:T(8,128)(2,1)S(1)}, bf16[128,1024]{1,0:T(8,128)(2,1)S(1)}, bf16[1,128,1024]{2,1,0:T(8,128)(2,1)S(1)}, f32[2,256]{1,0:T(2,128)S(1)}) custom-call(f32[2,256]{1,0:T(2,128)} %add.55.refs_0_, f32[2,256]{1,0:T(2,128)} %collective-permute-done.8.refs_1_, f32[320,1024]{1,0:T(8,128)S(1)} %copy-done.4, ...), custom_call_target="tpu_custom_call" | custom-call | flops 67108864 | bytes 4462592 | tf_op jit(solution)/shard_map/gate_backward/pallas_call | solution.py:753
  57.1 5.9 %within_backward.2 = (bf16[256,1024]{1,0:T(8,128)(2,1)S(1)}, f32[256,1024]{1,0:T(8,128)S(1)}, f32[256,256]{1,0:T(8,128)S(1)}, f32[16,256]{1,0:T(8,128)S(1)}, f32[8,1024]{1,0:T(8,128)S(1)}) custom-call(f32[2,256]{1,0:T(2,128)S(1)} %get-tuple-element.141.totals_ref, f32[320,1024]{1,0:T(8,128)S(1)} %copy-done.7, bf16[256,2048]{1,0:T(8,128)(2,1)S(1)} %bitcast.49, ...), custom_call_target="tpu_custom_call" | custom-call | flops 335544320 | bytes 7838720 | tf_op jit(solution)/shard_map/within_backward/pallas_call | solution.py:753
  64.9 5.9 %within_backward.3 = (bf16[256,1024]{1,0:T(8,128)(2,1)S(1)}, f32[256,1024]{1,0:T(8,128)S(1)}, f32[256,256]{1,0:T(8,128)S(1)}, f32[16,256]{1,0:T(8,128)S(1)}, f32[8,1024]{1,0:T(8,128)S(1)}) custom-call(f32[2,256]{1,0:T(2,128)S(1)} %get-tuple-element.152.totals_ref, f32[320,1024]{1,0:T(8,128)S(1)} %copy-done.4, bf16[256,2048]{1,0:T(8,128)(2,1)S(1)} %bitcast.50, ...), custom_call_target="tpu_custom_call" | custom-call | flops 335544320 | bytes 7838720 | tf_op jit(solution)/shard_map/within_backward/pallas_call | solution.py:753
  75.0 10.8 %collective-permute-done.12.later_last = bf16[128,1024]{1,0:T(8,128)(2,1)S(1)} collective-permute-done((bf16[128,1024]{1,0:T(8,128)(2,1)S(1)}, bf16[128,1024]{1,0:T(8,128)(2,1)S(1)}, u32[]{:S(2)}, u32[]{:S(2)}) %collective-permute-start.12) | collective-permute-done | bytes 262176 | tf_op jit(solution)/shard_map/ppermute | solution.py:786
  85.8 6.4 %finish_backward.2 = (bf16[256,1024]{1,0:T(8,128)(2,1)S(1)}, f32[3,1024]{1,0:T(4,128)S(1)}, f32[10,1024]{1,0:T(8,128)S(1)}, bf16[256,256]{1,0:T(8,128)(2,1)S(1)}...) custom-call(bf16[128,1024]{1,0:T(8,128)(2,1)S(1)} %get-tuple-element.205.later_early, ...), custom_call_target="tpu_custom_call" | custom-call | flops 134217728 | bytes 7661568 | tf_op jit(solution)/shard_map/finish_backward/pallas_call | solution.py:753
  92.2 6.4 %finish_backward.3 = (bf16[256,1024]{1,0:T(8,128)(2,1)S(1)}, f32[3,1024]{1,0:T(4,128)S(1)}, f32[10,1024]{1,0:T(8,128)S(1)}, bf16[256,256]{1,0:T(8,128)(2,1)S(1)}...) custom-call(bf16[128,1024]{1,0:T(8,128)(2,1)S(1)} %get-tuple-element.207.later_early, ...), custom_call_target="tpu_custom_call" | custom-call | flops 134217728 | bytes 7661568 | tf_op jit(solution)/shard_map/finish_backward/pallas_call | solution.py:753
  100.5 4.1 %collective-permute-start.18 = (bf16[10,2560]{1,0:T(8,128)(2,1)S(1)}, bf16[10,2560]{1,0:T(8,128)(2,1)S(1)}, u32[]{:S(2)}, u32[]{:S(2)}) collective-permute-start(bf16[10,2560]{1,0:T(8,128)(2,1)S(1)} %get-tuple-element.202), channel_id=1, source_target_pairs={{0,12},{4,8},{8,4},{12,0},{1,13},{5,9},{9,5},{13,1},{2,14},{6,10},... | collective-permute-start | bytes 153608 | tf_op jit(solution)/shard_map/ppermute | solution.py:1007
  105.8 4.3 %collective-permute-done.17.refs_4_ = bf16[10,2560]{1,0:T(8,128)(2,1)S(1)} collective-permute-done((bf16[10,2560]{1,0:T(8,128)(2,1)S(1)}, bf16[10,2560]{1,0:T(8,128)(2,1)S(1)}, u32[]{:S(2)}, u32[]{:S(2)}) %collective-permute-start.17) | collective-permute-done | bytes 51232 | tf_op jit(solution)/shard_map/ppermute | solution.py:1007
  (200 shorter events, 22.8 us)
Async XLA Ops:
  2.5 6.9 %collective-permute-start = (f32[3,2560]{1,0:T(4,128)}, f32[3,2560]{1,0:T(4,128)S(1)}, u32[]{:S(2)}, u32[]{:S(2)}) collective-permute-start(f32[3,2560]{1,0:T(4,128)} %tails.1), channel_id=1, source_target_pairs={{0,4},{4,8},{8,12},{1,5},{5,9},{9,13},{2,6},{6,10},{10,14},{3,7},{... | collective-permute-start | bytes 92168 | tf_op jit(solution)/shard_map/ppermute | solution.py:839
  13.5 19.4 %copy-start.18 = (bf16[1,128,1024]{2,1,0:T(8,128)(2,1)}, bf16[1,128,1024]{2,1,0:T(8,128)(2,1)S(1)}, u32[]{:S(2)}) copy-start(bf16[1,128,1024]{2,1,0:T(8,128)(2,1)S(1)} %get-tuple-element.135.refs_3_.sloc_ref) | copy-start | bytes 786436
  13.5 19.4 %copy-start.24 = (bf16[256,1024]{1,0:T(8,128)(2,1)}, bf16[256,1024]{1,0:T(8,128)(2,1)S(1)}, u32[]{:S(2)}) copy-start(bf16[256,1024]{1,0:T(8,128)(2,1)S(1)} %get-tuple-element.136.refs_8_.xc_ref) | copy-start | bytes 1572868
  13.5 19.4 %copy-start.30 = (bf16[256,256]{1,0:T(8,128)(2,1)}, bf16[256,256]{1,0:T(8,128)(2,1)S(1)}, u32[]{:S(2)}) copy-start(bf16[256,256]{1,0:T(8,128)(2,1)S(1)} %get-tuple-element.145.refs_1_.refs_5_.bcc_ref) | copy-start | bytes 393220
  13.5 19.4 %copy-start.41 = (f32[16,256]{1,0:T(8,128)}, f32[16,256]{1,0:T(8,128)S(1)}, u32[]{:S(2)}) copy-start(f32[16,256]{1,0:T(8,128)S(1)} %get-tuple-element.113.refs_2_.refs_6_.run_ref) | copy-start | bytes 49156
  13.6 11.5 %collective-permute-start.1 = (bf16[128,1024]{1,0:T(8,128)(2,1)S(1)}, bf16[128,1024]{1,0:T(8,128)(2,1)S(1)}, u32[]{:S(2)}, u32[]{:S(2)}) collective-permute-start(bf16[128,1024]{1,0:T(8,128)(2,1)S(1)} %get-tuple-element.108), channel_id=1, source_target_pairs={{0,4},{1,5},{2,6},{3,7},{16,20},{17,21},{18,22},{19,23}} | collective-permute-start | bytes 786440 | tf_op jit(solution)/shard_map/ppermute | solution.py:786
  21.2 15.3 %copy-start.16 = (bf16[1,128,1024]{2,1,0:T(8,128)(2,1)}, bf16[1,128,1024]{2,1,0:T(8,128)(2,1)S(1)}, u32[]{:S(2)}) copy-start(bf16[1,128,1024]{2,1,0:T(8,128)(2,1)S(1)} %get-tuple-element.131.refs_3_.sloc_ref) | copy-start | bytes 786436
  21.2 6.4 %collective-permute-start.3 = (bf16[128,1024]{1,0:T(8,128)(2,1)S(1)}, bf16[128,1024]{1,0:T(8,128)(2,1)S(1)}, u32[]{:S(2)}, u32[]{:S(2)}) collective-permute-start(bf16[128,1024]{1,0:T(8,128)(2,1)S(1)} %get-tuple-element.111), channel_id=1, source_target_pairs={{0,4},{1,5},{2,6},{3,7},{16,20},{17,21},{18,22},{19,23}} | collective-permute-start | bytes 786440 | tf_op jit(solution)/shard_map/ppermute | solution.py:786
  25.2 5.8 %collective-permute-start.2 = (bf16[128,1024]{1,0:T(8,128)(2,1)S(1)}, bf16[128,1024]{1,0:T(8,128)(2,1)S(1)}, u32[]{:S(2)}, u32[]{:S(2)}) collective-permute-start(bf16[128,1024]{1,0:T(8,128)(2,1)S(1)} %fusion), channel_id=1, source_target_pairs={{4,8},{5,9},{6,10},{7,11},{20,24},{21,25},{22,26},{23,27}} | collective-permute-start | bytes 786440 | tf_op jit(solution)/shard_map/ppermute | solution.py:786
  27.8 4.2 %collective-permute-start.4 = (bf16[128,1024]{1,0:T(8,128)(2,1)S(1)}, bf16[128,1024]{1,0:T(8,128)(2,1)S(1)}, u32[]{:S(2)}, u32[]{:S(2)}) collective-permute-start(bf16[128,1024]{1,0:T(8,128)(2,1)S(1)} %fusion.2), channel_id=1, source_target_pairs={{4,8},{5,9},{6,10},{7,11},{20,24},{21,25},{22,26},{23,27}} | collective-permute-start | bytes 786440 | tf_op jit(solution)/shard_map/ppermute | solution.py:786
  31.2 1.7 %collective-permute-start.6 = (bf16[128,1024]{1,0:T(8,128)(2,1)S(1)}, bf16[128,1024]{1,0:T(8,128)(2,1)S(1)}, u32[]{:S(2)}, u32[]{:S(2)}) collective-permute-start(bf16[128,1024]{1,0:T(8,128)(2,1)S(1)} %get-tuple-element.208), channel_id=1, source_target_pairs={{8,12},{9,13},{10,14},{11,15},{24,28},{25,29},{26,30},{27,31}} | collective-permute-start | bytes 786440 | tf_op jit(solution)/shard_map/ppermute | solution.py:786
  32.2 4.3 %collective-permute-start.5 = (bf16[128,1024]{1,0:T(8,128)(2,1)S(1)}, bf16[128,1024]{1,0:T(8,128)(2,1)S(1)}, u32[]{:S(2)}, u32[]{:S(2)}) collective-permute-start(bf16[128,1024]{1,0:T(8,128)(2,1)S(1)} %get-tuple-element.210), channel_id=1, source_target_pairs={{8,12},{9,13},{10,14},{11,15},{24,28},{25,29},{26,30},{27,31}} | collective-permute-start | bytes 786440 | tf_op jit(solution)/shard_map/ppermute | solution.py:786
  40.0 3.6 %collective-permute-start.7 = (f32[2,256]{1,0:T(2,128)S(1)}, f32[2,256]{1,0:T(2,128)S(1)}, u32[]{:S(2)}, u32[]{:S(2)}) collective-permute-start(f32[2,256]{1,0:T(2,128)S(1)} %get-tuple-element.138), channel_id=1, source_target_pairs={{0,1},{1,0},{2,3},{3,2},{4,5},{5,4},{6,7},{7,6},{8,9},{9,8},{10,11... | collective-permute-start | bytes 6152 | tf_op jit(solution)/shard_map/ppermute | solution.py:802
  44.2 3.9 %collective-permute-start.8 = (f32[2,256]{1,0:T(2,128)}, f32[2,256]{1,0:T(2,128)}, u32[]{:S(2)}, u32[]{:S(2)}) collective-permute-start(f32[2,256]{1,0:T(2,128)} %add.55.refs_0_), channel_id=1, source_target_pairs={{0,2},{1,3},{2,0},{3,1},{4,6},{5,7},{6,4},{7,5},{8,10},{9,11},{10,... | collective-permute-start | bytes 6152 | tf_op jit(solution)/shard_map/ppermute | solution.py:802
  52.1 11.0 %collective-permute-start.9 = (bf16[128,1024]{1,0:T(8,128)(2,1)S(1)}, bf16[128,1024]{1,0:T(8,128)(2,1)S(1)}, u32[]{:S(2)}, u32[]{:S(2)}) collective-permute-start(bf16[128,1024]{1,0:T(8,128)(2,1)S(1)} %get-tuple-element.140), channel_id=1, source_target_pairs={{12,8},{13,9},{14,10},{15,11},{28,24},{29,25},{30,26},{31,27}} | collective-permute-start | bytes 786440 | tf_op jit(solution)/shard_map/ppermute | solution.py:786
  56.2 7.9 %collective-permute-start.11 = (bf16[128,1024]{1,0:T(8,128)(2,1)S(1)}, bf16[128,1024]{1,0:T(8,128)(2,1)S(1)}, u32[]{:S(2)}, u32[]{:S(2)}) collective-permute-start(bf16[128,1024]{1,0:T(8,128)(2,1)S(1)} %get-tuple-element.144), channel_id=1, source_target_pairs={{12,8},{13,9},{14,10},{15,11},{28,24},{29,25},{30,26},{31,27}} | collective-permute-start | bytes 786440 | tf_op jit(solution)/shard_map/ppermute | solution.py:786
  63.2 7.6 %collective-permute-start.10 = (bf16[128,1024]{1,0:T(8,128)(2,1)S(1)}, bf16[128,1024]{1,0:T(8,128)(2,1)S(1)}, u32[]{:S(2)}, u32[]{:S(2)}) collective-permute-start(bf16[128,1024]{1,0:T(8,128)(2,1)S(1)} %fusion.4), channel_id=1, source_target_pairs={{8,4},{9,5},{10,6},{11,7},{24,20},{25,21},{26,22},{27,23}} | collective-permute-start | bytes 786440 | tf_op jit(solution)/shard_map/ppermute | solution.py:786
  64.2 8.1 %collective-permute-start.13 = (bf16[128,1024]{1,0:T(8,128)(2,1)S(1)}, bf16[128,1024]{1,0:T(8,128)(2,1)S(1)}, u32[]{:S(2)}, u32[]{:S(2)}) collective-permute-start(bf16[128,1024]{1,0:T(8,128)(2,1)S(1)} %fusion.6), channel_id=1, source_target_pairs={{8,4},{9,5},{10,6},{11,7},{24,20},{25,21},{26,22},{27,23}} | collective-permute-start | bytes 786440 | tf_op jit(solution)/shard_map/ppermute | solution.py:786
  71.0 14.8 %collective-permute-start.12 = (bf16[128,1024]{1,0:T(8,128)(2,1)S(1)}, bf16[128,1024]{1,0:T(8,128)(2,1)S(1)}, u32[]{:S(2)}, u32[]{:S(2)}) collective-permute-start(bf16[128,1024]{1,0:T(8,128)(2,1)S(1)} %get-tuple-element.204), channel_id=1, source_target_pairs={{4,0},{5,1},{6,2},{7,3},{20,16},{21,17},{22,18},{23,19}} | collective-permute-start | bytes 786440 | tf_op jit(solution)/shard_map/ppermute | solution.py:786
  72.5 19.7 %collective-permute-start.14 = (bf16[128,1024]{1,0:T(8,128)(2,1)S(1)}, bf16[128,1024]{1,0:T(8,128)(2,1)S(1)}, u32[]{:S(2)}, u32[]{:S(2)}) collective-permute-start(bf16[128,1024]{1,0:T(8,128)(2,1)S(1)} %get-tuple-element.206), channel_id=1, source_target_pairs={{4,0},{5,1},{6,2},{7,3},{20,16},{21,17},{22,18},{23,19}} | collective-permute-start | bytes 786440 | tf_op jit(solution)/shard_map/ppermute | solution.py:786
  98.7 1.5 %collective-permute-start.15 = (f32[10,2560]{1,0:T(8,128)S(1)}, f32[10,2560]{1,0:T(8,128)S(1)}, u32[]{:S(2)}, u32[]{:S(2)}) collective-permute-start(f32[10,2560]{1,0:T(8,128)S(1)} %constant_dynamic-update-slice_fusion), channel_id=1, source_target_pairs={{0,16},{16,0},{1,17},{17,1},{2,18},{18,2},{3,19},{19,3},{4,20},{20... | collective-permute-start | bytes 307208 | tf_op jit(solution)/shard_map/ppermute | solution.py:1001
  100.2 5.6 %collective-permute-start.16 = (bf16[10,2560]{1,0:T(8,128)(2,1)S(1)}, bf16[10,2560]{1,0:T(8,128)(2,1)S(1)}, u32[]{:S(2)}, u32[]{:S(2)}) collective-permute-start(bf16[10,2560]{1,0:T(8,128)(2,1)S(1)} %get-tuple-element.202), channel_id=1, source_target_pairs={{0,4},{4,0},{8,12},{12,8},{1,5},{5,1},{9,13},{13,9},{2,6},{6,2},{1... | collective-permute-start | bytes 153608 | tf_op jit(solution)/shard_map/ppermute | solution.py:1007
  100.3 9.8 %collective-permute-start.17 = (bf16[10,2560]{1,0:T(8,128)(2,1)S(1)}, bf16[10,2560]{1,0:T(8,128)(2,1)S(1)}, u32[]{:S(2)}, u32[]{:S(2)}) collective-permute-start(bf16[10,2560]{1,0:T(8,128)(2,1)S(1)} %get-tuple-element.202), channel_id=1, source_target_pairs={{0,8},{4,12},{8,0},{12,4},{1,9},{5,13},{9,1},{13,5},{2,10},{6,14},... | collective-permute-start | bytes 153608 | tf_op jit(solution)/shard_map/ppermute | solution.py:1007
  100.5 9.6 %collective-permute-start.18 = (bf16[10,2560]{1,0:T(8,128)(2,1)S(1)}, bf16[10,2560]{1,0:T(8,128)(2,1)S(1)}, u32[]{:S(2)}, u32[]{:S(2)}) collective-permute-start(bf16[10,2560]{1,0:T(8,128)(2,1)S(1)} %get-tuple-element.202), channel_id=1, source_target_pairs={{0,12},{4,8},{8,4},{12,0},{1,13},{5,9},{9,5},{13,1},{2,14},{6,10},... | collective-permute-start | bytes 153608 | tf_op jit(solution)/shard_map/ppermute | solution.py:1007
  (64 other events, 383.2 us)

commit v4 on v3

--- a/solution.py
+++ b/solution.py
@@ -2,6 +2,7 @@
 
 import jax
 import jax.numpy as jnp
+import numpy as np
 from jax import lax
 from jax.experimental import pallas as pl
 from jax.experimental.pallas import tpu as pltpu
@@ -23,9 +24,9 @@
 A_LOG, DT_BIAS, SKIP_WEIGHT = range(3)
 STAGES = 2
 STREAM_LIMIT = 62 * 1024 * 1024
+PIECES = 2
 BLOCKED_LIMIT = 40 * 1024 * 1024
 VMEM_LIMIT = 24 * 1024 * 1024
-UNROLL = 2
 
 f32 = jnp.float32
 bf16 = jnp.bfloat16
@@ -94,7 +95,19 @@
 
 
 def lanes(position, size):
-    return pl.ds(pl.multiple_of(position * size, size), size)
+    return slice(position * size, (position + 1) * size)
+
+
+def repeat(count, body, carry):
+    for step in range(count):
+        carry = body(step, carry)
+    return carry
+
+
+def piece_of(refs, part):
+    width = refs[0].shape[1]
+    ref = refs[part.start // width]
+    return ref[:, part.start % width : part.start % width + part.stop - part.start]
 
 
 def to_column(row, first, heads):
@@ -186,9 +199,10 @@
 
 def conv_and_state(
     x_ref, xh_ref, bc_ref, bch_ref, wx_ref, bx_ref, wb_ref, bb_ref, dtr_ref, rows_ref,
-    flags_ref, xc_ref, xp_ref, ux_ref, bcc_ref, ubc_ref, dt_ref, run_ref, keep_ref, sdev_ref,
-    sloc_ref, x_ext, bc_ext, clear, live, dt_wide, end_wide, state, *, group,
+    flags_ref, xc_ref, xp_ref, ux_ref, bcc_ref, ubc_ref, run_ref, keep_ref, sloc_ref, *refs, group,
 ):
+    sdev_refs, decay_refs = refs[:PIECES], refs[PIECES : 2 * PIECES]
+    x_ext, bc_ext, clear, live, dt_wide, end_wide, state = refs[2 * PIECES :]
     rows, channels = x_ref.shape
     heads = dtr_ref.shape[0]
     fill_extended(x_ext, xh_ref, x_ref)
@@ -196,7 +210,7 @@
     fill_live(flags_ref, clear, live)
     blocks = rows // STRETCH
     rate = jnp.exp(head_column(rows_ref, A_LOG, group, heads))
-    dt_ref[...] = step_sizes(dtr_ref, rows_ref, group)
+    dt_all = step_sizes(dtr_ref, rows_ref, group)
     product = None
     for block in range(blocks):
         first = block * STRETCH
@@ -208,7 +222,7 @@
         bcc_ref[here, :] = bc_now
         b_turned = jnp.transpose(bc_now[:, 0:NSTATE].astype(f32)).astype(bf16)
         seen = resets_seen(flags_ref[:, here])
-        dt = dt_ref[:, here]
+        dt = dt_all[:, here]
         running = dot_full(-rate * dt, upper_ones())
         run_ref[:, here] = running
         final = running[:, STRETCH - 1 : STRETCH]
@@ -235,11 +249,13 @@
                 state[:, part] = fresh
                 sloc_ref[block, :, part] = fresh.astype(bf16)
             else:
-                sdev_ref[:, part] = fresh.astype(bf16)
+                put_piece(sdev_refs, part, fresh.astype(bf16))
             return carry
 
-        lax.fori_loop(0, channels // CHUNK, chunk, 0, unroll=UNROLL)
-    keep_ref[blocks : blocks + 1, :] = product
+        repeat(channels // CHUNK, chunk, 0)
+    for place, ref in enumerate(decay_refs):
+        size = ref.shape[1]
+        ref[...] = product[:, place * size : (place + 1) * size]
 
 
 def place_runs(run_ref, here, run_wide, run_tall):
@@ -253,7 +269,7 @@
 
 def block_weights(scores, mask, run_wide, run_tall, head):
     column = run_wide[:, lanes(head, STRETCH)]
-    row = run_tall[pl.ds(pl.multiple_of(head * PAD, PAD), PAD), :][0:1]
+    row = run_tall[head * PAD : head * PAD + 1, :]
     segment = jnp.exp(column - row + mask)
     return segment, (scores * segment).astype(bf16)
 
@@ -266,6 +282,12 @@
         [jnp.where(is_first, wide, zero).astype(bf16), jnp.where(is_first, zero, wide).astype(bf16)],
         axis=0,
     )
+
+
+def put_piece(refs, part, value):
+    width = refs[0].shape[1]
+    ref = refs[part.start // width]
+    ref[:, part.start % width : part.start % width + part.stop - part.start] = value
 
 
 def slope_of(total):
@@ -294,7 +316,7 @@
             sx_ref[here, part] = slope_of(ux_ref[here, part])
             return carry
 
-        lax.fori_loop(0, channels // PAIR, pair, 0, unroll=UNROLL)
+        repeat(channels // PAIR, pair, 0)
 
 
 def start_factor(run_ref, flags_ref, here):
@@ -303,7 +325,7 @@
 
 
 def block_state(block, prior_ref, sloc_ref, keep_ref, part):
-    state = prior_ref[0][:, part] + prior_ref[1][:, part]
+    state = piece_of(prior_ref[:PIECES], part) + piece_of(prior_ref[PIECES:], part)
     if block == 0:
         return state
     whole = keep_ref[0:1, part]
@@ -320,13 +342,13 @@
 
 
 def gate_forward(
-    y_ref, early_ref, last_ref, sloc_ref, keep_ref, bcc_ref, run_ref, flags_ref, xc_ref, rows_ref,
-    z_ref, go_ref, gain_ref, *refs, group,
+    y_ref, sloc_ref, keep_ref, bcc_ref, run_ref, flags_ref, xc_ref, rows_ref, z_ref, go_ref, gain_ref,
+    *refs, group,
 ):
+    prior_ref, refs = refs[: 2 * PIECES], refs[2 * PIECES :]
     *before, bundle_ref, sums_ref, start_wide, skip_wide = refs
     rows, channels = xc_ref.shape
     heads = run_ref.shape[0]
-    prior_ref = (early_ref, last_ref)
     at_keep, at_gain, at_start, at_turned, _ = bundle_rows(rows)
     bundle_ref[at_keep:at_gain, :] = keep_ref[0:PAD, :]
     bundle_ref[at_gain:at_start, :] = jnp.broadcast_to(gain_ref[...], (PAD, channels))
@@ -358,9 +380,7 @@
             return squares + gated * gated, products + gated * gained
 
         zero = jnp.zeros((STRETCH, CHUNK), f32)
-        squares, products = lax.fori_loop(
-            0, channels // CHUNK, chunk, (zero, zero), unroll=UNROLL
-        )
+        squares, products = repeat(channels // CHUNK, chunk, (zero, zero))
         square_column = jnp.sum(squares, axis=1, keepdims=True)
         product_column = jnp.sum(products, axis=1, keepdims=True)
         shape = (STRETCH, STRETCH)
@@ -384,9 +404,9 @@
 
 
 def gate_backward(
-    own_ref, other_ref, bundle_ref, z_ref, go_ref, dy_ref, adev_ref, aloc_ref, totals_ref,
-    start_wide, adjoint, *, heads,
+    own_ref, other_ref, bundle_ref, z_ref, go_ref, dy_ref, aloc_ref, totals_ref, y_ref, *refs, heads,
 ):
+    adev_refs, (start_wide, adjoint) = refs[:PIECES], refs[PIECES:]
     rows, channels = z_ref.shape
     blocks = rows // STRETCH
     at_keep, at_gain, at_start, at_turned, end = bundle_rows(rows)
@@ -405,7 +425,9 @@
             z = z_ref[here, part].astype(f32)
             gate = z * sigmoid(z)
             gained = go_ref[here, part].astype(f32) * bundle_ref[at_gain : at_gain + 1, part]
-            mixed = bundle_ref[here, part].astype(bf16).astype(f32)
+            y_now = bundle_ref[here, part]
+            y_ref[here, part] = y_now
+            mixed = y_now.astype(bf16).astype(f32)
             d_gated = gained * inv_rms - mixed * gate * pull
             dy = (d_gated * gate).astype(bf16)
             dy_ref[here, part] = dy
@@ -417,21 +439,20 @@
                 adjoint[:, part] = fresh
                 aloc_ref[block - 1, :, part] = fresh.astype(bf16)
             else:
-                adev_ref[:, part] = fresh.astype(bf16)
+                put_piece(adev_refs, part, fresh.astype(bf16))
             return carry
 
-        lax.fori_loop(0, channels // CHUNK, chunk, 0, unroll=UNROLL)
+        repeat(channels // CHUNK, chunk, 0)
 
 
 def within_backward(
-    totals_ref, bundle_ref, z_ref, go_ref, dy_ref, xc_ref, xp_ref, bcc_ref,
-    run_ref, flags_ref, early_ref, last_ref, sloc_ref, keep_ref, rows_ref,
-    gz_ref, dxp_ref, dbc_ref, drun_ref, chan_ref, run_wide, run_tall, start_wide, skip_wide, *, group,
+    totals_ref, y_ref, z_ref, go_ref, gain_ref, dy_ref, xc_ref, xp_ref, bcc_ref,
+    run_ref, flags_ref, sloc_ref, keep_ref, rows_ref, *refs, group,
 ):
+    prior_ref, refs = refs[: 2 * PIECES], refs[2 * PIECES :]
+    gz_ref, dxp_ref, dbc_ref, drun_ref, chan_ref, run_wide, run_tall, start_wide, skip_wide = refs
     rows, channels = xc_ref.shape
     heads = run_ref.shape[0]
-    prior_ref = (early_ref, last_ref)
-    at_gain = bundle_rows(rows)[1]
     skip_wide[0:1, :] = over_channels(head_column(rows_ref, SKIP_WEIGHT, group, heads))
     chan_ref[...] = jnp.zeros_like(chan_ref)
     for block in range(rows // STRETCH):
@@ -452,11 +473,11 @@
             gate = z * gate_up
             go = go_ref[here, part].astype(f32)
             xc = xc_ref[here, part].astype(f32)
-            y_now = bundle_ref[here, part]
+            y_now = y_ref[here, part]
             y_ssd = y_now - skip_wide[0:1, part] * xc
             mixed = y_now.astype(bf16).astype(f32)
             gated = mixed * gate
-            d_gated = go * bundle_ref[at_gain : at_gain + 1, part] * inv_rms - gated * pull
+            d_gated = go * gain_ref[0:1, part] * inv_rms - gated * pull
             slope = gate_up + gate * (1.0 - gate_up)
             gz_ref[here, part] = (d_gated * mixed * slope).astype(bf16)
             dy = dy_ref[here, part].astype(f32)
@@ -467,12 +488,10 @@
             state = block_state(block, prior_ref, sloc_ref, keep_ref, part)
             return d_c + dot(started, state, ((1,), (1,))), d_run
 
-        d_c, d_run = lax.fori_loop(
-            0,
+        d_c, d_run = repeat(
             channels // CHUNK,
             chunk,
             (jnp.zeros((STRETCH, NSTATE), f32), jnp.zeros((heads, STRETCH), f32)),
-            unroll=UNROLL,
         )
         drun_ref[:, here] = d_run
 
@@ -489,9 +508,7 @@
                 d_scores + d_weights[:, 0:STRETCH] * s_first + d_weights[:, STRETCH:] * s_second
             )
 
-        d_scores = lax.fori_loop(
-            0, channels // PAIR, pair, jnp.zeros((STRETCH, STRETCH), f32), unroll=UNROLL
-        ).astype(bf16)
+        d_scores = repeat(channels // PAIR, pair, jnp.zeros((STRETCH, STRETCH), f32)).astype(bf16)
         dbc_ref[here, 0:NSTATE] = dot(d_scores, c_now, ((0,), (0,)))
         dbc_ref[here, NSTATE:] = d_c + dot(d_scores, b_now)
 
@@ -532,16 +549,16 @@
 
 
 def finish_backward(
-    later_early, later_last, aloc_ref, early_ref, last_ref, sloc_ref, keep_ref, dxp_ref, dbc_ref,
-    drun_ref, xp_ref, dy_ref, bcc_ref, run_ref, dt_ref, flags_ref, sx_ref, sbc_ref,
-    x_ref, xh_ref, bc_ref, bch_ref, wx_ref, wb_ref, rows_ref, dtr_ref, chan_ref,
-    gx_ref, xtail_ref, xpack_ref, gbc_ref, bctail_ref, bcpack_ref, gdt_ref,
-    clear, live, dx_ext, dbc_ext, d_x, d_bc, dt_wide, end_wide, ends, skip_wide, *, group,
+    aloc_ref, sloc_ref, keep_ref, dxp_ref, dbc_ref, drun_ref, xp_ref, dy_ref, bcc_ref, run_ref,
+    flags_ref, sx_ref, sbc_ref, x_ref, xh_ref, bc_ref, bch_ref, wx_ref, wb_ref, rows_ref, dtr_ref,
+    chan_ref, *refs, group,
 ):
+    later_refs, prior_ref, refs = refs[: 2 * PIECES], refs[2 * PIECES : 4 * PIECES], refs[4 * PIECES :]
+    gx_ref, xtail_ref, xpack_ref, gbc_ref, bctail_ref, bcpack_ref, gdt_ref, *refs = refs
+    clear, live, dx_ext, dbc_ext, d_x, d_bc, dt_wide, end_wide, ends, skip_wide = refs
     rows, channels = xp_ref.shape
     heads = run_ref.shape[0]
     blocks = rows // STRETCH
-    prior_ref = (early_ref, last_ref)
     fill_live(flags_ref, clear, live)
     live[:, PAD + rows :, :] = jnp.zeros((HALO, PAD, STRETCH), f32)
     live[:, 0:PAD, :] = jnp.zeros((HALO, PAD, STRETCH), f32)
@@ -551,13 +568,14 @@
     skip_wide[0:1, :] = over_channels(head_column(rows_ref, SKIP_WEIGHT, group, heads))
     rate = jnp.exp(head_column(rows_ref, A_LOG, group, heads))
     dt_bias = head_column(rows_ref, DT_BIAS, group, heads)
+    dt_all = step_sizes(dtr_ref, rows_ref, group)
     d_alog = jnp.zeros((heads, 1), f32)
     d_dtb = jnp.zeros((heads, 1), f32)
     for block in range(blocks):
         here = slice(block * STRETCH, (block + 1) * STRETCH)
         seen = resets_seen(flags_ref[:, here])
         running = run_ref[:, here]
-        dt = dt_ref[:, here]
+        dt = dt_all[:, here]
         dt_wide[...] = spread_heads(dt, HEAD_DIM)
         end_wide[...] = spread_heads(to_end_factor(running, seen), HEAD_DIM)
         b_now = bcc_ref[here, 0:NSTATE]
@@ -565,7 +583,7 @@
         def chunk(step, carry):
             d_b, per_step = carry
             part = lanes(step, CHUNK)
-            later = later_early[:, part] + later_last[:, part]
+            later = piece_of(later_refs[:PIECES], part) + piece_of(later_refs[PIECES:], part)
             if block < blocks - 1:
                 whole = keep_ref[block + 1 : block + 2, part]
                 for place in range(block + 2, blocks):
@@ -590,12 +608,10 @@
                 per_step + head_sums(stepped * d_stepped, step * CHUNK, heads),
             )
 
-        d_b, per_step = lax.fori_loop(
-            0,
+        d_b, per_step = repeat(
             channels // CHUNK,
             chunk,
             (jnp.zeros((STRETCH, NSTATE), f32), jnp.zeros((heads, STRETCH), f32)),
-            unroll=UNROLL,
         )
         d_bc[here, 0:NSTATE] = dbc_ref[here, 0:NSTATE] + d_b
         d_bc[here, NSTATE:] = dbc_ref[here, NSTATE:]
@@ -625,7 +641,7 @@
         )
         return carry
 
-    lax.fori_loop(0, channels // STRETCH, conv_chunk, 0, unroll=UNROLL)
+    repeat(channels // STRETCH, conv_chunk, 0)
     for step in range(2):
         conv_backward(
             dbc_ext, live, wb_ref, sbc_ref, d_bc, bc_ref, bch_ref, gbc_ref, bctail_ref, bcpack_ref,
@@ -633,22 +649,48 @@
         )
 
 
+def pack(*refs):
+    *pieces, out_ref = refs
+    at = 0
+    for ref in pieces:
+        size = ref.shape[1]
+        out_ref[0 : BACK + 1, at : at + size] = ref[0 : BACK + 1, :]
+        at += size
+    whole = jnp.concatenate([ref[BACK + 1 : PACKED, :] for ref in pieces], axis=1)
+    short = out_ref.shape[1] - at
+    for row in range(PAD):
+        first = row % (PAD // 2) * short
+        out_ref[row : row + 1, at:] = whole[row // (PAD // 2) :][0:1, first : first + short]
+
+
+def unpack_back(value, length):
+    short = value.shape[1] - length
+    rows = [value[BACK : BACK + 1, 0:length]]
+    for half in range(2):
+        pieces = [value[half * (PAD // 2) + turn :][0:1, length:] for turn in range(PAD // 2)]
+        rows.append(jnp.concatenate(pieces, axis=1))
+    return jnp.concatenate(rows, axis=0)
+
+
 def final_sums(mine_ref, pick_ref, flags_ref, *refs, arrivals, groups, scale):
-    arrived, tails_x, tails_bc = refs[:arrivals], refs[arrivals], refs[arrivals + 1]
-    out_wx, out_bx, out_wb, out_bb, out_alog, out_dtb, out_skip, out_gain, ending_ref = refs[
-        arrivals + 2 :
-    ]
-    inner = tails_x.shape[1]
-    total = mine_ref[0:BACK, :]
-    back = jnp.zeros((HALO, total.shape[1]), f32)
+    arrived, refs = refs[:arrivals], refs[arrivals:]
+    tails_x, tails_bc, refs = refs[:groups], refs[groups : 2 * groups], refs[2 * groups :]
+    out_wx, out_bx, out_wb, out_bb, out_alog, out_dtb, out_skip, out_gain, ending_ref = refs
+    inner = out_wx.shape[1]
+    length = ending_ref.shape[1]
+    total = mine_ref[0:BACK, 0:length]
+    back = jnp.zeros((HALO, length), f32)
     for place, ref in enumerate(arrived):
         value = ref[...].astype(f32)
-        total = total + value[0:BACK]
-        back = back + value[BACK:PACKED] * pick_ref[place : place + 1, 0:1]
+        total = total + value[0:BACK, 0:length]
+        back = back + unpack_back(value, length) * pick_ref[place : place + 1, 0:1]
     total = total * scale
     back = back * tail_factors(flags_ref)
-    ending_ref[:, 0:inner] = (tails_x[...] + back[:, 0:inner]).astype(bf16)
-    ending_ref[:, inner:] = (tails_bc[...] + back[:, inner:]).astype(bf16)
+    at = 0
+    for ref in tails_x + tails_bc:
+        size = ref.shape[1]
+        ending_ref[:, at : at + size] = (ref[...] + back[:, at : at + size]).astype(bf16)
+        at += size
     out_wx[...] = total[0:CONV, 0:inner]
     out_bx[...] = total[CONV : CONV + 1, 0:inner]
     for which in range(2):
@@ -777,14 +819,17 @@
         leaving = list(parts)
         if hop > 0:
             for place, part in enumerate(parts):
+                if place:
+                    last[place] = together(last[place], leaving[place - 1])[0]
                 early[place] = early[place] + last[place] if hop > 1 else last[place]
                 arrived = early[place].astype(f32)
                 leaving[place] = (decays[place] * arrived + part.astype(f32)).astype(bf16)
-        if hop < len(fillers):
-            work, array = fillers[hop]
+        filler = fillers[hop - 1] if 0 < hop <= len(fillers) else None
+        if filler:
+            work, array = filler
             array = together(array, *leaving)[0]
         last = [lax.ppermute(each, axis, pairs) for each in leaving]
-        if hop < len(fillers):
+        if filler:
             done = work(array)
             last[0], *done = together(last[0], *done)
             results.append(done)
@@ -854,30 +899,39 @@
     def whole(array):
         return (array, None)
 
-    keep_rows = -(-(blocks + 1) // PAD) * PAD
+    keep_rows = -(-blocks // PAD) * PAD
     tall, thin, row_shape = (rows, channels), (rows, width), (heads, rows)
     state_shape = (NSTATE, channels)
+    piece_shape = (NSTATE, channels // PIECES)
     local_shape = (blocks - 1, NSTATE, channels)
     clear_shape, live_shape = (rows + PAD, STRETCH), (HALO, rows + 2 * PAD, STRETCH)
     wide_scratch = (STRETCH, channels)
     run_scratch = [(STRETCH, heads * STRETCH), (heads * PAD, STRETCH)]
     work = rows * channels * STRETCH
     group_range = range(groups)
+    here = lax.axis_index("ctx")
+    picks = [(here ^ shift) == here + 1 for shift in range(1, count)]
+    pick = jnp.broadcast_to(jnp.stack(picks).astype(f32)[:, None], (count - 1, STRETCH))
+    flags, pick = together(flags, pick)
     held = []
+    flags_now = flags
     for g in group_range:
+        if held:
+            flags_now = together(flags, held[-1][-1])[0]
         held.append(
             call(
                 functools.partial(conv_and_state, group=g),
                 [
                     wide(x_own, g), wide(halo, g), narrow(bc_own, g), narrow(halo, g, inner),
                     wide(conv_x_weight, g), wide(bx, g), narrow(wb, g), narrow(bb, g),
-                    per_head(dt_own, g), whole(head_rows), whole(flags),
+                    per_head(dt_own, g), whole(head_rows), whole(flags_now),
                 ],
                 [
                     (tall, bf16), (tall, bf16), (tall, f32), (thin, bf16), (thin, f32),
-                    (row_shape, f32), (row_shape, f32), ((keep_rows, channels), f32),
-                    (state_shape, bf16), (local_shape, bf16),
-                ],
+                    (row_shape, f32), ((keep_rows, channels), f32), (local_shape, bf16),
+                ]
+                + [(piece_shape, bf16)] * PIECES
+                + [((1, channels // PIECES), f32)] * PIECES,
                 [
                     (rows + PAD, channels), (rows + PAD, width), clear_shape, live_shape,
                     wide_scratch, wide_scratch, state_shape,
@@ -886,8 +940,18 @@
                 "conv_and_state",
             )
         )
-    xc, xp, ux, bcc, ubc, dt, run, keep, s_dev, s_loc = zip(*held)
-    decay = [k[blocks : blocks + 1] for k in keep]
+    xc, xp, ux, bcc, ubc, run, keep, s_loc, *pieces = zip(*held)
+    s_dev, decay = pieces[:PIECES], pieces[PIECES:]
+
+    def in_a_row(pieces):
+        return [piece[g] for g in group_range for piece in pieces]
+
+    def by_pieces(pairs):
+        return [
+            [pair[term] for term in range(2) for pair in pairs[g * PIECES : (g + 1) * PIECES]]
+            for g in group_range
+        ]
+
 
     def forward_work(g):
         return lambda bcc_now: call(
@@ -902,18 +966,20 @@
         )
 
     prior, held = chain(
-        s_dev, decay, "ctx", False, [(forward_work(g), bcc[g]) for g in group_range]
+        in_a_row(s_dev), in_a_row(decay), "ctx", False, [(forward_work(g), bcc[g]) for g in group_range]
     )
+    prior = by_pieces(prior)
     y_within, slope_x, slope_bc = zip(*held)
     held, sums = [], ()
     for g in group_range:
         bundle, total = call(
             functools.partial(gate_forward, group=g),
             [
-                whole(y_within[g]), whole(prior[g][0]), whole(prior[g][1]), whole(s_loc[g]),
-                whole(keep[g]), whole(bcc[g]), whole(run[g]), whole(flags), whole(xc[g]),
-                whole(head_rows), wide(z_own, g), wide(go_own, g), wide(gain, g),
+                whole(y_within[g]), whole(s_loc[g]), whole(keep[g]), whole(bcc[g]), whole(run[g]),
+                whole(flags), whole(xc[g]), whole(head_rows), wide(z_own, g), wide(go_own, g),
+                wide(gain, g),
             ]
+            + [whole(each) for each in prior[g]]
             + [whole(each) for each in sums],
             [((bundle_rows(rows)[-1], channels), f32), ((2, rows), f32)],
             [wide_scratch, (PAD, channels)],
@@ -924,28 +990,31 @@
         held.append(bundle)
     bundle = held
     own, other = exchange_terms(sums[0], "head")
-    held = [
-        call(
-            functools.partial(gate_backward, heads=heads),
-            [whole(own), whole(other), whole(bundle[g]), wide(z_own, g), wide(go_own, g)],
-            [(tall, bf16), (state_shape, bf16), (local_shape, bf16), ((2, rows), f32)],
-            [wide_scratch, state_shape],
-            2 * work,
-            "gate_backward",
-        )
-        for g in group_range
-    ]
-    dy, a_dev, a_loc, totals = zip(*held)
+    held = []
+    for g in group_range:
+        bundle_now = together(bundle[g], held[-1][-1])[0] if held else bundle[g]
+        held.append(
+            call(
+                functools.partial(gate_backward, heads=heads),
+                [whole(own), whole(other), whole(bundle_now), wide(z_own, g), wide(go_own, g)],
+                [(tall, bf16), (local_shape, bf16), ((2, rows), f32), (tall, f32)]
+                + [(piece_shape, bf16)] * PIECES,
+                [wide_scratch, state_shape],
+                2 * work,
+                "gate_backward",
+            )
+        )
+    dy, a_loc, totals, y_all, *a_dev = zip(*held)
 
     def backward_work(g):
         return lambda bcc_now: call(
             functools.partial(within_backward, group=g),
             [
-                whole(totals[g]), whole(bundle[g]), wide(z_own, g), wide(go_own, g),
+                whole(totals[g]), whole(y_all[g]), wide(z_own, g), wide(go_own, g), wide(gain, g),
                 whole(dy[g]), whole(xc[g]), whole(xp[g]), whole(bcc_now),
-                whole(run[g]), whole(flags), whole(prior[g][0]), whole(prior[g][1]), whole(s_loc[g]),
-                whole(keep[g]), whole(head_rows),
-            ],
+                whole(run[g]), whole(flags), whole(s_loc[g]), whole(keep[g]), whole(head_rows),
+            ]
+            + [whole(each) for each in prior[g]],
             [
                 (tall, bf16), (tall, f32), (thin, f32), (row_shape, f32), ((PAD, channels), f32),
             ],
@@ -956,20 +1025,23 @@
         )
 
     later, held = chain(
-        a_dev, decay, "ctx", True, [(backward_work(g), bcc[g]) for g in group_range]
+        in_a_row(a_dev), in_a_row(decay), "ctx", True, [(backward_work(g), bcc[g]) for g in group_range]
     )
+    later = by_pieces(later)
     gz, dxp, dbc, drun, chan = zip(*held)
-    held = [
-        call(
+    held = []
+    for g in group_range:
+        rows_now = together(head_rows, held[-1][-1])[0] if held else head_rows
+        held.append(call(
             functools.partial(finish_backward, group=g),
             [
-                whole(later[g][0]), whole(later[g][1]), whole(a_loc[g]), whole(prior[g][0]),
-                whole(prior[g][1]), whole(s_loc[g]), whole(keep[g]), whole(dxp[g]), whole(dbc[g]),
+                whole(a_loc[g]), whole(s_loc[g]), whole(keep[g]), whole(dxp[g]), whole(dbc[g]),
                 whole(drun[g]), whole(xp[g]), whole(dy[g]), whole(bcc[g]), whole(run[g]),
-                whole(dt[g]), whole(flags), whole(slope_x[g]), whole(slope_bc[g]), wide(x_own, g),
+                whole(flags), whole(slope_x[g]), whole(slope_bc[g]), wide(x_own, g),
                 wide(halo, g), narrow(bc_own, g), narrow(halo, g, inner), wide(conv_x_weight, g),
-                narrow(wb, g), whole(head_rows), per_head(dt_own, g), whole(chan[g]),
-            ],
+                narrow(wb, g), whole(rows_now), per_head(dt_own, g), whole(chan[g]),
+            ]
+            + [whole(each) for each in later[g] + prior[g]],
             [
                 (tall, bf16), ((HALO, channels), f32), ((PACKED, channels), f32), (thin, bf16),
                 ((HALO, width), f32), ((PACKED, width), f32), (row_shape, f32),
@@ -981,9 +1053,7 @@
             4 * work,
             "finish_backward",
             BLOCKED_LIMIT,
-        )
-        for g in group_range
-    ]
+        ))
     gx, x_tail, x_pack, gbc, bc_tail, bc_pack, gdt = zip(*held)
 
     def joined(pieces):
@@ -994,19 +1064,28 @@
         split = value.reshape(lead + (groups, 2, NSTATE))
         return jnp.moveaxis(split, -3, -2).reshape(lead + (2, groups * NSTATE))
 
-    packed = joined(x_pack + bc_pack)
+    length = inner + groups * width
+    packed = call(
+        pack,
+        [whole(each) for each in x_pack + bc_pack],
+        [((PAD, length + 2 * length // PAD), f32)],
+        [],
+        rows,
+        "pack",
+    )[0]
     mine = packed
+    own_rows = np.ones((PAD, packed.shape[1]), np.float32)
+    own_rows[BACK:] = 0.0
+    own_rows[:, length:] = 0.0
     for shift in range(1, lax.axis_size("dp")):
         size = lax.axis_size("dp")
         other = lax.ppermute(packed, "dp", [(i, (i + shift) % size) for i in range(size)])
-        mine = jnp.where(jnp.arange(PACKED)[:, None] < BACK, mine + other, mine)
+        mine = mine + other * own_rows
     leaving = mine.astype(bf16)
-    here = lax.axis_index("ctx")
-    arrived, picks = [], []
-    for shift in range(1, count):
-        arrived.append(lax.ppermute(leaving, "ctx", [(i, i ^ shift) for i in range(count)]))
-        picks.append((here ^ shift) == here + 1)
-    pick = jnp.broadcast_to(jnp.stack(picks).astype(f32)[:, None], (count - 1, STRETCH))
+    arrived = [
+        lax.ppermute(leaving, "ctx", [(i, i ^ shift) for i in range(count)])
+        for shift in range(1, count)
+    ]
     out_wx, out_bx, out_wb, out_bb, out_alog, out_dtb, out_skip, out_gain, ending = call(
         functools.partial(
             final_sums,
@@ -1016,7 +1095,7 @@
         ),
         [whole(mine), whole(pick), whole(flags)]
         + [whole(each) for each in arrived]
-        + [whole(joined(x_tail)), whole(joined(bc_tail))],
+        + [whole(each) for each in x_tail + bc_tail],
         [
             ((CONV, inner), f32), ((1, inner), f32), ((CONV, 2, groups * NSTATE), f32),
             ((2, groups * NSTATE), f32),

time: 113 us -> 96.7 us (0.86)
  Pallas kernels: 49 us -> 33 us
  starting transfers between devices: 26.5 us -> 36.8 us
  local copies, waits for them, and re-layouts: 5.99 us -> 1.56 us
  waiting for transfers between devices: 24.8 us -> 20.6 us
  other arithmetic: 4.02 us -> 2.78 us
    pallas_call x14 -> x15, Pallas kernels: 49 us -> 33 us  [call(): pl.pallas_call(kernel if blocked else body, in_specs=in_specs, out_specs=...]
    ppermute x12 -> x24, starting transfers between devices: 14 us -> 24.2 us  [chain(): last = [lax.ppermute(each, axis, pairs) for each in leaving]]
    unnamed x141 -> x34, local copies, waits for them, and re-layouts: 5.46 us -> 1.04 us
    ppermute x12 -> x24, waiting for transfers between devices: 12.6 us -> 10.2 us  [chain(): last = [lax.ppermute(each, axis, pairs) for each in leaving]]
  transfers between devices with their start and end apart: 19 -> 31, of which waited for: 8 -> 11; matrix products, arithmetic and copies ran while one was open for 3% -> 3% of each run, Pallas kernels for 28% -> 21%
where the time goes in v4:
time: 96.7 us; the launch traced here: 96.2 us
  starting transfers between devices  36.8 us (38%)
  Pallas kernels  33 us (34%)
  waiting for transfers between devices  20.6 us (21%)
  other arithmetic  2.78 us (3%)
  local copies, waits for them, and re-layouts  1.56 us (2%)
  between operations  1.45 us (1%)
    pallas_call x15, Pallas kernels, call(): pl.pallas_call(kernel if blocked else body, in_specs=in_specs, out_specs=...  33 us
    ppermute x24, starting transfers between devices, chain(): last = [lax.ppermute(each, axis, pairs) for each in leaving]  24.2 us
    ppermute x24, waiting for transfers between devices, chain(): last = [lax.ppermute(each, axis, pairs) for each in leaving]  10.2 us
    ppermute x1, starting transfers between devices, per_device(): halo = lax.ppermute(sent, 'ctx', [(i, i + 1) for i in range(count - 1)])  4.93 us
    ppermute x3, starting transfers between devices, per_device(): lax.ppermute(leaving, 'ctx', [(i, i ^ shift) for i in range(count)])  4.58 us
    ppermute x3, waiting for transfers between devices, per_device(): lax.ppermute(leaving, 'ctx', [(i, i ^ shift) for i in range(count)])  4.46 us
    ppermute x2, waiting for transfers between devices, exchange_terms(): other = lax.ppermute(value, axis, [(i, i ^ stride) for i in range(count)])  4.16 us
    ppermute x2, starting transfers between devices, exchange_terms(): other = lax.ppermute(value, axis, [(i, i ^ stride) for i in range(count)])  3.05 us
  transfers between devices with their start and end apart: 31, of which 11 were waited for; matrix products, arithmetic and copies ran while one was open for 3% of the time, Pallas kernels for 21%

profile of v4, /device:TPU:0, one launch (start us, length us, event | category | flops | bytes accessed | tf_op | source)
XLA Modules:
  0.0 96.2 jit_solution(8796269676230011561)
XLA Ops:
  0.8 1.8 %tails.1 = f32[3,2560]{1,0:T(4,128)} custom-call(bf16[1,256,2048]{2,1,0:T(8,128)(2,1)} %refs_0_.1, bf16[1,256,2,256]{3,2,1,0:T(2,128)(2,1)} %refs_1_.1, s32[1,256]{1,0:T(1,128)} %refs_2_.2), custom_call_target="tpu_custom_call" | custom-call | flops 256 | bytes 1342464 | tf_op jit(solution)/shard_map/tails/pallas_call | solution.py:795
  2.5 4.9 %collective-permute-start = (f32[3,2560]{1,0:T(4,128)}, f32[3,2560]{1,0:T(4,128)S(1)}, u32[]{:S(2)}, u32[]{:S(2)}) collective-permute-start(f32[3,2560]{1,0:T(4,128)} %tails.1), channel_id=1, source_target_pairs={{0,4},{4,8},{8,12},{1,5},{5,9},{9,13},{2,6},{6,10},{10,14},{3,7},{... | collective-permute-start | bytes 92168 | tf_op jit(solution)/shard_map/ppermute | solution.py:884
  7.8 1.6 %collective-permute-done.refs_1_.refs_3_.xh_ref.bch_ref = f32[3,2560]{1,0:T(4,128)S(1)} collective-permute-done((f32[3,2560]{1,0:T(4,128)}, f32[3,2560]{1,0:T(4,128)S(1)}, u32[]{:S(2)}, u32[]{:S(2)}) %collective-permute-start) | collective-permute-done | bytes 30752 | tf_op jit(solution)/shard_map/ppermute | solution.py:884
  9.5 2.7 %conv_and_state.2 = (bf16[256,1024]{1,0:T(8,128)(2,1)S(1)}, bf16[256,1024]{1,0:T(8,128)(2,1)S(1)}, f32[256,1024]{1,0:T(8,128)S(1)}, bf16[256,256]{1,0:T(8,128)(2...) custom-call(bf16[256,2048]{1,0:T(8,128)(2,1)S(1)} %bitcast.59, ...), custom_call_target="tpu_custom_call" | custom-call | flops 67108864 | bytes 4512768 | tf_op jit(solution)/shard_map/conv_and_state/pallas_call | solution.py:795
  12.2 4.1 %collective-permute-start.1 = (bf16[128,512]{1,0:T(8,128)(2,1)S(1)}, bf16[128,512]{1,0:T(8,128)(2,1)S(1)}, u32[]{:S(2)}, u32[]{:S(2)}) collective-permute-start(bf16[128,512]{1,0:T(8,128)(2,1)S(1)} %get-tuple-element.134), channel_id=1, source_target_pairs={{0,4},{1,5},{2,6},{3,7},{16,20},{17,21},{18,22},{19,23}} | collective-permute-start | bytes 393224 | tf_op jit(solution)/shard_map/ppermute | solution.py:831
  16.3 1.3 %collective-permute-start.3 = (bf16[128,512]{1,0:T(8,128)(2,1)S(1)}, bf16[128,512]{1,0:T(8,128)(2,1)S(1)}, u32[]{:S(2)}, u32[]{:S(2)}) collective-permute-start(bf16[128,512]{1,0:T(8,128)(2,1)S(1)} %get-tuple-element.138), channel_id=1, source_target_pairs={{0,4},{1,5},{2,6},{3,7},{16,20},{17,21},{18,22},{19,23}} | collective-permute-start | bytes 393224 | tf_op jit(solution)/shard_map/ppermute | solution.py:831
  17.6 2.6 %conv_and_state.3 = (bf16[256,1024]{1,0:T(8,128)(2,1)S(1)}, bf16[256,1024]{1,0:T(8,128)(2,1)S(1)}, f32[256,1024]{1,0:T(8,128)S(1)}, bf16[256,256]{1,0:T(8,128)(2...) custom-call(bf16[256,2048]{1,0:T(8,128)(2,1)S(1)} %bitcast.60, ...), custom_call_target="tpu_custom_call" | custom-call | flops 67108864 | bytes 4512768 | tf_op jit(solution)/shard_map/conv_and_state/pallas_call | solution.py:795
  20.2 1.3 %collective-permute-start.4 = (bf16[128,512]{1,0:T(8,128)(2,1)S(1)}, bf16[128,512]{1,0:T(8,128)(2,1)S(1)}, u32[]{:S(2)}, u32[]{:S(2)}) collective-permute-start(bf16[128,512]{1,0:T(8,128)(2,1)S(1)} %get-tuple-element.142), channel_id=1, source_target_pairs={{0,4},{1,5},{2,6},{3,7},{16,20},{17,21},{18,22},{19,23}} | collective-permute-start | bytes 393224 | tf_op jit(solution)/shard_map/ppermute | solution.py:831
  27.0 1.4 %within_blocks.2 = (f32[256,1024]{1,0:T(8,128)S(1)}, f32[256,1024]{1,0:T(8,128)S(1)}, f32[256,256]{1,0:T(8,128)S(1)}) custom-call(bf16[256,1024]{1,0:T(8,128)(2,1)S(1)} %get-tuple-element.135.refs_0_.xp_ref, bf16[256,256]{1,0:T(8,128)(2,1)S(1)} %get-tuple-element.192.refs_1_.refs_3_.bcc_ref, f32[16,256]{1,0:T(8,128)S(1)} %get-tuple-element.148.refs_2_.refs_4_.run_ref, ...), custom_call_target="tpu_custom_call" | custom-call | flops 201326592 | bytes 4342784 | tf_op jit(solution)/shard_map/within_blocks/pallas_call | solution.py:795
  31.7 1.4 %within_blocks.3 = (f32[256,1024]{1,0:T(8,128)S(1)}, f32[256,1024]{1,0:T(8,128)S(1)}, f32[256,256]{1,0:T(8,128)S(1)}) custom-call(bf16[256,1024]{1,0:T(8,128)(2,1)S(1)} %get-tuple-element.155.refs_0_.xp_ref, bf16[256,256]{1,0:T(8,128)(2,1)S(1)} %get-tuple-element.211.refs_1_.refs_3_.bcc_ref, f32[16,256]{1,0:T(8,128)S(1)} %get-tuple-element.161.refs_2_.refs_4_.run_ref, ...), custom_call_target="tpu_custom_call" | custom-call | flops 201326592 | bytes 4342784 | tf_op jit(solution)/shard_map/within_blocks/pallas_call | solution.py:795
  33.1 1.5 %gate_forward.2 = (f32[320,1024]{1,0:T(8,128)S(1)}, f32[2,256]{1,0:T(2,128)S(1)}) custom-call(f32[256,1024]{1,0:T(8,128)S(1)} %get-tuple-element.171.refs_0_, bf16[1,128,1024]{2,1,0:T(8,128)(2,1)S(1)} %get-tuple-element.172.refs_1_.sloc_ref, f32[8,1024]{1,0:T(8,128)S(1)} %get-tuple-element.173.refs_2_.keep_ref, ...), custom_call_target="tpu_custom_call" | custom-call | flops 67108864 | bytes 5962752 | tf_op jit(solution)/shard_map/gate_forward/pallas_call | solution.py:795
  34.7 1.6 %gate_forward.3 = (f32[320,1024]{1,0:T(8,128)S(1)}, f32[2,256]{1,0:T(2,128)S(1)}) custom-call(f32[256,1024]{1,0:T(8,128)S(1)} %get-tuple-element.167.refs_0_, bf16[1,128,1024]{2,1,0:T(8,128)(2,1)S(1)} %get-tuple-element.168.refs_1_.sloc_ref, f32[8,1024]{1,0:T(8,128)S(1)} %get-tuple-element.169.refs_2_.keep_ref, ...), custom_call_target="tpu_custom_call" | custom-call | flops 67108864 | bytes 5964800 | tf_op jit(solution)/shard_map/gate_forward/pallas_call | solution.py:795
  36.3 1.5 %collective-permute-start.13 = (f32[2,256]{1,0:T(2,128)S(1)}, f32[2,256]{1,0:T(2,128)S(1)}, u32[]{:S(2)}, u32[]{:S(2)}) collective-permute-start(f32[2,256]{1,0:T(2,128)S(1)} %get-tuple-element.177), channel_id=1, source_target_pairs={{0,1},{1,0},{2,3},{3,2},{4,5},{5,4},{6,7},{7,6},{8,9},{9,8},{10,11... | collective-permute-start | bytes 6152 | tf_op jit(solution)/shard_map/ppermute | solution.py:847
  37.8 2.1 %collective-permute-done.13 = f32[2,256]{1,0:T(2,128)S(1)} collective-permute-done((f32[2,256]{1,0:T(2,128)S(1)}, f32[2,256]{1,0:T(2,128)S(1)}, u32[]{:S(2)}, u32[]{:S(2)}) %collective-permute-start.13) | collective-permute-done | bytes 2080 | tf_op jit(solution)/shard_map/ppermute | solution.py:847
  39.9 1.5 %collective-permute-start.14 = (f32[2,256]{1,0:T(2,128)S(1)}, f32[2,256]{1,0:T(2,128)S(1)}, u32[]{:S(2)}, u32[]{:S(2)}) collective-permute-start(f32[2,256]{1,0:T(2,128)S(1)} %add.98.refs_0_), channel_id=1, source_target_pairs={{0,2},{1,3},{2,0},{3,1},{4,6},{5,7},{6,4},{7,5},{8,10},{9,11},{10,... | collective-permute-start | bytes 6152 | tf_op jit(solution)/shard_map/ppermute | solution.py:847
  41.4 2.1 %collective-permute-done.14.refs_1_ = f32[2,256]{1,0:T(2,128)S(1)} collective-permute-done((f32[2,256]{1,0:T(2,128)S(1)}, f32[2,256]{1,0:T(2,128)S(1)}, u32[]{:S(2)}, u32[]{:S(2)}) %collective-permute-start.14) | collective-permute-done | bytes 2080 | tf_op jit(solution)/shard_map/ppermute | solution.py:847
  51.4 3.4 %within_backward.2 = (bf16[256,1024]{1,0:T(8,128)(2,1)S(1)}, f32[256,1024]{1,0:T(8,128)S(1)}, f32[256,256]{1,0:T(8,128)S(1)}, f32[16,256]{1,0:T(8,128)S(1)}, f32[8,1024]{1,0:T(8,128)S(1)}) custom-call(f32[2,256]{1,0:T(2,128)S(1)} %get-tuple-element.181.totals_ref, f32[256,1024]{1,0:T(8,128)S(1)} %get-tuple-element.182.y_ref, bf16[256,2048]{1,0:T(8,128)(2,1)S(1)} %bitcast.51, ...), custom_call_target="tpu_custom_call" | custom-call | flops 335544320 | bytes 7584768 | tf_op jit(solution)/shard_map/within_backward/pallas_call | solution.py:795
  60.4 3.4 %within_backward.3 = (bf16[256,1024]{1,0:T(8,128)(2,1)S(1)}, f32[256,1024]{1,0:T(8,128)S(1)}, f32[256,256]{1,0:T(8,128)S(1)}, f32[16,256]{1,0:T(8,128)S(1)}, f32[8,1024]{1,0:T(8,128)S(1)}) custom-call(f32[2,256]{1,0:T(2,128)S(1)} %get-tuple-element.206.totals_ref, f32[256,1024]{1,0:T(8,128)S(1)} %get-tuple-element.207.y_ref, bf16[256,2048]{1,0:T(8,128)(2,1)S(1)} %bitcast.52, ...), custom_call_target="tpu_custom_call" | custom-call | flops 335544320 | bytes 7584768 | tf_op jit(solution)/shard_map/within_backward/pallas_call | solution.py:795
  63.8 7.3 %collective-permute-done.21.refs_2_ = bf16[128,512]{1,0:T(8,128)(2,1)S(1)} collective-permute-done((bf16[128,512]{1,0:T(8,128)(2,1)S(1)}, bf16[128,512]{1,0:T(8,128)(2,1)S(1)}, u32[]{:S(2)}, u32[]{:S(2)}) %collective-permute-start.21) | collective-permute-done | bytes 131104 | tf_op jit(solution)/shard_map/ppermute | solution.py:831
  71.1 1.6 %collective-permute-done.24.refs_3_ = bf16[128,512]{1,0:T(8,128)(2,1)S(1)} collective-permute-done((bf16[128,512]{1,0:T(8,128)(2,1)S(1)}, bf16[128,512]{1,0:T(8,128)(2,1)S(1)}, u32[]{:S(2)}, u32[]{:S(2)}) %collective-permute-start.24) | collective-permute-done | bytes 131104 | tf_op jit(solution)/shard_map/ppermute | solution.py:831
  72.7 5.1 %finish_backward.2 = (bf16[256,1024]{1,0:T(8,128)(2,1)S(1)}, f32[3,1024]{1,0:T(4,128)S(1)}, f32[10,1024]{1,0:T(8,128)S(1)}, bf16[256,256]{1,0:T(8,128)(2,1)S(1)}...) custom-call(bf16[1,128,1024]{2,1,0:T(8,128)(2,1)S(1)} %get-tuple-element.179.aloc_ref, ...), custom_call_target="tpu_custom_call" | custom-call | flops 134217728 | bytes 7645184 | tf_op jit(solution)/shard_map/finish_backward/pallas_call | solution.py:795
  77.8 5.1 %finish_backward.3 = (bf16[256,1024]{1,0:T(8,128)(2,1)S(1)}, f32[3,1024]{1,0:T(4,128)S(1)}, f32[10,1024]{1,0:T(8,128)S(1)}, bf16[256,256]{1,0:T(8,128)(2,1)S(1)}...) custom-call(bf16[1,128,1024]{2,1,0:T(8,128)(2,1)S(1)} %get-tuple-element.219.aloc_ref, ...), custom_call_target="tpu_custom_call" | custom-call | flops 134217728 | bytes 7645184 | tf_op jit(solution)/shard_map/finish_backward/pallas_call | solution.py:795
  85.4 3.6 %collective-permute-start.29 = (bf16[8,3200]{1,0:T(8,128)(2,1)S(1)}, bf16[8,3200]{1,0:T(8,128)(2,1)S(1)}, u32[]{:S(2)}, u32[]{:S(2)}) collective-permute-start(bf16[8,3200]{1,0:T(8,128)(2,1)S(1)} %get-tuple-element.252), channel_id=1, source_target_pairs={{0,8},{4,12},{8,0},{12,4},{1,9},{5,13},{9,1},{13,5},{2,10},{6,14},... | collective-permute-start | bytes 153608 | tf_op jit(solution)/shard_map/ppermute | solution.py:1086
  90.4 3.4 %collective-permute-done.29.refs_4_ = bf16[8,3200]{1,0:T(8,128)(2,1)S(1)} collective-permute-done((bf16[8,3200]{1,0:T(8,128)(2,1)S(1)}, bf16[8,3200]{1,0:T(8,128)(2,1)S(1)}, u32[]{:S(2)}, u32[]{:S(2)}) %collective-permute-start.29) | collective-permute-done | bytes 51232 | tf_op jit(solution)/shard_map/ppermute | solution.py:1086
  (120 shorter events, 28.3 us)
Async XLA Ops:
  2.5 6.9 %collective-permute-start = (f32[3,2560]{1,0:T(4,128)}, f32[3,2560]{1,0:T(4,128)S(1)}, u32[]{:S(2)}, u32[]{:S(2)}) collective-permute-start(f32[3,2560]{1,0:T(4,128)} %tails.1), channel_id=1, source_target_pairs={{0,4},{4,8},{8,12},{1,5},{5,9},{9,13},{2,6},{6,10},{10,14},{3,7},{... | collective-permute-start | bytes 92168 | tf_op jit(solution)/shard_map/ppermute | solution.py:884
  12.2 10.7 %collective-permute-start.1 = (bf16[128,512]{1,0:T(8,128)(2,1)S(1)}, bf16[128,512]{1,0:T(8,128)(2,1)S(1)}, u32[]{:S(2)}, u32[]{:S(2)}) collective-permute-start(bf16[128,512]{1,0:T(8,128)(2,1)S(1)} %get-tuple-element.134), channel_id=1, source_target_pairs={{0,4},{1,5},{2,6},{3,7},{16,20},{17,21},{18,22},{19,23}} | collective-permute-start | bytes 393224 | tf_op jit(solution)/shard_map/ppermute | solution.py:831
  16.3 7.3 %collective-permute-start.3 = (bf16[128,512]{1,0:T(8,128)(2,1)S(1)}, bf16[128,512]{1,0:T(8,128)(2,1)S(1)}, u32[]{:S(2)}, u32[]{:S(2)}) collective-permute-start(bf16[128,512]{1,0:T(8,128)(2,1)S(1)} %get-tuple-element.138), channel_id=1, source_target_pairs={{0,4},{1,5},{2,6},{3,7},{16,20},{17,21},{18,22},{19,23}} | collective-permute-start | bytes 393224 | tf_op jit(solution)/shard_map/ppermute | solution.py:831
  20.2 4.7 %collective-permute-start.4 = (bf16[128,512]{1,0:T(8,128)(2,1)S(1)}, bf16[128,512]{1,0:T(8,128)(2,1)S(1)}, u32[]{:S(2)}, u32[]{:S(2)}) collective-permute-start(bf16[128,512]{1,0:T(8,128)(2,1)S(1)} %get-tuple-element.142), channel_id=1, source_target_pairs={{0,4},{1,5},{2,6},{3,7},{16,20},{17,21},{18,22},{19,23}} | collective-permute-start | bytes 393224 | tf_op jit(solution)/shard_map/ppermute | solution.py:831
  21.5 4.8 %collective-permute-start.5 = (bf16[128,512]{1,0:T(8,128)(2,1)S(1)}, bf16[128,512]{1,0:T(8,128)(2,1)S(1)}, u32[]{:S(2)}, u32[]{:S(2)}) collective-permute-start(bf16[128,512]{1,0:T(8,128)(2,1)S(1)} %get-tuple-element.145), channel_id=1, source_target_pairs={{0,4},{1,5},{2,6},{3,7},{16,20},{17,21},{18,22},{19,23}} | collective-permute-start | bytes 393224 | tf_op jit(solution)/shard_map/ppermute | solution.py:831
  22.9 5.5 %collective-permute-start.2 = (bf16[128,512]{1,0:T(8,128)(2,1)S(1)}, bf16[128,512]{1,0:T(8,128)(2,1)S(1)}, u32[]{:S(2)}, u32[]{:S(2)}) collective-permute-start(bf16[128,512]{1,0:T(8,128)(2,1)S(1)} %fusion), channel_id=1, source_target_pairs={{4,8},{5,9},{6,10},{7,11},{20,24},{21,25},{22,26},{23,27}} | collective-permute-start | bytes 393224 | tf_op jit(solution)/shard_map/ppermute | solution.py:831
  23.6 5.6 %collective-permute-start.7 = (bf16[128,512]{1,0:T(8,128)(2,1)S(1)}, bf16[128,512]{1,0:T(8,128)(2,1)S(1)}, u32[]{:S(2)}, u32[]{:S(2)}) collective-permute-start(bf16[128,512]{1,0:T(8,128)(2,1)S(1)} %fusion.2), channel_id=1, source_target_pairs={{4,8},{5,9},{6,10},{7,11},{20,24},{21,25},{22,26},{23,27}} | collective-permute-start | bytes 393224 | tf_op jit(solution)/shard_map/ppermute | solution.py:831
  24.9 5.0 %collective-permute-start.8 = (bf16[128,512]{1,0:T(8,128)(2,1)S(1)}, bf16[128,512]{1,0:T(8,128)(2,1)S(1)}, u32[]{:S(2)}, u32[]{:S(2)}) collective-permute-start(bf16[128,512]{1,0:T(8,128)(2,1)S(1)} %fusion.4), channel_id=1, source_target_pairs={{4,8},{5,9},{6,10},{7,11},{20,24},{21,25},{22,26},{23,27}} | collective-permute-start | bytes 393224 | tf_op jit(solution)/shard_map/ppermute | solution.py:831
  28.5 4.6 %collective-permute-start.6 = (bf16[128,512]{1,0:T(8,128)(2,1)S(1)}, bf16[128,512]{1,0:T(8,128)(2,1)S(1)}, u32[]{:S(2)}, u32[]{:S(2)}) collective-permute-start(bf16[128,512]{1,0:T(8,128)(2,1)S(1)} %get-tuple-element.268), channel_id=1, source_target_pairs={{8,12},{9,13},{10,14},{11,15},{24,28},{25,29},{26,30},{27,31}} | collective-permute-start | bytes 393224 | tf_op jit(solution)/shard_map/ppermute | solution.py:831
  29.3 3.8 %collective-permute-start.12 = (bf16[128,512]{1,0:T(8,128)(2,1)S(1)}, bf16[128,512]{1,0:T(8,128)(2,1)S(1)}, u32[]{:S(2)}, u32[]{:S(2)}) collective-permute-start(bf16[128,512]{1,0:T(8,128)(2,1)S(1)} %get-tuple-element.266), channel_id=1, source_target_pairs={{8,12},{9,13},{10,14},{11,15},{24,28},{25,29},{26,30},{27,31}} | collective-permute-start | bytes 393224 | tf_op jit(solution)/shard_map/ppermute | solution.py:831
  30.2 4.5 %collective-permute-start.11 = (bf16[128,512]{1,0:T(8,128)(2,1)S(1)}, bf16[128,512]{1,0:T(8,128)(2,1)S(1)}, u32[]{:S(2)}, u32[]{:S(2)}) collective-permute-start(bf16[128,512]{1,0:T(8,128)(2,1)S(1)} %get-tuple-element.262), channel_id=1, source_target_pairs={{8,12},{9,13},{10,14},{11,15},{24,28},{25,29},{26,30},{27,31}} | collective-permute-start | bytes 393224 | tf_op jit(solution)/shard_map/ppermute | solution.py:831
  44.5 3.9 %collective-permute-start.15 = (bf16[128,512]{1,0:T(8,128)(2,1)S(1)}, bf16[128,512]{1,0:T(8,128)(2,1)S(1)}, u32[]{:S(2)}, u32[]{:S(2)}) collective-permute-start(bf16[128,512]{1,0:T(8,128)(2,1)S(1)} %get-tuple-element.180), channel_id=1, source_target_pairs={{12,8},{13,9},{14,10},{15,11},{28,24},{29,25},{30,26},{31,27}} | collective-permute-start | bytes 393224 | tf_op jit(solution)/shard_map/ppermute | solution.py:831
  45.2 4.0 %collective-permute-start.17 = (bf16[128,512]{1,0:T(8,128)(2,1)S(1)}, bf16[128,512]{1,0:T(8,128)(2,1)S(1)}, u32[]{:S(2)}, u32[]{:S(2)}) collective-permute-start(bf16[128,512]{1,0:T(8,128)(2,1)S(1)} %get-tuple-element.184), channel_id=1, source_target_pairs={{12,8},{13,9},{14,10},{15,11},{28,24},{29,25},{30,26},{31,27}} | collective-permute-start | bytes 393224 | tf_op jit(solution)/shard_map/ppermute | solution.py:831
  48.5 6.3 %collective-permute-start.16 = (bf16[128,512]{1,0:T(8,128)(2,1)S(1)}, bf16[128,512]{1,0:T(8,128)(2,1)S(1)}, u32[]{:S(2)}, u32[]{:S(2)}) collective-permute-start(bf16[128,512]{1,0:T(8,128)(2,1)S(1)} %fusion.8), channel_id=1, source_target_pairs={{8,4},{9,5},{10,6},{11,7},{24,20},{25,21},{26,22},{27,23}} | collective-permute-start | bytes 393224 | tf_op jit(solution)/shard_map/ppermute | solution.py:831
  49.3 7.0 %collective-permute-start.20 = (bf16[128,512]{1,0:T(8,128)(2,1)S(1)}, bf16[128,512]{1,0:T(8,128)(2,1)S(1)}, u32[]{:S(2)}, u32[]{:S(2)}) collective-permute-start(bf16[128,512]{1,0:T(8,128)(2,1)S(1)} %fusion.10), channel_id=1, source_target_pairs={{8,4},{9,5},{10,6},{11,7},{24,20},{25,21},{26,22},{27,23}} | collective-permute-start | bytes 393224 | tf_op jit(solution)/shard_map/ppermute | solution.py:831
  50.0 7.6 %collective-permute-start.22 = (bf16[128,512]{1,0:T(8,128)(2,1)S(1)}, bf16[128,512]{1,0:T(8,128)(2,1)S(1)}, u32[]{:S(2)}, u32[]{:S(2)}) collective-permute-start(bf16[128,512]{1,0:T(8,128)(2,1)S(1)} %fusion.12), channel_id=1, source_target_pairs={{8,4},{9,5},{10,6},{11,7},{24,20},{25,21},{26,22},{27,23}} | collective-permute-start | bytes 393224 | tf_op jit(solution)/shard_map/ppermute | solution.py:831
  50.7 6.9 %collective-permute-start.23 = (bf16[128,512]{1,0:T(8,128)(2,1)S(1)}, bf16[128,512]{1,0:T(8,128)(2,1)S(1)}, u32[]{:S(2)}, u32[]{:S(2)}) collective-permute-start(bf16[128,512]{1,0:T(8,128)(2,1)S(1)} %fusion.14), channel_id=1, source_target_pairs={{8,4},{9,5},{10,6},{11,7},{24,20},{25,21},{26,22},{27,23}} | collective-permute-start | bytes 393224 | tf_op jit(solution)/shard_map/ppermute | solution.py:831
  54.9 16.2 %collective-permute-start.21 = (bf16[128,512]{1,0:T(8,128)(2,1)S(1)}, bf16[128,512]{1,0:T(8,128)(2,1)S(1)}, u32[]{:S(2)}, u32[]{:S(2)}) collective-permute-start(bf16[128,512]{1,0:T(8,128)(2,1)S(1)} %get-tuple-element.260), channel_id=1, source_target_pairs={{4,0},{5,1},{6,2},{7,3},{20,16},{21,17},{22,18},{23,19}} | collective-permute-start | bytes 393224 | tf_op jit(solution)/shard_map/ppermute | solution.py:831
  56.3 16.4 %collective-permute-start.24 = (bf16[128,512]{1,0:T(8,128)(2,1)S(1)}, bf16[128,512]{1,0:T(8,128)(2,1)S(1)}, u32[]{:S(2)}, u32[]{:S(2)}) collective-permute-start(bf16[128,512]{1,0:T(8,128)(2,1)S(1)} %get-tuple-element.258), channel_id=1, source_target_pairs={{4,0},{5,1},{6,2},{7,3},{20,16},{21,17},{22,18},{23,19}} | collective-permute-start | bytes 393224 | tf_op jit(solution)/shard_map/ppermute | solution.py:831
  57.8 20.0 %collective-permute-start.26 = (bf16[128,512]{1,0:T(8,128)(2,1)S(1)}, bf16[128,512]{1,0:T(8,128)(2,1)S(1)}, u32[]{:S(2)}, u32[]{:S(2)}) collective-permute-start(bf16[128,512]{1,0:T(8,128)(2,1)S(1)} %get-tuple-element.254), channel_id=1, source_target_pairs={{4,0},{5,1},{6,2},{7,3},{20,16},{21,17},{22,18},{23,19}} | collective-permute-start | bytes 393224 | tf_op jit(solution)/shard_map/ppermute | solution.py:831
  59.1 18.7 %collective-permute-start.25 = (bf16[128,512]{1,0:T(8,128)(2,1)S(1)}, bf16[128,512]{1,0:T(8,128)(2,1)S(1)}, u32[]{:S(2)}, u32[]{:S(2)}) collective-permute-start(bf16[128,512]{1,0:T(8,128)(2,1)S(1)} %get-tuple-element.256), channel_id=1, source_target_pairs={{4,0},{5,1},{6,2},{7,3},{20,16},{21,17},{22,18},{23,19}} | collective-permute-start | bytes 393224 | tf_op jit(solution)/shard_map/ppermute | solution.py:831
  84.4 6.0 %collective-permute-start.30 = (bf16[8,3200]{1,0:T(8,128)(2,1)S(1)}, bf16[8,3200]{1,0:T(8,128)(2,1)S(1)}, u32[]{:S(2)}, u32[]{:S(2)}) collective-permute-start(bf16[8,3200]{1,0:T(8,128)(2,1)S(1)} %get-tuple-element.252), channel_id=1, source_target_pairs={{0,12},{4,8},{8,4},{12,0},{1,13},{5,9},{9,5},{13,1},{2,14},{6,10},... | collective-permute-start | bytes 153608 | tf_op jit(solution)/shard_map/ppermute | solution.py:1086
  85.4 8.4 %collective-permute-start.29 = (bf16[8,3200]{1,0:T(8,128)(2,1)S(1)}, bf16[8,3200]{1,0:T(8,128)(2,1)S(1)}, u32[]{:S(2)}, u32[]{:S(2)}) collective-permute-start(bf16[8,3200]{1,0:T(8,128)(2,1)S(1)} %get-tuple-element.252), channel_id=1, source_target_pairs={{0,8},{4,12},{8,0},{12,4},{1,9},{5,13},{9,1},{13,5},{2,10},{6,14},... | collective-permute-start | bytes 153608 | tf_op jit(solution)/shard_map/ppermute | solution.py:1086
  88.9 5.2 %collective-permute-start.28 = (bf16[8,3200]{1,0:T(8,128)(2,1)S(1)}, bf16[8,3200]{1,0:T(8,128)(2,1)S(1)}, u32[]{:S(2)}, u32[]{:S(2)}) collective-permute-start(bf16[8,3200]{1,0:T(8,128)(2,1)S(1)} %get-tuple-element.252), channel_id=1, source_target_pairs={{0,4},{4,0},{8,12},{12,8},{1,5},{5,1},{9,13},{13,9},{2,6},{6,2},{1... | collective-permute-start | bytes 153608 | tf_op jit(solution)/shard_map/ppermute | solution.py:1086
  (24 other events, 120.9 us)

commit v5 on v4

--- a/solution.py
+++ b/solution.py
@@ -61,13 +61,13 @@
     return dot(split3(rows), jnp.concatenate([pick] * 3, axis=0), ((0,), (0,)))
 
 
-def head_sums(value, first, heads):
-    shape = (heads, value.shape[1])
-    pick = ((iota(shape, 1) + first) // HEAD_DIM == iota(shape, 0)).astype(f32).astype(bf16)
+def head_sums(value, first):
+    shape = (value.shape[1], STRETCH)
+    pick = ((iota(shape, 0) + first) // HEAD_DIM == iota(shape, 1)).astype(f32).astype(bf16)
     high = value.astype(bf16)
     low = (value - high.astype(f32)).astype(bf16)
-    last = ((1,), (1,))
-    return dot(pick, high, last) + dot(pick, low, last)
+    both = dot(jnp.concatenate([high, low], axis=0), pick)
+    return both[: value.shape[0]] + both[value.shape[0] :]
 
 
 def as_columns(row):
@@ -160,20 +160,25 @@
 
 
 def fill_extended(extended, halo_ref, rows_ref):
-    extended[PAD - HALO : PAD, :] = halo_ref[...]
-    extended[PAD:, :] = rows_ref[...].astype(f32)
+    for tile in range(extended.shape[0]):
+        part = lanes(tile, STRETCH)
+        extended[tile, PAD - HALO : PAD, :] = halo_ref[:, part]
+        extended[tile, PAD:, :] = rows_ref[:, part].astype(f32)
 
 
 def conv_total(extended, live, weight_ref, bias_ref, first, part):
     begin = PAD + first
-    total = bias_ref[0:1, part] + weight_ref[0:1, part] * extended[begin : begin + STRETCH, part]
-    width = total.shape[1] // STRETCH
-    for lag in range(1, CONV):
-        mask = jnp.concatenate([live[lag - 1, begin : begin + STRETCH, :]] * width, axis=1)
-        total = total + weight_ref[lag : lag + 1, part] * (
-            extended[begin - lag : begin - lag + STRETCH, part] * mask
-        )
-    return total
+    totals = []
+    for tile in range(part.start // STRETCH, part.stop // STRETCH):
+        cut = lanes(tile, STRETCH)
+        total = bias_ref[0:1, cut] + weight_ref[0:1, cut] * extended[tile, begin : begin + STRETCH, :]
+        for lag in range(1, CONV):
+            total = total + weight_ref[lag : lag + 1, cut] * (
+                extended[tile, begin - lag : begin - lag + STRETCH, :]
+                * live[lag - 1, begin : begin + STRETCH, :]
+            )
+        totals.append(total)
+    return totals[0] if len(totals) == 1 else jnp.concatenate(totals, axis=1)
 
 
 def tail_factors(flags_ref):
@@ -215,7 +220,7 @@
     for block in range(blocks):
         first = block * STRETCH
         here = slice(first, first + STRETCH)
-        every = slice(None)
+        every = slice(0, 2 * NSTATE)
         total = conv_total(bc_ext, live, wb_ref, bb_ref, first, every)
         ubc_ref[here, :] = total
         bc_now = (total * sigmoid(total)).astype(bf16)
@@ -446,18 +451,23 @@
 
 
 def within_backward(
-    totals_ref, y_ref, z_ref, go_ref, gain_ref, dy_ref, xc_ref, xp_ref, bcc_ref,
-    run_ref, flags_ref, sloc_ref, keep_ref, rows_ref, *refs, group,
+    totals_ref, y_ref, z_ref, go_ref, gain_ref, dy_ref, xc_ref, xp_ref, bcc_ref, run_ref, flags_ref,
+    sloc_ref, keep_ref, rows_ref, sx_ref, dtr_ref, *refs, group,
 ):
     prior_ref, refs = refs[: 2 * PIECES], refs[2 * PIECES :]
-    gz_ref, dxp_ref, dbc_ref, drun_ref, chan_ref, run_wide, run_tall, start_wide, skip_wide = refs
+    gz_ref, dux_ref, dts_ref, ended_ref, dbc_ref, drun_ref, step_ref, chan_ref, *refs = refs
+    run_wide, run_tall, start_wide, skip_wide, dt_wide, end_wide = refs
     rows, channels = xc_ref.shape
     heads = run_ref.shape[0]
     skip_wide[0:1, :] = over_channels(head_column(rows_ref, SKIP_WEIGHT, group, heads))
     chan_ref[...] = jnp.zeros_like(chan_ref)
+    dt_all = step_sizes(dtr_ref, rows_ref, group)
     for block in range(rows // STRETCH):
         here = slice(block * STRETCH, (block + 1) * STRETCH)
-        mask = decay_mask(resets_seen(flags_ref[:, here]))
+        seen = resets_seen(flags_ref[:, here])
+        mask = decay_mask(seen)
+        dt_wide[...] = spread_heads(dt_all[:, here], HEAD_DIM)
+        end_wide[...] = spread_heads(to_end_factor(run_ref[:, here], seen), HEAD_DIM)
         b_now = bcc_ref[here, 0:NSTATE]
         c_now = bcc_ref[here, NSTATE:]
         scores = dot(c_now, b_now, ((1,), (1,)))
@@ -483,7 +493,7 @@
             dy = dy_ref[here, part].astype(f32)
             chan_ref[0:1, part] += jnp.sum(go * gated * inv_rms, axis=0, keepdims=True)
             chan_ref[1:2, part] += jnp.sum(dy * xc, axis=0, keepdims=True)
-            d_run = d_run + head_sums(dy * y_ssd, step * CHUNK, heads)
+            d_run = d_run + head_sums(dy * y_ssd, step * CHUNK)
             started = (dy * start_wide[:, part]).astype(bf16)
             state = block_state(block, prior_ref, sloc_ref, keep_ref, part)
             return d_c + dot(started, state, ((1,), (1,))), d_run
@@ -491,45 +501,59 @@
         d_c, d_run = repeat(
             channels // CHUNK,
             chunk,
-            (jnp.zeros((STRETCH, NSTATE), f32), jnp.zeros((heads, STRETCH), f32)),
-        )
-        drun_ref[:, here] = d_run
-
-        def pair(step, d_scores):
+            (jnp.zeros((STRETCH, NSTATE), f32), jnp.zeros((STRETCH, STRETCH), f32)),
+        )
+        drun_ref[:, here] = jnp.transpose(d_run)[0:heads]
+
+        def pair(step, carry):
+            d_scores, per_step = carry
             part = lanes(step, PAIR)
             s_first, w_first = block_weights(scores, mask, run_wide, run_tall, 2 * step)
             s_second, w_second = block_weights(scores, mask, run_wide, run_tall, 2 * step + 1)
             dy = dy_ref[here, part]
             d_weights = dot(dy, both_heads(xp_ref[here, part]), ((1,), (1,)))
-            dxp_ref[here, part] = dot(
+            d_stepped = dot(
                 jnp.concatenate([w_first, w_second], axis=0), both_heads(dy), ((0,), (0,))
             )
+            stepped = xp_ref[here, part].astype(f32)
+            ended_ref[here, part] = (stepped * end_wide[:, part]).astype(bf16)
+            slope = sx_ref[here, part]
+            scaled = dt_wide[:, part] * slope
+            dts_ref[here, part] = scaled
+            dux_ref[here, part] = d_stepped * scaled + skip_wide[0:1, part] * dy.astype(f32) * slope
             return (
-                d_scores + d_weights[:, 0:STRETCH] * s_first + d_weights[:, STRETCH:] * s_second
+                d_scores + d_weights[:, 0:STRETCH] * s_first + d_weights[:, STRETCH:] * s_second,
+                per_step + head_sums(stepped * d_stepped, step * PAIR),
             )
 
-        d_scores = repeat(channels // PAIR, pair, jnp.zeros((STRETCH, STRETCH), f32)).astype(bf16)
+        d_scores, per_step = repeat(
+            channels // PAIR,
+            pair,
+            (jnp.zeros((STRETCH, STRETCH), f32), jnp.zeros((STRETCH, STRETCH), f32)),
+        )
+        d_scores = d_scores.astype(bf16)
+        step_ref[:, here] = jnp.transpose(per_step)[0:heads]
         dbc_ref[here, 0:NSTATE] = dot(d_scores, c_now, ((0,), (0,)))
         dbc_ref[here, NSTATE:] = d_c + dot(d_scores, b_now)
 
 
-def conv_backward(d_ext, live, weight_ref, slope_ref, d_ref, x_ref, halo_ref, grad_ref, tail_ref,
-                  pack_ref, rows, part):
+def put_total(d_ext, pack_ref, first, part, d_total):
+    for tile in range(part.start // STRETCH, part.stop // STRETCH):
+        at = tile * STRETCH - part.start
+        d_ext[tile, PAD + first : PAD + first + STRETCH, :] = d_total[:, at : at + STRETCH]
+    now = jnp.sum(d_total, axis=0, keepdims=True)
+    pack_ref[CONV : CONV + 1, part] = pack_ref[CONV : CONV + 1, part] + now if first else now
+
+
+def conv_backward(d_ext, live_up, weight_ref, x_ref, halo_ref, grad_ref, tail_ref, pack_ref, rows, tile):
     sums = None
-    total = None
-    for first in range(0, rows, STRETCH):
-        here = slice(first, first + STRETCH)
-        d_total = d_ref[here, part] * slope_ref[here, part]
-        d_ext[PAD + first : PAD + first + STRETCH, part] = d_total
-        now = jnp.sum(d_total, axis=0, keepdims=True)
-        total = now if total is None else total + now
-    pack_ref[CONV : CONV + 1, part] = total
+    part = lanes(tile, STRETCH)
     for first, count in [(-PAD, PAD)] + [(at, STRETCH) for at in range(0, rows, STRETCH)]:
         begin = PAD + first
-        pieces = [d_ext[begin : begin + count, part]]
+        pieces = [d_ext[tile, begin : begin + count, :]]
         for lag in range(1, CONV):
             moved = slice(begin + lag, begin + lag + count)
-            pieces.append(d_ext[moved, part] * live[lag - 1, moved, :])
+            pieces.append(d_ext[tile, moved, :] * live_up[lag - 1, begin : begin + count, :])
         grad = weight_ref[0:1, part] * pieces[0]
         for lag in range(1, CONV):
             grad = grad + weight_ref[lag : lag + 1, part] * pieces[lag]
@@ -549,23 +573,24 @@
 
 
 def finish_backward(
-    aloc_ref, sloc_ref, keep_ref, dxp_ref, dbc_ref, drun_ref, xp_ref, dy_ref, bcc_ref, run_ref,
-    flags_ref, sx_ref, sbc_ref, x_ref, xh_ref, bc_ref, bch_ref, wx_ref, wb_ref, rows_ref, dtr_ref,
-    chan_ref, *refs, group,
+    aloc_ref, sloc_ref, keep_ref, dux_ref, dts_ref, ended_ref, dbc_ref, drun_ref, step_ref, xp_ref,
+    bcc_ref, run_ref, flags_ref, sbc_ref, x_ref, xh_ref, bc_ref, bch_ref, wx_ref, wb_ref, rows_ref,
+    dtr_ref, chan_ref, *refs, group,
 ):
     later_refs, prior_ref, refs = refs[: 2 * PIECES], refs[2 * PIECES : 4 * PIECES], refs[4 * PIECES :]
     gx_ref, xtail_ref, xpack_ref, gbc_ref, bctail_ref, bcpack_ref, gdt_ref, *refs = refs
-    clear, live, dx_ext, dbc_ext, d_x, d_bc, dt_wide, end_wide, ends, skip_wide = refs
+    clear, live, live_up, dx_ext, dbc_ext, end_wide, ends = refs
     rows, channels = xp_ref.shape
     heads = run_ref.shape[0]
     blocks = rows // STRETCH
     fill_live(flags_ref, clear, live)
     live[:, PAD + rows :, :] = jnp.zeros((HALO, PAD, STRETCH), f32)
     live[:, 0:PAD, :] = jnp.zeros((HALO, PAD, STRETCH), f32)
+    for lag in range(1, CONV):
+        live_up[lag - 1] = live[lag - 1, lag : lag + rows + PAD, :]
     for ext in (dx_ext, dbc_ext):
-        ext[0:PAD, :] = jnp.zeros((PAD, ext.shape[1]), f32)
-        ext[PAD + rows :, :] = jnp.zeros((PAD, ext.shape[1]), f32)
-    skip_wide[0:1, :] = over_channels(head_column(rows_ref, SKIP_WEIGHT, group, heads))
+        ext[:, 0:PAD, :] = jnp.zeros((ext.shape[0], PAD, STRETCH), f32)
+        ext[:, PAD + rows :, :] = jnp.zeros((ext.shape[0], PAD, STRETCH), f32)
     rate = jnp.exp(head_column(rows_ref, A_LOG, group, heads))
     dt_bias = head_column(rows_ref, DT_BIAS, group, heads)
     dt_all = step_sizes(dtr_ref, rows_ref, group)
@@ -573,11 +598,11 @@
     d_dtb = jnp.zeros((heads, 1), f32)
     for block in range(blocks):
         here = slice(block * STRETCH, (block + 1) * STRETCH)
-        seen = resets_seen(flags_ref[:, here])
         running = run_ref[:, here]
         dt = dt_all[:, here]
-        dt_wide[...] = spread_heads(dt, HEAD_DIM)
-        end_wide[...] = spread_heads(to_end_factor(running, seen), HEAD_DIM)
+        end_wide[...] = spread_heads(
+            to_end_factor(running, resets_seen(flags_ref[:, here])), HEAD_DIM
+        )
         b_now = bcc_ref[here, 0:NSTATE]
 
         def chunk(step, carry):
@@ -591,31 +616,25 @@
                 later = (aloc_ref[block, :, part].astype(f32) + whole * later.astype(f32)).astype(bf16)
             state = block_state(block, prior_ref, sloc_ref, keep_ref, part)
             d_keep = jnp.sum(later.astype(f32) * state.astype(f32), axis=0, keepdims=True)
-            stepped = xp_ref[here, part].astype(f32)
-            end = end_wide[:, part]
-            d_end = dot(b_now, later) * end
-            d_stepped = dxp_ref[here, part] + d_end
-            ended = stepped * end
-            ends[0:1, part] = (
-                jnp.sum(stepped * d_end, axis=0, keepdims=True)
-                + d_keep * keep_ref[block : block + 1, part]
+            d_end = dot(b_now, later) * end_wide[:, part]
+            product = xp_ref[here, part].astype(f32) * d_end
+            at_ends = jnp.sum(product, axis=0, keepdims=True)
+            at_ends = at_ends + d_keep * keep_ref[block : block + 1, part]
+            ends[:, part] = jnp.broadcast_to(at_ends, (PAD, CHUNK))
+            d_total = dux_ref[here, part] + d_end * dts_ref[here, part]
+            put_total(dx_ext, xpack_ref, block * STRETCH, part, d_total)
+            return (
+                d_b + dot(ended_ref[here, part], later, ((1,), (1,))),
+                per_step + head_sums(product, step * CHUNK),
             )
-            d_x[here, part] = d_stepped * dt_wide[:, part] + skip_wide[0:1, part] * dy_ref[
-                here, part
-            ].astype(f32)
-            return (
-                d_b + dot(ended.astype(bf16), later, ((1,), (1,))),
-                per_step + head_sums(stepped * d_stepped, step * CHUNK, heads),
-            )
-
-        d_b, per_step = repeat(
-            channels // CHUNK,
-            chunk,
-            (jnp.zeros((STRETCH, NSTATE), f32), jnp.zeros((heads, STRETCH), f32)),
-        )
-        d_bc[here, 0:NSTATE] = dbc_ref[here, 0:NSTATE] + d_b
-        d_bc[here, NSTATE:] = dbc_ref[here, NSTATE:]
-        at_end = head_sums(jnp.broadcast_to(ends[0:1, :], (STRETCH, channels)), 0, heads)
+
+        zero = jnp.zeros((STRETCH, NSTATE), f32)
+        d_b, per_step = repeat(channels // CHUNK, chunk, (zero, jnp.zeros((STRETCH, STRETCH), f32)))
+        per_step = step_ref[:, here] + jnp.transpose(per_step)[0:heads]
+        for place, d_part in enumerate((dbc_ref[here, 0:NSTATE] + d_b, dbc_ref[here, NSTATE:])):
+            part = lanes(place, NSTATE)
+            put_total(dbc_ext, bcpack_ref, block * STRETCH, part, d_part * sbc_ref[here, part])
+        at_end = to_column(head_sums(ends[...], 0)[0:1], 0, heads)
         is_last = iota((heads, STRETCH), 1) == STRETCH - 1
         d_run = drun_ref[:, here] - per_step + jnp.where(is_last, at_end, 0.0)
         shape = (STRETCH, STRETCH)
@@ -633,19 +652,13 @@
         pick = iota(shape, 1) == iota(shape, 0) + group * heads
         row = jnp.sum(jnp.where(pick, jnp.broadcast_to(column, shape), 0.0), axis=0, keepdims=True)
         bcpack_ref[GAIN : GAIN + 1, place * STRETCH : (place + 1) * STRETCH] = row
-
-    def conv_chunk(step, carry):
+    for step in range(channels // STRETCH):
         conv_backward(
-            dx_ext, live, wx_ref, sx_ref, d_x, x_ref, xh_ref, gx_ref, xtail_ref, xpack_ref, rows,
-            lanes(step, STRETCH),
-        )
-        return carry
-
-    repeat(channels // STRETCH, conv_chunk, 0)
+            dx_ext, live_up, wx_ref, x_ref, xh_ref, gx_ref, xtail_ref, xpack_ref, rows, step
+        )
     for step in range(2):
         conv_backward(
-            dbc_ext, live, wb_ref, sbc_ref, d_bc, bc_ref, bch_ref, gbc_ref, bctail_ref, bcpack_ref,
-            rows, slice(step * NSTATE, (step + 1) * NSTATE),
+            dbc_ext, live_up, wb_ref, bc_ref, bch_ref, gbc_ref, bctail_ref, bcpack_ref, rows, step
         )
 
 
@@ -933,7 +946,8 @@
                 + [(piece_shape, bf16)] * PIECES
                 + [((1, channels // PIECES), f32)] * PIECES,
                 [
-                    (rows + PAD, channels), (rows + PAD, width), clear_shape, live_shape,
+                    (channels // STRETCH, rows + PAD, STRETCH), (width // STRETCH, rows + PAD, STRETCH),
+                    clear_shape, live_shape,
                     wide_scratch, wide_scratch, state_shape,
                 ],
                 2 * work,
@@ -1013,12 +1027,14 @@
                 whole(totals[g]), whole(y_all[g]), wide(z_own, g), wide(go_own, g), wide(gain, g),
                 whole(dy[g]), whole(xc[g]), whole(xp[g]), whole(bcc_now),
                 whole(run[g]), whole(flags), whole(s_loc[g]), whole(keep[g]), whole(head_rows),
+                whole(slope_x[g]), per_head(dt_own, g),
             ]
             + [whole(each) for each in prior[g]],
             [
-                (tall, bf16), (tall, f32), (thin, f32), (row_shape, f32), ((PAD, channels), f32),
+                (tall, bf16), (tall, f32), (tall, f32), (tall, bf16), (thin, f32), (row_shape, f32),
+                (row_shape, f32), ((PAD, channels), f32),
             ],
-            run_scratch + [wide_scratch, (PAD, channels)],
+            run_scratch + [wide_scratch, (PAD, channels), wide_scratch, wide_scratch],
             10 * work,
             "within_backward",
             BLOCKED_LIMIT,
@@ -1028,16 +1044,16 @@
         in_a_row(a_dev), in_a_row(decay), "ctx", True, [(backward_work(g), bcc[g]) for g in group_range]
     )
     later = by_pieces(later)
-    gz, dxp, dbc, drun, chan = zip(*held)
+    gz, dux, dts, ended, dbc, drun, per_step, chan = zip(*held)
     held = []
     for g in group_range:
         rows_now = together(head_rows, held[-1][-1])[0] if held else head_rows
         held.append(call(
             functools.partial(finish_backward, group=g),
             [
-                whole(a_loc[g]), whole(s_loc[g]), whole(keep[g]), whole(dxp[g]), whole(dbc[g]),
-                whole(drun[g]), whole(xp[g]), whole(dy[g]), whole(bcc[g]), whole(run[g]),
-                whole(flags), whole(slope_x[g]), whole(slope_bc[g]), wide(x_own, g),
+                whole(a_loc[g]), whole(s_loc[g]), whole(keep[g]), whole(dux[g]), whole(dts[g]),
+                whole(ended[g]), whole(dbc[g]), whole(drun[g]), whole(per_step[g]), whole(xp[g]),
+                whole(bcc[g]), whole(run[g]), whole(flags), whole(slope_bc[g]), wide(x_own, g),
                 wide(halo, g), narrow(bc_own, g), narrow(halo, g, inner), wide(conv_x_weight, g),
                 narrow(wb, g), whole(rows_now), per_head(dt_own, g), whole(chan[g]),
             ]
@@ -1047,8 +1063,9 @@
                 ((HALO, width), f32), ((PACKED, width), f32), (row_shape, f32),
             ],
             [
-                clear_shape, live_shape, (rows + 2 * PAD, channels), (rows + 2 * PAD, width), tall,
-                thin, wide_scratch, wide_scratch, (PAD, channels), (PAD, channels),
+                clear_shape, live_shape, (HALO, rows + PAD, STRETCH),
+                (channels // STRETCH, rows + 2 * PAD, STRETCH),
+                (width // STRETCH, rows + 2 * PAD, STRETCH), wide_scratch, (PAD, channels),
             ],
             4 * work,
             "finish_backward",

time: 96.7 us -> 93.7 us (0.969)
  waiting for transfers between devices: 20.6 us -> 18.1 us
  Pallas kernels: 33 us -> 31.6 us
    ppermute x24, waiting for transfers between devices: 10.2 us -> 8.7 us  [chain(): last = [lax.ppermute(each, axis, pairs) for each in leaving]]
    pallas_call x15, Pallas kernels: 33 us -> 31.6 us  [call(): pl.pallas_call(kernel if blocked else body, in_specs=in_specs, out_specs=...]
  transfers between devices with their start and end apart: 31 -> 31, of which waited for: 11 -> 10; matrix products, arithmetic and copies ran while one was open for 3% -> 3% of each run, Pallas kernels for 21% -> 22%
where the time goes in v5:
time: 93.7 us; the launch traced here: 93.2 us
  starting transfers between devices  37.6 us (40%)
  Pallas kernels  31.6 us (34%)
  waiting for transfers between devices  18.1 us (19%)
  other arithmetic  2.83 us (3%)
  local copies, waits for them, and re-layouts  1.56 us (2%)
  between operations  1.43 us (2%)
    pallas_call x15, Pallas kernels, call(): pl.pallas_call(kernel if blocked else body, in_specs=in_specs, out_specs=...  31.6 us
    ppermute x24, starting transfers between devices, chain(): last = [lax.ppermute(each, axis, pairs) for each in leaving]  24.2 us
    ppermute x24, waiting for transfers between devices, chain(): last = [lax.ppermute(each, axis, pairs) for each in leaving]  8.7 us
    ppermute x3, starting transfers between devices, per_device(): lax.ppermute(leaving, 'ctx', [(i, i ^ shift) for i in range(count)])  5.36 us
    ppermute x1, starting transfers between devices, per_device(): halo = lax.ppermute(sent, 'ctx', [(i, i + 1) for i in range(count - 1)])  4.93 us
    ppermute x2, waiting for transfers between devices, exchange_terms(): other = lax.ppermute(value, axis, [(i, i ^ stride) for i in range(count)])  4.15 us
    ppermute x3, waiting for transfers between devices, per_device(): lax.ppermute(leaving, 'ctx', [(i, i ^ shift) for i in range(count)])  3.55 us
    ppermute x2, starting transfers between devices, exchange_terms(): other = lax.ppermute(value, axis, [(i, i ^ stride) for i in range(count)])  3.05 us
  transfers between devices with their start and end apart: 31, of which 10 were waited for; matrix products, arithmetic and copies ran while one was open for 3% of the time, Pallas kernels for 22%

profile of v5, /device:TPU:0, one launch (start us, length us, event | category | flops | bytes accessed | tf_op | source)
XLA Modules:
  0.0 93.2 jit_solution(14462182863725729030)
XLA Ops:
  0.8 1.8 %tails.1 = f32[3,2560]{1,0:T(4,128)} custom-call(bf16[1,256,2048]{2,1,0:T(8,128)(2,1)} %refs_0_.1, bf16[1,256,2,256]{3,2,1,0:T(2,128)(2,1)} %refs_1_.1, s32[1,256]{1,0:T(1,128)} %refs_2_.2), custom_call_target="tpu_custom_call" | custom-call | flops 256 | bytes 1342464 | tf_op jit(solution)/shard_map/tails/pallas_call | solution.py:808
  2.5 4.9 %collective-permute-start = (f32[3,2560]{1,0:T(4,128)}, f32[3,2560]{1,0:T(4,128)S(1)}, u32[]{:S(2)}, u32[]{:S(2)}) collective-permute-start(f32[3,2560]{1,0:T(4,128)} %tails.1), channel_id=1, source_target_pairs={{0,4},{4,8},{8,12},{1,5},{5,9},{9,13},{2,6},{6,10},{10,14},{3,7},{... | collective-permute-start | bytes 92168 | tf_op jit(solution)/shard_map/ppermute | solution.py:897
  7.8 1.6 %collective-permute-done.refs_1_.refs_3_.xh_ref.bch_ref = f32[3,2560]{1,0:T(4,128)S(1)} collective-permute-done((f32[3,2560]{1,0:T(4,128)}, f32[3,2560]{1,0:T(4,128)S(1)}, u32[]{:S(2)}, u32[]{:S(2)}) %collective-permute-start) | collective-permute-done | bytes 30752 | tf_op jit(solution)/shard_map/ppermute | solution.py:897
  9.5 2.4 %conv_and_state.2 = (bf16[256,1024]{1,0:T(8,128)(2,1)S(1)}, bf16[256,1024]{1,0:T(8,128)(2,1)S(1)}, f32[256,1024]{1,0:T(8,128)S(1)}, bf16[256,256]{1,0:T(8,128)(2...) custom-call(bf16[256,2048]{1,0:T(8,128)(2,1)S(1)} %bitcast.59, ...), custom_call_target="tpu_custom_call" | custom-call | flops 67108864 | bytes 4512768 | tf_op jit(solution)/shard_map/conv_and_state/pallas_call | solution.py:808
  11.9 4.1 %collective-permute-start.1 = (bf16[128,512]{1,0:T(8,128)(2,1)S(1)}, bf16[128,512]{1,0:T(8,128)(2,1)S(1)}, u32[]{:S(2)}, u32[]{:S(2)}) collective-permute-start(bf16[128,512]{1,0:T(8,128)(2,1)S(1)} %get-tuple-element.146), channel_id=1, source_target_pairs={{0,4},{1,5},{2,6},{3,7},{16,20},{17,21},{18,22},{19,23}} | collective-permute-start | bytes 393224 | tf_op jit(solution)/shard_map/ppermute | solution.py:844
  16.0 1.3 %collective-permute-start.3 = (bf16[128,512]{1,0:T(8,128)(2,1)S(1)}, bf16[128,512]{1,0:T(8,128)(2,1)S(1)}, u32[]{:S(2)}, u32[]{:S(2)}) collective-permute-start(bf16[128,512]{1,0:T(8,128)(2,1)S(1)} %get-tuple-element.150), channel_id=1, source_target_pairs={{0,4},{1,5},{2,6},{3,7},{16,20},{17,21},{18,22},{19,23}} | collective-permute-start | bytes 393224 | tf_op jit(solution)/shard_map/ppermute | solution.py:844
  17.3 2.4 %conv_and_state.3 = (bf16[256,1024]{1,0:T(8,128)(2,1)S(1)}, bf16[256,1024]{1,0:T(8,128)(2,1)S(1)}, f32[256,1024]{1,0:T(8,128)S(1)}, bf16[256,256]{1,0:T(8,128)(2...) custom-call(bf16[256,2048]{1,0:T(8,128)(2,1)S(1)} %bitcast.60, ...), custom_call_target="tpu_custom_call" | custom-call | flops 67108864 | bytes 4512768 | tf_op jit(solution)/shard_map/conv_and_state/pallas_call | solution.py:808
  26.7 1.4 %within_blocks.2 = (f32[256,1024]{1,0:T(8,128)S(1)}, f32[256,1024]{1,0:T(8,128)S(1)}, f32[256,256]{1,0:T(8,128)S(1)}) custom-call(bf16[256,1024]{1,0:T(8,128)(2,1)S(1)} %get-tuple-element.147.refs_0_.xp_ref, bf16[256,256]{1,0:T(8,128)(2,1)S(1)} %get-tuple-element.204.refs_1_.refs_3_.bcc_ref, f32[16,256]{1,0:T(8,128)S(1)} %get-tuple-element.160.refs_2_.refs_4_.run_ref, ...), custom_call_target="tpu_custom_call" | custom-call | flops 201326592 | bytes 4342784 | tf_op jit(solution)/shard_map/within_blocks/pallas_call | solution.py:808
  31.4 1.4 %within_blocks.3 = (f32[256,1024]{1,0:T(8,128)S(1)}, f32[256,1024]{1,0:T(8,128)S(1)}, f32[256,256]{1,0:T(8,128)S(1)}) custom-call(bf16[256,1024]{1,0:T(8,128)(2,1)S(1)} %get-tuple-element.167.refs_0_.xp_ref, bf16[256,256]{1,0:T(8,128)(2,1)S(1)} %get-tuple-element.229.refs_1_.refs_3_.bcc_ref, f32[16,256]{1,0:T(8,128)S(1)} %get-tuple-element.173.refs_2_.refs_4_.run_ref, ...), custom_call_target="tpu_custom_call" | custom-call | flops 201326592 | bytes 4342784 | tf_op jit(solution)/shard_map/within_blocks/pallas_call | solution.py:808
  32.9 1.5 %gate_forward.2 = (f32[320,1024]{1,0:T(8,128)S(1)}, f32[2,256]{1,0:T(2,128)S(1)}) custom-call(f32[256,1024]{1,0:T(8,128)S(1)} %get-tuple-element.183.refs_0_, bf16[1,128,1024]{2,1,0:T(8,128)(2,1)S(1)} %get-tuple-element.184.refs_1_.sloc_ref, f32[8,1024]{1,0:T(8,128)S(1)} %get-tuple-element.185.refs_2_.keep_ref, ...), custom_call_target="tpu_custom_call" | custom-call | flops 67108864 | bytes 5962752 | tf_op jit(solution)/shard_map/gate_forward/pallas_call | solution.py:808
  34.4 1.6 %gate_forward.3 = (f32[320,1024]{1,0:T(8,128)S(1)}, f32[2,256]{1,0:T(2,128)S(1)}) custom-call(f32[256,1024]{1,0:T(8,128)S(1)} %get-tuple-element.179.refs_0_, bf16[1,128,1024]{2,1,0:T(8,128)(2,1)S(1)} %get-tuple-element.180.refs_1_.sloc_ref, f32[8,1024]{1,0:T(8,128)S(1)} %get-tuple-element.181.refs_2_.keep_ref, ...), custom_call_target="tpu_custom_call" | custom-call | flops 67108864 | bytes 5964800 | tf_op jit(solution)/shard_map/gate_forward/pallas_call | solution.py:808
  36.0 1.5 %collective-permute-start.13 = (f32[2,256]{1,0:T(2,128)S(1)}, f32[2,256]{1,0:T(2,128)S(1)}, u32[]{:S(2)}, u32[]{:S(2)}) collective-permute-start(f32[2,256]{1,0:T(2,128)S(1)} %get-tuple-element.189), channel_id=1, source_target_pairs={{0,1},{1,0},{2,3},{3,2},{4,5},{5,4},{6,7},{7,6},{8,9},{9,8},{10,11... | collective-permute-start | bytes 6152 | tf_op jit(solution)/shard_map/ppermute | solution.py:860
  37.5 2.1 %collective-permute-done.13 = f32[2,256]{1,0:T(2,128)S(1)} collective-permute-done((f32[2,256]{1,0:T(2,128)S(1)}, f32[2,256]{1,0:T(2,128)S(1)}, u32[]{:S(2)}, u32[]{:S(2)}) %collective-permute-start.13) | collective-permute-done | bytes 2080 | tf_op jit(solution)/shard_map/ppermute | solution.py:860
  39.6 1.5 %collective-permute-start.14 = (f32[2,256]{1,0:T(2,128)S(1)}, f32[2,256]{1,0:T(2,128)S(1)}, u32[]{:S(2)}, u32[]{:S(2)}) collective-permute-start(f32[2,256]{1,0:T(2,128)S(1)} %add.98.refs_0_), channel_id=1, source_target_pairs={{0,2},{1,3},{2,0},{3,1},{4,6},{5,7},{6,4},{7,5},{8,10},{9,11},{10,... | collective-permute-start | bytes 6152 | tf_op jit(solution)/shard_map/ppermute | solution.py:860
  41.1 2.1 %collective-permute-done.14.refs_1_ = f32[2,256]{1,0:T(2,128)S(1)} collective-permute-done((f32[2,256]{1,0:T(2,128)S(1)}, f32[2,256]{1,0:T(2,128)S(1)}, u32[]{:S(2)}, u32[]{:S(2)}) %collective-permute-start.14) | collective-permute-done | bytes 2080 | tf_op jit(solution)/shard_map/ppermute | solution.py:860
  51.2 4.7 %within_backward.2 = (bf16[256,1024]{1,0:T(8,128)(2,1)S(1)}, f32[256,1024]{1,0:T(8,128)S(1)}, f32[256,1024]{1,0:T(8,128)S(1)}, bf16[256,1024]{1,0:T(8,128)(2,1)S...) custom-call(f32[2,256]{1,0:T(2,128)S(1)} %get-tuple-element.193.totals_ref,, ...), custom_call_target="tpu_custom_call" | custom-call | flops 335544320 | bytes 10238976 | tf_op jit(solution)/shard_map/within_backward/pallas_call | solution.py:808
  61.4 4.7 %within_backward.3 = (bf16[256,1024]{1,0:T(8,128)(2,1)S(1)}, f32[256,1024]{1,0:T(8,128)S(1)}, f32[256,1024]{1,0:T(8,128)S(1)}, bf16[256,1024]{1,0:T(8,128)(2,1)S...) custom-call(f32[2,256]{1,0:T(2,128)S(1)} %get-tuple-element.224.totals_ref,, ...), custom_call_target="tpu_custom_call" | custom-call | flops 335544320 | bytes 10238976 | tf_op jit(solution)/shard_map/within_backward/pallas_call | solution.py:808
  66.1 4.9 %collective-permute-done.21.refs_2_ = bf16[128,512]{1,0:T(8,128)(2,1)S(1)} collective-permute-done((bf16[128,512]{1,0:T(8,128)(2,1)S(1)}, bf16[128,512]{1,0:T(8,128)(2,1)S(1)}, u32[]{:S(2)}, u32[]{:S(2)}) %collective-permute-start.21) | collective-permute-done | bytes 131104 | tf_op jit(solution)/shard_map/ppermute | solution.py:844
  71.0 2.2 %collective-permute-done.24.refs_3_ = bf16[128,512]{1,0:T(8,128)(2,1)S(1)} collective-permute-done((bf16[128,512]{1,0:T(8,128)(2,1)S(1)}, bf16[128,512]{1,0:T(8,128)(2,1)S(1)}, u32[]{:S(2)}, u32[]{:S(2)}) %collective-permute-start.24) | collective-permute-done | bytes 131104 | tf_op jit(solution)/shard_map/ppermute | solution.py:844
  73.2 3.4 %finish_backward.2 = (bf16[256,1024]{1,0:T(8,128)(2,1)S(1)}, f32[3,1024]{1,0:T(4,128)S(1)}, f32[10,1024]{1,0:T(8,128)S(1)}, bf16[256,256]{1,0:T(8,128)(2,1)S(1)}...) custom-call(bf16[1,128,1024]{2,1,0:T(8,128)(2,1)S(1)} %get-tuple-element.191.aloc_ref, ...), custom_call_target="tpu_custom_call" | custom-call | flops 134217728 | bytes 7661568 | tf_op jit(solution)/shard_map/finish_backward/pallas_call | solution.py:808
  76.6 3.4 %finish_backward.3 = (bf16[256,1024]{1,0:T(8,128)(2,1)S(1)}, f32[3,1024]{1,0:T(4,128)S(1)}, f32[10,1024]{1,0:T(8,128)S(1)}, bf16[256,256]{1,0:T(8,128)(2,1)S(1)}...) custom-call(bf16[1,128,1024]{2,1,0:T(8,128)(2,1)S(1)} %get-tuple-element.241.aloc_ref, ...), custom_call_target="tpu_custom_call" | custom-call | flops 134217728 | bytes 7661568 | tf_op jit(solution)/shard_map/finish_backward/pallas_call | solution.py:808
  81.5 2.8 %collective-permute-start.30 = (bf16[8,3200]{1,0:T(8,128)(2,1)S(1)}, bf16[8,3200]{1,0:T(8,128)(2,1)S(1)}, u32[]{:S(2)}, u32[]{:S(2)}) collective-permute-start(bf16[8,3200]{1,0:T(8,128)(2,1)S(1)} %get-tuple-element.276), channel_id=1, source_target_pairs={{0,12},{4,8},{8,4},{12,0},{1,13},{5,9},{9,5},{13,1},{2,14},{6,10},... | collective-permute-start | bytes 153608 | tf_op jit(solution)/shard_map/ppermute | solution.py:1103
  84.3 2.6 %collective-permute-start.29 = (bf16[8,3200]{1,0:T(8,128)(2,1)S(1)}, bf16[8,3200]{1,0:T(8,128)(2,1)S(1)}, u32[]{:S(2)}, u32[]{:S(2)}) collective-permute-start(bf16[8,3200]{1,0:T(8,128)(2,1)S(1)} %get-tuple-element.276), channel_id=1, source_target_pairs={{0,8},{4,12},{8,0},{12,4},{1,9},{5,13},{9,1},{13,5},{2,10},{6,14},... | collective-permute-start | bytes 153608 | tf_op jit(solution)/shard_map/ppermute | solution.py:1103
  87.6 3.1 %collective-permute-done.29.refs_4_ = bf16[8,3200]{1,0:T(8,128)(2,1)S(1)} collective-permute-done((bf16[8,3200]{1,0:T(8,128)(2,1)S(1)}, bf16[8,3200]{1,0:T(8,128)(2,1)S(1)}, u32[]{:S(2)}, u32[]{:S(2)}) %collective-permute-start.29) | collective-permute-done | bytes 51232 | tf_op jit(solution)/shard_map/ppermute | solution.py:1103
  (120 shorter events, 28.3 us)
Async XLA Ops:
  2.5 6.9 %collective-permute-start = (f32[3,2560]{1,0:T(4,128)}, f32[3,2560]{1,0:T(4,128)S(1)}, u32[]{:S(2)}, u32[]{:S(2)}) collective-permute-start(f32[3,2560]{1,0:T(4,128)} %tails.1), channel_id=1, source_target_pairs={{0,4},{4,8},{8,12},{1,5},{5,9},{9,13},{2,6},{6,10},{10,14},{3,7},{... | collective-permute-start | bytes 92168 | tf_op jit(solution)/shard_map/ppermute | solution.py:897
  11.9 10.4 %collective-permute-start.1 = (bf16[128,512]{1,0:T(8,128)(2,1)S(1)}, bf16[128,512]{1,0:T(8,128)(2,1)S(1)}, u32[]{:S(2)}, u32[]{:S(2)}) collective-permute-start(bf16[128,512]{1,0:T(8,128)(2,1)S(1)} %get-tuple-element.146), channel_id=1, source_target_pairs={{0,4},{1,5},{2,6},{3,7},{16,20},{17,21},{18,22},{19,23}} | collective-permute-start | bytes 393224 | tf_op jit(solution)/shard_map/ppermute | solution.py:844
  16.0 7.0 %collective-permute-start.3 = (bf16[128,512]{1,0:T(8,128)(2,1)S(1)}, bf16[128,512]{1,0:T(8,128)(2,1)S(1)}, u32[]{:S(2)}, u32[]{:S(2)}) collective-permute-start(bf16[128,512]{1,0:T(8,128)(2,1)S(1)} %get-tuple-element.150), channel_id=1, source_target_pairs={{0,4},{1,5},{2,6},{3,7},{16,20},{17,21},{18,22},{19,23}} | collective-permute-start | bytes 393224 | tf_op jit(solution)/shard_map/ppermute | solution.py:844
  19.7 4.9 %collective-permute-start.4 = (bf16[128,512]{1,0:T(8,128)(2,1)S(1)}, bf16[128,512]{1,0:T(8,128)(2,1)S(1)}, u32[]{:S(2)}, u32[]{:S(2)}) collective-permute-start(bf16[128,512]{1,0:T(8,128)(2,1)S(1)} %get-tuple-element.154), channel_id=1, source_target_pairs={{0,4},{1,5},{2,6},{3,7},{16,20},{17,21},{18,22},{19,23}} | collective-permute-start | bytes 393224 | tf_op jit(solution)/shard_map/ppermute | solution.py:844
  21.0 5.0 %collective-permute-start.5 = (bf16[128,512]{1,0:T(8,128)(2,1)S(1)}, bf16[128,512]{1,0:T(8,128)(2,1)S(1)}, u32[]{:S(2)}, u32[]{:S(2)}) collective-permute-start(bf16[128,512]{1,0:T(8,128)(2,1)S(1)} %get-tuple-element.157), channel_id=1, source_target_pairs={{0,4},{1,5},{2,6},{3,7},{16,20},{17,21},{18,22},{19,23}} | collective-permute-start | bytes 393224 | tf_op jit(solution)/shard_map/ppermute | solution.py:844
  22.4 5.8 %collective-permute-start.2 = (bf16[128,512]{1,0:T(8,128)(2,1)S(1)}, bf16[128,512]{1,0:T(8,128)(2,1)S(1)}, u32[]{:S(2)}, u32[]{:S(2)}) collective-permute-start(bf16[128,512]{1,0:T(8,128)(2,1)S(1)} %fusion), channel_id=1, source_target_pairs={{4,8},{5,9},{6,10},{7,11},{20,24},{21,25},{22,26},{23,27}} | collective-permute-start | bytes 393224 | tf_op jit(solution)/shard_map/ppermute | solution.py:844
  23.1 5.8 %collective-permute-start.7 = (bf16[128,512]{1,0:T(8,128)(2,1)S(1)}, bf16[128,512]{1,0:T(8,128)(2,1)S(1)}, u32[]{:S(2)}, u32[]{:S(2)}) collective-permute-start(bf16[128,512]{1,0:T(8,128)(2,1)S(1)} %fusion.2), channel_id=1, source_target_pairs={{4,8},{5,9},{6,10},{7,11},{20,24},{21,25},{22,26},{23,27}} | collective-permute-start | bytes 393224 | tf_op jit(solution)/shard_map/ppermute | solution.py:844
  24.7 5.0 %collective-permute-start.8 = (bf16[128,512]{1,0:T(8,128)(2,1)S(1)}, bf16[128,512]{1,0:T(8,128)(2,1)S(1)}, u32[]{:S(2)}, u32[]{:S(2)}) collective-permute-start(bf16[128,512]{1,0:T(8,128)(2,1)S(1)} %fusion.4), channel_id=1, source_target_pairs={{4,8},{5,9},{6,10},{7,11},{20,24},{21,25},{22,26},{23,27}} | collective-permute-start | bytes 393224 | tf_op jit(solution)/shard_map/ppermute | solution.py:844
  28.3 4.6 %collective-permute-start.6 = (bf16[128,512]{1,0:T(8,128)(2,1)S(1)}, bf16[128,512]{1,0:T(8,128)(2,1)S(1)}, u32[]{:S(2)}, u32[]{:S(2)}) collective-permute-start(bf16[128,512]{1,0:T(8,128)(2,1)S(1)} %get-tuple-element.292), channel_id=1, source_target_pairs={{8,12},{9,13},{10,14},{11,15},{24,28},{25,29},{26,30},{27,31}} | collective-permute-start | bytes 393224 | tf_op jit(solution)/shard_map/ppermute | solution.py:844
  29.0 3.8 %collective-permute-start.12 = (bf16[128,512]{1,0:T(8,128)(2,1)S(1)}, bf16[128,512]{1,0:T(8,128)(2,1)S(1)}, u32[]{:S(2)}, u32[]{:S(2)}) collective-permute-start(bf16[128,512]{1,0:T(8,128)(2,1)S(1)} %get-tuple-element.290), channel_id=1, source_target_pairs={{8,12},{9,13},{10,14},{11,15},{24,28},{25,29},{26,30},{27,31}} | collective-permute-start | bytes 393224 | tf_op jit(solution)/shard_map/ppermute | solution.py:844
  29.9 4.5 %collective-permute-start.11 = (bf16[128,512]{1,0:T(8,128)(2,1)S(1)}, bf16[128,512]{1,0:T(8,128)(2,1)S(1)}, u32[]{:S(2)}, u32[]{:S(2)}) collective-permute-start(bf16[128,512]{1,0:T(8,128)(2,1)S(1)} %get-tuple-element.286), channel_id=1, source_target_pairs={{8,12},{9,13},{10,14},{11,15},{24,28},{25,29},{26,30},{27,31}} | collective-permute-start | bytes 393224 | tf_op jit(solution)/shard_map/ppermute | solution.py:844
  44.3 3.9 %collective-permute-start.15 = (bf16[128,512]{1,0:T(8,128)(2,1)S(1)}, bf16[128,512]{1,0:T(8,128)(2,1)S(1)}, u32[]{:S(2)}, u32[]{:S(2)}) collective-permute-start(bf16[128,512]{1,0:T(8,128)(2,1)S(1)} %get-tuple-element.192), channel_id=1, source_target_pairs={{12,8},{13,9},{14,10},{15,11},{28,24},{29,25},{30,26},{31,27}} | collective-permute-start | bytes 393224 | tf_op jit(solution)/shard_map/ppermute | solution.py:844
  44.9 4.0 %collective-permute-start.17 = (bf16[128,512]{1,0:T(8,128)(2,1)S(1)}, bf16[128,512]{1,0:T(8,128)(2,1)S(1)}, u32[]{:S(2)}, u32[]{:S(2)}) collective-permute-start(bf16[128,512]{1,0:T(8,128)(2,1)S(1)} %get-tuple-element.196), channel_id=1, source_target_pairs={{12,8},{13,9},{14,10},{15,11},{28,24},{29,25},{30,26},{31,27}} | collective-permute-start | bytes 393224 | tf_op jit(solution)/shard_map/ppermute | solution.py:844
  48.3 7.6 %collective-permute-start.16 = (bf16[128,512]{1,0:T(8,128)(2,1)S(1)}, bf16[128,512]{1,0:T(8,128)(2,1)S(1)}, u32[]{:S(2)}, u32[]{:S(2)}) collective-permute-start(bf16[128,512]{1,0:T(8,128)(2,1)S(1)} %fusion.8), channel_id=1, source_target_pairs={{8,4},{9,5},{10,6},{11,7},{24,20},{25,21},{26,22},{27,23}} | collective-permute-start | bytes 393224 | tf_op jit(solution)/shard_map/ppermute | solution.py:844
  49.0 8.2 %collective-permute-start.20 = (bf16[128,512]{1,0:T(8,128)(2,1)S(1)}, bf16[128,512]{1,0:T(8,128)(2,1)S(1)}, u32[]{:S(2)}, u32[]{:S(2)}) collective-permute-start(bf16[128,512]{1,0:T(8,128)(2,1)S(1)} %fusion.10), channel_id=1, source_target_pairs={{8,4},{9,5},{10,6},{11,7},{24,20},{25,21},{26,22},{27,23}} | collective-permute-start | bytes 393224 | tf_op jit(solution)/shard_map/ppermute | solution.py:844
  49.8 8.9 %collective-permute-start.22 = (bf16[128,512]{1,0:T(8,128)(2,1)S(1)}, bf16[128,512]{1,0:T(8,128)(2,1)S(1)}, u32[]{:S(2)}, u32[]{:S(2)}) collective-permute-start(bf16[128,512]{1,0:T(8,128)(2,1)S(1)} %fusion.12), channel_id=1, source_target_pairs={{8,4},{9,5},{10,6},{11,7},{24,20},{25,21},{26,22},{27,23}} | collective-permute-start | bytes 393224 | tf_op jit(solution)/shard_map/ppermute | solution.py:844
  50.5 8.2 %collective-permute-start.23 = (bf16[128,512]{1,0:T(8,128)(2,1)S(1)}, bf16[128,512]{1,0:T(8,128)(2,1)S(1)}, u32[]{:S(2)}, u32[]{:S(2)}) collective-permute-start(bf16[128,512]{1,0:T(8,128)(2,1)S(1)} %fusion.14), channel_id=1, source_target_pairs={{8,4},{9,5},{10,6},{11,7},{24,20},{25,21},{26,22},{27,23}} | collective-permute-start | bytes 393224 | tf_op jit(solution)/shard_map/ppermute | solution.py:844
  56.0 15.1 %collective-permute-start.21 = (bf16[128,512]{1,0:T(8,128)(2,1)S(1)}, bf16[128,512]{1,0:T(8,128)(2,1)S(1)}, u32[]{:S(2)}, u32[]{:S(2)}) collective-permute-start(bf16[128,512]{1,0:T(8,128)(2,1)S(1)} %get-tuple-element.284), channel_id=1, source_target_pairs={{4,0},{5,1},{6,2},{7,3},{20,16},{21,17},{22,18},{23,19}} | collective-permute-start | bytes 393224 | tf_op jit(solution)/shard_map/ppermute | solution.py:844
  57.3 15.9 %collective-permute-start.24 = (bf16[128,512]{1,0:T(8,128)(2,1)S(1)}, bf16[128,512]{1,0:T(8,128)(2,1)S(1)}, u32[]{:S(2)}, u32[]{:S(2)}) collective-permute-start(bf16[128,512]{1,0:T(8,128)(2,1)S(1)} %get-tuple-element.282), channel_id=1, source_target_pairs={{4,0},{5,1},{6,2},{7,3},{20,16},{21,17},{22,18},{23,19}} | collective-permute-start | bytes 393224 | tf_op jit(solution)/shard_map/ppermute | solution.py:844
  58.8 17.8 %collective-permute-start.26 = (bf16[128,512]{1,0:T(8,128)(2,1)S(1)}, bf16[128,512]{1,0:T(8,128)(2,1)S(1)}, u32[]{:S(2)}, u32[]{:S(2)}) collective-permute-start(bf16[128,512]{1,0:T(8,128)(2,1)S(1)} %get-tuple-element.278), channel_id=1, source_target_pairs={{4,0},{5,1},{6,2},{7,3},{20,16},{21,17},{22,18},{23,19}} | collective-permute-start | bytes 393224 | tf_op jit(solution)/shard_map/ppermute | solution.py:844
  60.1 16.5 %collective-permute-start.25 = (bf16[128,512]{1,0:T(8,128)(2,1)S(1)}, bf16[128,512]{1,0:T(8,128)(2,1)S(1)}, u32[]{:S(2)}, u32[]{:S(2)}) collective-permute-start(bf16[128,512]{1,0:T(8,128)(2,1)S(1)} %get-tuple-element.280), channel_id=1, source_target_pairs={{4,0},{5,1},{6,2},{7,3},{20,16},{21,17},{22,18},{23,19}} | collective-permute-start | bytes 393224 | tf_op jit(solution)/shard_map/ppermute | solution.py:844
  81.5 6.1 %collective-permute-start.30 = (bf16[8,3200]{1,0:T(8,128)(2,1)S(1)}, bf16[8,3200]{1,0:T(8,128)(2,1)S(1)}, u32[]{:S(2)}, u32[]{:S(2)}) collective-permute-start(bf16[8,3200]{1,0:T(8,128)(2,1)S(1)} %get-tuple-element.276), channel_id=1, source_target_pairs={{0,12},{4,8},{8,4},{12,0},{1,13},{5,9},{9,5},{13,1},{2,14},{6,10},... | collective-permute-start | bytes 153608 | tf_op jit(solution)/shard_map/ppermute | solution.py:1103
  84.3 6.4 %collective-permute-start.29 = (bf16[8,3200]{1,0:T(8,128)(2,1)S(1)}, bf16[8,3200]{1,0:T(8,128)(2,1)S(1)}, u32[]{:S(2)}, u32[]{:S(2)}) collective-permute-start(bf16[8,3200]{1,0:T(8,128)(2,1)S(1)} %get-tuple-element.276), channel_id=1, source_target_pairs={{0,8},{4,12},{8,0},{12,4},{1,9},{5,13},{9,1},{13,5},{2,10},{6,14},... | collective-permute-start | bytes 153608 | tf_op jit(solution)/shard_map/ppermute | solution.py:1103
  86.9 4.2 %collective-permute-start.28 = (bf16[8,3200]{1,0:T(8,128)(2,1)S(1)}, bf16[8,3200]{1,0:T(8,128)(2,1)S(1)}, u32[]{:S(2)}, u32[]{:S(2)}) collective-permute-start(bf16[8,3200]{1,0:T(8,128)(2,1)S(1)} %get-tuple-element.276), channel_id=1, source_target_pairs={{0,4},{4,0},{8,12},{12,8},{1,5},{5,1},{9,13},{13,9},{2,6},{6,2},{1... | collective-permute-start | bytes 153608 | tf_op jit(solution)/shard_map/ppermute | solution.py:1103
  (24 other events, 121.1 us)

commit v6 on v5

--- a/solution.py
+++ b/solution.py
@@ -117,7 +117,7 @@
 
 
 def over_channels(column):
-    return spread_heads(jnp.broadcast_to(column, (column.shape[0], STRETCH)), HEAD_DIM)[0:1]
+    return spread_heads(jnp.broadcast_to(column, (column.shape[0], PAD)), HEAD_DIM)[0:1]
 
 
 def softplus(value):
@@ -1069,7 +1069,6 @@
             ],
             4 * work,
             "finish_backward",
-            BLOCKED_LIMIT,
         ))
     gx, x_tail, x_pack, gbc, bc_tail, bc_pack, gdt = zip(*held)
 

time: 93.7 us -> 92.7 us (0.989)
  waiting for transfers between devices: 18.1 us -> 17.1 us
    ppermute x24, waiting for transfers between devices: 8.7 us -> 7.71 us  [chain(): last = [lax.ppermute(each, axis, pairs) for each in leaving]]
where the time goes in v6:
time: 92.7 us; the launch traced here: 92.3 us
  starting transfers between devices  38 us (41%)
  Pallas kernels  31.3 us (34%)
  waiting for transfers between devices  17.1 us (18%)
  other arithmetic  2.8 us (3%)
  local copies, waits for them, and re-layouts  1.56 us (2%)
  between operations  1.44 us (2%)
    pallas_call x15, Pallas kernels, call(): pl.pallas_call(kernel if blocked else body, in_specs=in_specs, out_specs=...  31.3 us
    ppermute x24, starting transfers between devices, chain(): last = [lax.ppermute(each, axis, pairs) for each in leaving]  24.2 us
    ppermute x24, waiting for transfers between devices, chain(): last = [lax.ppermute(each, axis, pairs) for each in leaving]  7.71 us
    ppermute x3, starting transfers between devices, per_device(): lax.ppermute(leaving, 'ctx', [(i, i ^ shift) for i in range(count)])  5.76 us
    ppermute x1, starting transfers between devices, per_device(): halo = lax.ppermute(sent, 'ctx', [(i, i + 1) for i in range(count - 1)])  4.93 us
    ppermute x2, waiting for transfers between devices, exchange_terms(): other = lax.ppermute(value, axis, [(i, i ^ stride) for i in range(count)])  4.16 us
    ppermute x3, waiting for transfers between devices, per_device(): lax.ppermute(leaving, 'ctx', [(i, i ^ shift) for i in range(count)])  3.52 us
    ppermute x2, starting transfers between devices, exchange_terms(): other = lax.ppermute(value, axis, [(i, i ^ stride) for i in range(count)])  3.04 us
  transfers between devices with their start and end apart: 31, of which 10 were waited for; matrix products, arithmetic and copies ran while one was open for 3% of the time, Pallas kernels for 22%

profile of v6, /device:TPU:0, one launch (start us, length us, event | category | flops | bytes accessed | tf_op | source)
XLA Modules:
  0.0 92.3 jit_solution(3374231180503916043)
XLA Ops:
  0.8 1.8 %tails.1 = f32[3,2560]{1,0:T(4,128)} custom-call(bf16[1,256,2048]{2,1,0:T(8,128)(2,1)} %refs_0_.1, bf16[1,256,2,256]{3,2,1,0:T(2,128)(2,1)} %refs_1_.1, s32[1,256]{1,0:T(1,128)} %refs_2_.2), custom_call_target="tpu_custom_call" | custom-call | flops 256 | bytes 1342464 | tf_op jit(solution)/shard_map/tails/pallas_call | solution.py:808
  2.5 4.9 %collective-permute-start = (f32[3,2560]{1,0:T(4,128)}, f32[3,2560]{1,0:T(4,128)S(1)}, u32[]{:S(2)}, u32[]{:S(2)}) collective-permute-start(f32[3,2560]{1,0:T(4,128)} %tails.1), channel_id=1, source_target_pairs={{0,4},{4,8},{8,12},{1,5},{5,9},{9,13},{2,6},{6,10},{10,14},{3,7},{... | collective-permute-start | bytes 92168 | tf_op jit(solution)/shard_map/ppermute | solution.py:897
  7.8 1.6 %collective-permute-done.refs_1_.refs_3_.refs_15_.refs_17_ = f32[3,2560]{1,0:T(4,128)S(1)} collective-permute-done((f32[3,2560]{1,0:T(4,128)}, f32[3,2560]{1,0:T(4,128)S(1)}, u32[]{:S(2)}, u32[]{:S(2)}) %collective-permute-start) | collective-permute-done | bytes 30752 | tf_op jit(solution)/shard_map/ppermute | solution.py:897
  9.5 2.3 %conv_and_state.2 = (bf16[256,1024]{1,0:T(8,128)(2,1)S(1)}, bf16[256,1024]{1,0:T(8,128)(2,1)S(1)}, f32[256,1024]{1,0:T(8,128)S(1)}, bf16[256,256]{1,0:T(8,128)(2...) custom-call(bf16[256,2048]{1,0:T(8,128)(2,1)S(1)} %bitcast.59, ...), custom_call_target="tpu_custom_call" | custom-call | flops 67108864 | bytes 4512768 | tf_op jit(solution)/shard_map/conv_and_state/pallas_call | solution.py:808
  11.8 4.1 %collective-permute-start.1 = (bf16[128,512]{1,0:T(8,128)(2,1)S(1)}, bf16[128,512]{1,0:T(8,128)(2,1)S(1)}, u32[]{:S(2)}, u32[]{:S(2)}) collective-permute-start(bf16[128,512]{1,0:T(8,128)(2,1)S(1)} %get-tuple-element.146), channel_id=1, source_target_pairs={{0,4},{1,5},{2,6},{3,7},{16,20},{17,21},{18,22},{19,23}} | collective-permute-start | bytes 393224 | tf_op jit(solution)/shard_map/ppermute | solution.py:844
  17.2 2.3 %conv_and_state.3 = (bf16[256,1024]{1,0:T(8,128)(2,1)S(1)}, bf16[256,1024]{1,0:T(8,128)(2,1)S(1)}, f32[256,1024]{1,0:T(8,128)S(1)}, bf16[256,256]{1,0:T(8,128)(2...) custom-call(bf16[256,2048]{1,0:T(8,128)(2,1)S(1)} %bitcast.60, ...), custom_call_target="tpu_custom_call" | custom-call | flops 67108864 | bytes 4512768 | tf_op jit(solution)/shard_map/conv_and_state/pallas_call | solution.py:808
  19.5 1.3 %collective-permute-start.4 = (bf16[128,512]{1,0:T(8,128)(2,1)S(1)}, bf16[128,512]{1,0:T(8,128)(2,1)S(1)}, u32[]{:S(2)}, u32[]{:S(2)}) collective-permute-start(bf16[128,512]{1,0:T(8,128)(2,1)S(1)} %get-tuple-element.154), channel_id=1, source_target_pairs={{0,4},{1,5},{2,6},{3,7},{16,20},{17,21},{18,22},{19,23}} | collective-permute-start | bytes 393224 | tf_op jit(solution)/shard_map/ppermute | solution.py:844
  26.6 1.4 %within_blocks.2 = (f32[256,1024]{1,0:T(8,128)S(1)}, f32[256,1024]{1,0:T(8,128)S(1)}, f32[256,256]{1,0:T(8,128)S(1)}) custom-call(bf16[256,1024]{1,0:T(8,128)(2,1)S(1)} %get-tuple-element.147.refs_0_.xp_ref.refs_9_, bf16[256,256]{1,0:T(8,128)(2,1)S(1)} %get-tuple-element.204.refs_1_.refs_3_.bcc_ref.refs_10_, ...), custom_call_target="tpu_custom_call" | custom-call | flops 201326592 | bytes 4342784 | tf_op jit(solution)/shard_map/within_blocks/pallas_call | solution.py:808
  31.3 1.4 %within_blocks.3 = (f32[256,1024]{1,0:T(8,128)S(1)}, f32[256,1024]{1,0:T(8,128)S(1)}, f32[256,256]{1,0:T(8,128)S(1)}) custom-call(bf16[256,1024]{1,0:T(8,128)(2,1)S(1)} %get-tuple-element.167.refs_0_.xp_ref.refs_9_, bf16[256,256]{1,0:T(8,128)(2,1)S(1)} %get-tuple-element.229.refs_1_.refs_3_.bcc_ref.refs_10_, ...), custom_call_target="tpu_custom_call" | custom-call | flops 201326592 | bytes 4342784 | tf_op jit(solution)/shard_map/within_blocks/pallas_call | solution.py:808
  32.8 1.5 %gate_forward.2 = (f32[320,1024]{1,0:T(8,128)S(1)}, f32[2,256]{1,0:T(2,128)S(1)}) custom-call(f32[256,1024]{1,0:T(8,128)S(1)} %get-tuple-element.183.refs_0_, bf16[1,128,1024]{2,1,0:T(8,128)(2,1)S(1)} %get-tuple-element.184.refs_1_.sloc_ref, f32[8,1024]{1,0:T(8,128)S(1)} %get-tuple-element.185.refs_2_.keep_ref, ...), custom_call_target="tpu_custom_call" | custom-call | flops 67108864 | bytes 5962752 | tf_op jit(solution)/shard_map/gate_forward/pallas_call | solution.py:808
  34.3 1.5 %gate_forward.3 = (f32[320,1024]{1,0:T(8,128)S(1)}, f32[2,256]{1,0:T(2,128)S(1)}) custom-call(f32[256,1024]{1,0:T(8,128)S(1)} %get-tuple-element.179.refs_0_, bf16[1,128,1024]{2,1,0:T(8,128)(2,1)S(1)} %get-tuple-element.180.refs_1_.sloc_ref, f32[8,1024]{1,0:T(8,128)S(1)} %get-tuple-element.181.refs_2_.keep_ref, ...), custom_call_target="tpu_custom_call" | custom-call | flops 67108864 | bytes 5964800 | tf_op jit(solution)/shard_map/gate_forward/pallas_call | solution.py:808
  35.8 1.5 %collective-permute-start.13 = (f32[2,256]{1,0:T(2,128)S(1)}, f32[2,256]{1,0:T(2,128)S(1)}, u32[]{:S(2)}, u32[]{:S(2)}) collective-permute-start(f32[2,256]{1,0:T(2,128)S(1)} %get-tuple-element.189), channel_id=1, source_target_pairs={{0,1},{1,0},{2,3},{3,2},{4,5},{5,4},{6,7},{7,6},{8,9},{9,8},{10,11... | collective-permute-start | bytes 6152 | tf_op jit(solution)/shard_map/ppermute | solution.py:860
  37.3 2.1 %collective-permute-done.13 = f32[2,256]{1,0:T(2,128)S(1)} collective-permute-done((f32[2,256]{1,0:T(2,128)S(1)}, f32[2,256]{1,0:T(2,128)S(1)}, u32[]{:S(2)}, u32[]{:S(2)}) %collective-permute-start.13) | collective-permute-done | bytes 2080 | tf_op jit(solution)/shard_map/ppermute | solution.py:860
  39.4 1.5 %collective-permute-start.14 = (f32[2,256]{1,0:T(2,128)S(1)}, f32[2,256]{1,0:T(2,128)S(1)}, u32[]{:S(2)}, u32[]{:S(2)}) collective-permute-start(f32[2,256]{1,0:T(2,128)S(1)} %add.98.refs_0_), channel_id=1, source_target_pairs={{0,2},{1,3},{2,0},{3,1},{4,6},{5,7},{6,4},{7,5},{8,10},{9,11},{10,... | collective-permute-start | bytes 6152 | tf_op jit(solution)/shard_map/ppermute | solution.py:860
  40.9 2.1 %collective-permute-done.14.refs_1_ = f32[2,256]{1,0:T(2,128)S(1)} collective-permute-done((f32[2,256]{1,0:T(2,128)S(1)}, f32[2,256]{1,0:T(2,128)S(1)}, u32[]{:S(2)}, u32[]{:S(2)}) %collective-permute-start.14) | collective-permute-done | bytes 2080 | tf_op jit(solution)/shard_map/ppermute | solution.py:860
  50.9 4.7 %within_backward.2 = (bf16[256,1024]{1,0:T(8,128)(2,1)S(1)}, f32[256,1024]{1,0:T(8,128)S(1)}, f32[256,1024]{1,0:T(8,128)S(1)}, bf16[256,1024]{1,0:T(8,128)(2,1)S...) custom-call(f32[2,256]{1,0:T(2,128)S(1)} %get-tuple-element.193.totals_ref,, ...), custom_call_target="tpu_custom_call" | custom-call | flops 335544320 | bytes 10238976 | tf_op jit(solution)/shard_map/within_backward/pallas_call | solution.py:808
  61.2 4.7 %within_backward.3 = (bf16[256,1024]{1,0:T(8,128)(2,1)S(1)}, f32[256,1024]{1,0:T(8,128)S(1)}, f32[256,1024]{1,0:T(8,128)S(1)}, bf16[256,1024]{1,0:T(8,128)(2,1)S...) custom-call(f32[2,256]{1,0:T(2,128)S(1)} %get-tuple-element.224.totals_ref,, ...), custom_call_target="tpu_custom_call" | custom-call | flops 335544320 | bytes 10238976 | tf_op jit(solution)/shard_map/within_backward/pallas_call | solution.py:808
  65.9 4.3 %collective-permute-done.21.refs_25_ = bf16[128,512]{1,0:T(8,128)(2,1)S(1)} collective-permute-done((bf16[128,512]{1,0:T(8,128)(2,1)S(1)}, bf16[128,512]{1,0:T(8,128)(2,1)S(1)}, u32[]{:S(2)}, u32[]{:S(2)}) %collective-permute-start.21) | collective-permute-done | bytes 131104 | tf_op jit(solution)/shard_map/ppermute | solution.py:844
  70.2 1.7 %collective-permute-done.24.refs_26_ = bf16[128,512]{1,0:T(8,128)(2,1)S(1)} collective-permute-done((bf16[128,512]{1,0:T(8,128)(2,1)S(1)}, bf16[128,512]{1,0:T(8,128)(2,1)S(1)}, u32[]{:S(2)}, u32[]{:S(2)}) %collective-permute-start.24) | collective-permute-done | bytes 131104 | tf_op jit(solution)/shard_map/ppermute | solution.py:844
  72.0 3.4 %finish_backward.2 = (bf16[256,1024]{1,0:T(8,128)(2,1)S(1)}, f32[3,1024]{1,0:T(4,128)S(1)}, f32[10,1024]{1,0:T(8,128)S(1)}, bf16[256,256]{1,0:T(8,128)(2,1)S(1)}...) custom-call(bf16[1,128,1024]{2,1,0:T(8,128)(2,1)S(1)} %get-tuple-element.191.refs_0_, ...), custom_call_target="tpu_custom_call" | custom-call | flops 134217728 | bytes 7661568 | tf_op jit(solution)/shard_map/finish_backward/pallas_call | solution.py:808
  75.4 3.4 %finish_backward.3 = (bf16[256,1024]{1,0:T(8,128)(2,1)S(1)}, f32[3,1024]{1,0:T(4,128)S(1)}, f32[10,1024]{1,0:T(8,128)S(1)}, bf16[256,256]{1,0:T(8,128)(2,1)S(1)}...) custom-call(bf16[1,128,1024]{2,1,0:T(8,128)(2,1)S(1)} %get-tuple-element.241.refs_0_, ...), custom_call_target="tpu_custom_call" | custom-call | flops 134217728 | bytes 7661568 | tf_op jit(solution)/shard_map/finish_backward/pallas_call | solution.py:808
  80.2 3.4 %collective-permute-start.30 = (bf16[8,3200]{1,0:T(8,128)(2,1)S(1)}, bf16[8,3200]{1,0:T(8,128)(2,1)S(1)}, u32[]{:S(2)}, u32[]{:S(2)}) collective-permute-start(bf16[8,3200]{1,0:T(8,128)(2,1)S(1)} %get-tuple-element.276), channel_id=1, source_target_pairs={{0,12},{4,8},{8,4},{12,0},{1,13},{5,9},{9,5},{13,1},{2,14},{6,10},... | collective-permute-start | bytes 153608 | tf_op jit(solution)/shard_map/ppermute | solution.py:1102
  83.7 2.3 %collective-permute-start.29 = (bf16[8,3200]{1,0:T(8,128)(2,1)S(1)}, bf16[8,3200]{1,0:T(8,128)(2,1)S(1)}, u32[]{:S(2)}, u32[]{:S(2)}) collective-permute-start(bf16[8,3200]{1,0:T(8,128)(2,1)S(1)} %get-tuple-element.276), channel_id=1, source_target_pairs={{0,8},{4,12},{8,0},{12,4},{1,9},{5,13},{9,1},{13,5},{2,10},{6,14},... | collective-permute-start | bytes 153608 | tf_op jit(solution)/shard_map/ppermute | solution.py:1102
  86.7 3.0 %collective-permute-done.29.refs_4_ = bf16[8,3200]{1,0:T(8,128)(2,1)S(1)} collective-permute-done((bf16[8,3200]{1,0:T(8,128)(2,1)S(1)}, bf16[8,3200]{1,0:T(8,128)(2,1)S(1)}, u32[]{:S(2)}, u32[]{:S(2)}) %collective-permute-start.29) | collective-permute-done | bytes 51232 | tf_op jit(solution)/shard_map/ppermute | solution.py:1102
  (120 shorter events, 28.5 us)
Async XLA Ops:
  2.5 6.9 %collective-permute-start = (f32[3,2560]{1,0:T(4,128)}, f32[3,2560]{1,0:T(4,128)S(1)}, u32[]{:S(2)}, u32[]{:S(2)}) collective-permute-start(f32[3,2560]{1,0:T(4,128)} %tails.1), channel_id=1, source_target_pairs={{0,4},{4,8},{8,12},{1,5},{5,9},{9,13},{2,6},{6,10},{10,14},{3,7},{... | collective-permute-start | bytes 92168 | tf_op jit(solution)/shard_map/ppermute | solution.py:897
  11.8 10.3 %collective-permute-start.1 = (bf16[128,512]{1,0:T(8,128)(2,1)S(1)}, bf16[128,512]{1,0:T(8,128)(2,1)S(1)}, u32[]{:S(2)}, u32[]{:S(2)}) collective-permute-start(bf16[128,512]{1,0:T(8,128)(2,1)S(1)} %get-tuple-element.146), channel_id=1, source_target_pairs={{0,4},{1,5},{2,6},{3,7},{16,20},{17,21},{18,22},{19,23}} | collective-permute-start | bytes 393224 | tf_op jit(solution)/shard_map/ppermute | solution.py:844
  15.9 6.9 %collective-permute-start.3 = (bf16[128,512]{1,0:T(8,128)(2,1)S(1)}, bf16[128,512]{1,0:T(8,128)(2,1)S(1)}, u32[]{:S(2)}, u32[]{:S(2)}) collective-permute-start(bf16[128,512]{1,0:T(8,128)(2,1)S(1)} %get-tuple-element.150), channel_id=1, source_target_pairs={{0,4},{1,5},{2,6},{3,7},{16,20},{17,21},{18,22},{19,23}} | collective-permute-start | bytes 393224 | tf_op jit(solution)/shard_map/ppermute | solution.py:844
  19.5 5.0 %collective-permute-start.4 = (bf16[128,512]{1,0:T(8,128)(2,1)S(1)}, bf16[128,512]{1,0:T(8,128)(2,1)S(1)}, u32[]{:S(2)}, u32[]{:S(2)}) collective-permute-start(bf16[128,512]{1,0:T(8,128)(2,1)S(1)} %get-tuple-element.154), channel_id=1, source_target_pairs={{0,4},{1,5},{2,6},{3,7},{16,20},{17,21},{18,22},{19,23}} | collective-permute-start | bytes 393224 | tf_op jit(solution)/shard_map/ppermute | solution.py:844
  20.8 5.1 %collective-permute-start.5 = (bf16[128,512]{1,0:T(8,128)(2,1)S(1)}, bf16[128,512]{1,0:T(8,128)(2,1)S(1)}, u32[]{:S(2)}, u32[]{:S(2)}) collective-permute-start(bf16[128,512]{1,0:T(8,128)(2,1)S(1)} %get-tuple-element.157), channel_id=1, source_target_pairs={{0,4},{1,5},{2,6},{3,7},{16,20},{17,21},{18,22},{19,23}} | collective-permute-start | bytes 393224 | tf_op jit(solution)/shard_map/ppermute | solution.py:844
  22.1 5.9 %collective-permute-start.2 = (bf16[128,512]{1,0:T(8,128)(2,1)S(1)}, bf16[128,512]{1,0:T(8,128)(2,1)S(1)}, u32[]{:S(2)}, u32[]{:S(2)}) collective-permute-start(bf16[128,512]{1,0:T(8,128)(2,1)S(1)} %fusion), channel_id=1, source_target_pairs={{4,8},{5,9},{6,10},{7,11},{20,24},{21,25},{22,26},{23,27}} | collective-permute-start | bytes 393224 | tf_op jit(solution)/shard_map/ppermute | solution.py:844
  22.9 6.0 %collective-permute-start.7 = (bf16[128,512]{1,0:T(8,128)(2,1)S(1)}, bf16[128,512]{1,0:T(8,128)(2,1)S(1)}, u32[]{:S(2)}, u32[]{:S(2)}) collective-permute-start(bf16[128,512]{1,0:T(8,128)(2,1)S(1)} %fusion.2), channel_id=1, source_target_pairs={{4,8},{5,9},{6,10},{7,11},{20,24},{21,25},{22,26},{23,27}} | collective-permute-start | bytes 393224 | tf_op jit(solution)/shard_map/ppermute | solution.py:844
  24.6 5.1 %collective-permute-start.8 = (bf16[128,512]{1,0:T(8,128)(2,1)S(1)}, bf16[128,512]{1,0:T(8,128)(2,1)S(1)}, u32[]{:S(2)}, u32[]{:S(2)}) collective-permute-start(bf16[128,512]{1,0:T(8,128)(2,1)S(1)} %fusion.4), channel_id=1, source_target_pairs={{4,8},{5,9},{6,10},{7,11},{20,24},{21,25},{22,26},{23,27}} | collective-permute-start | bytes 393224 | tf_op jit(solution)/shard_map/ppermute | solution.py:844
  28.2 4.6 %collective-permute-start.6 = (bf16[128,512]{1,0:T(8,128)(2,1)S(1)}, bf16[128,512]{1,0:T(8,128)(2,1)S(1)}, u32[]{:S(2)}, u32[]{:S(2)}) collective-permute-start(bf16[128,512]{1,0:T(8,128)(2,1)S(1)} %get-tuple-element.292), channel_id=1, source_target_pairs={{8,12},{9,13},{10,14},{11,15},{24,28},{25,29},{26,30},{27,31}} | collective-permute-start | bytes 393224 | tf_op jit(solution)/shard_map/ppermute | solution.py:844
  28.9 3.8 %collective-permute-start.12 = (bf16[128,512]{1,0:T(8,128)(2,1)S(1)}, bf16[128,512]{1,0:T(8,128)(2,1)S(1)}, u32[]{:S(2)}, u32[]{:S(2)}) collective-permute-start(bf16[128,512]{1,0:T(8,128)(2,1)S(1)} %get-tuple-element.290), channel_id=1, source_target_pairs={{8,12},{9,13},{10,14},{11,15},{24,28},{25,29},{26,30},{27,31}} | collective-permute-start | bytes 393224 | tf_op jit(solution)/shard_map/ppermute | solution.py:844
  29.8 4.5 %collective-permute-start.11 = (bf16[128,512]{1,0:T(8,128)(2,1)S(1)}, bf16[128,512]{1,0:T(8,128)(2,1)S(1)}, u32[]{:S(2)}, u32[]{:S(2)}) collective-permute-start(bf16[128,512]{1,0:T(8,128)(2,1)S(1)} %get-tuple-element.286), channel_id=1, source_target_pairs={{8,12},{9,13},{10,14},{11,15},{24,28},{25,29},{26,30},{27,31}} | collective-permute-start | bytes 393224 | tf_op jit(solution)/shard_map/ppermute | solution.py:844
  44.0 4.0 %collective-permute-start.15 = (bf16[128,512]{1,0:T(8,128)(2,1)S(1)}, bf16[128,512]{1,0:T(8,128)(2,1)S(1)}, u32[]{:S(2)}, u32[]{:S(2)}) collective-permute-start(bf16[128,512]{1,0:T(8,128)(2,1)S(1)} %get-tuple-element.192), channel_id=1, source_target_pairs={{12,8},{13,9},{14,10},{15,11},{28,24},{29,25},{30,26},{31,27}} | collective-permute-start | bytes 393224 | tf_op jit(solution)/shard_map/ppermute | solution.py:844
  44.7 4.0 %collective-permute-start.17 = (bf16[128,512]{1,0:T(8,128)(2,1)S(1)}, bf16[128,512]{1,0:T(8,128)(2,1)S(1)}, u32[]{:S(2)}, u32[]{:S(2)}) collective-permute-start(bf16[128,512]{1,0:T(8,128)(2,1)S(1)} %get-tuple-element.196), channel_id=1, source_target_pairs={{12,8},{13,9},{14,10},{15,11},{28,24},{29,25},{30,26},{31,27}} | collective-permute-start | bytes 393224 | tf_op jit(solution)/shard_map/ppermute | solution.py:844
  48.0 7.6 %collective-permute-start.16 = (bf16[128,512]{1,0:T(8,128)(2,1)S(1)}, bf16[128,512]{1,0:T(8,128)(2,1)S(1)}, u32[]{:S(2)}, u32[]{:S(2)}) collective-permute-start(bf16[128,512]{1,0:T(8,128)(2,1)S(1)} %fusion.8), channel_id=1, source_target_pairs={{8,4},{9,5},{10,6},{11,7},{24,20},{25,21},{26,22},{27,23}} | collective-permute-start | bytes 393224 | tf_op jit(solution)/shard_map/ppermute | solution.py:844
  48.8 8.3 %collective-permute-start.20 = (bf16[128,512]{1,0:T(8,128)(2,1)S(1)}, bf16[128,512]{1,0:T(8,128)(2,1)S(1)}, u32[]{:S(2)}, u32[]{:S(2)}) collective-permute-start(bf16[128,512]{1,0:T(8,128)(2,1)S(1)} %fusion.10), channel_id=1, source_target_pairs={{8,4},{9,5},{10,6},{11,7},{24,20},{25,21},{26,22},{27,23}} | collective-permute-start | bytes 393224 | tf_op jit(solution)/shard_map/ppermute | solution.py:844
  49.5 8.9 %collective-permute-start.22 = (bf16[128,512]{1,0:T(8,128)(2,1)S(1)}, bf16[128,512]{1,0:T(8,128)(2,1)S(1)}, u32[]{:S(2)}, u32[]{:S(2)}) collective-permute-start(bf16[128,512]{1,0:T(8,128)(2,1)S(1)} %fusion.12), channel_id=1, source_target_pairs={{8,4},{9,5},{10,6},{11,7},{24,20},{25,21},{26,22},{27,23}} | collective-permute-start | bytes 393224 | tf_op jit(solution)/shard_map/ppermute | solution.py:844
  50.3 8.3 %collective-permute-start.23 = (bf16[128,512]{1,0:T(8,128)(2,1)S(1)}, bf16[128,512]{1,0:T(8,128)(2,1)S(1)}, u32[]{:S(2)}, u32[]{:S(2)}) collective-permute-start(bf16[128,512]{1,0:T(8,128)(2,1)S(1)} %fusion.14), channel_id=1, source_target_pairs={{8,4},{9,5},{10,6},{11,7},{24,20},{25,21},{26,22},{27,23}} | collective-permute-start | bytes 393224 | tf_op jit(solution)/shard_map/ppermute | solution.py:844
  55.8 14.5 %collective-permute-start.21 = (bf16[128,512]{1,0:T(8,128)(2,1)S(1)}, bf16[128,512]{1,0:T(8,128)(2,1)S(1)}, u32[]{:S(2)}, u32[]{:S(2)}) collective-permute-start(bf16[128,512]{1,0:T(8,128)(2,1)S(1)} %get-tuple-element.284), channel_id=1, source_target_pairs={{4,0},{5,1},{6,2},{7,3},{20,16},{21,17},{22,18},{23,19}} | collective-permute-start | bytes 393224 | tf_op jit(solution)/shard_map/ppermute | solution.py:844
  57.2 14.8 %collective-permute-start.24 = (bf16[128,512]{1,0:T(8,128)(2,1)S(1)}, bf16[128,512]{1,0:T(8,128)(2,1)S(1)}, u32[]{:S(2)}, u32[]{:S(2)}) collective-permute-start(bf16[128,512]{1,0:T(8,128)(2,1)S(1)} %get-tuple-element.282), channel_id=1, source_target_pairs={{4,0},{5,1},{6,2},{7,3},{20,16},{21,17},{22,18},{23,19}} | collective-permute-start | bytes 393224 | tf_op jit(solution)/shard_map/ppermute | solution.py:844
  58.6 16.7 %collective-permute-start.26 = (bf16[128,512]{1,0:T(8,128)(2,1)S(1)}, bf16[128,512]{1,0:T(8,128)(2,1)S(1)}, u32[]{:S(2)}, u32[]{:S(2)}) collective-permute-start(bf16[128,512]{1,0:T(8,128)(2,1)S(1)} %get-tuple-element.278), channel_id=1, source_target_pairs={{4,0},{5,1},{6,2},{7,3},{20,16},{21,17},{22,18},{23,19}} | collective-permute-start | bytes 393224 | tf_op jit(solution)/shard_map/ppermute | solution.py:844
  59.9 15.4 %collective-permute-start.25 = (bf16[128,512]{1,0:T(8,128)(2,1)S(1)}, bf16[128,512]{1,0:T(8,128)(2,1)S(1)}, u32[]{:S(2)}, u32[]{:S(2)}) collective-permute-start(bf16[128,512]{1,0:T(8,128)(2,1)S(1)} %get-tuple-element.280), channel_id=1, source_target_pairs={{4,0},{5,1},{6,2},{7,3},{20,16},{21,17},{22,18},{23,19}} | collective-permute-start | bytes 393224 | tf_op jit(solution)/shard_map/ppermute | solution.py:844
  80.2 6.5 %collective-permute-start.30 = (bf16[8,3200]{1,0:T(8,128)(2,1)S(1)}, bf16[8,3200]{1,0:T(8,128)(2,1)S(1)}, u32[]{:S(2)}, u32[]{:S(2)}) collective-permute-start(bf16[8,3200]{1,0:T(8,128)(2,1)S(1)} %get-tuple-element.276), channel_id=1, source_target_pairs={{0,12},{4,8},{8,4},{12,0},{1,13},{5,9},{9,5},{13,1},{2,14},{6,10},... | collective-permute-start | bytes 153608 | tf_op jit(solution)/shard_map/ppermute | solution.py:1102
  83.7 6.0 %collective-permute-start.29 = (bf16[8,3200]{1,0:T(8,128)(2,1)S(1)}, bf16[8,3200]{1,0:T(8,128)(2,1)S(1)}, u32[]{:S(2)}, u32[]{:S(2)}) collective-permute-start(bf16[8,3200]{1,0:T(8,128)(2,1)S(1)} %get-tuple-element.276), channel_id=1, source_target_pairs={{0,8},{4,12},{8,0},{12,4},{1,9},{5,13},{9,1},{13,5},{2,10},{6,14},... | collective-permute-start | bytes 153608 | tf_op jit(solution)/shard_map/ppermute | solution.py:1102
  86.0 4.2 %collective-permute-start.28 = (bf16[8,3200]{1,0:T(8,128)(2,1)S(1)}, bf16[8,3200]{1,0:T(8,128)(2,1)S(1)}, u32[]{:S(2)}, u32[]{:S(2)}) collective-permute-start(bf16[8,3200]{1,0:T(8,128)(2,1)S(1)} %get-tuple-element.276), channel_id=1, source_target_pairs={{0,4},{4,0},{8,12},{12,8},{1,5},{5,1},{9,13},{13,9},{2,6},{6,2},{1... | collective-permute-start | bytes 153608 | tf_op jit(solution)/shard_map/ppermute | solution.py:1102
  (24 other events, 121.3 us)
